TPU v7x, 32 devices: a whole 2x2x4 slice. The times are simulated.
32 devices in a mesh: dp: 4 (over x, core), expert: 8 (over z, y).
Axes of the slice: x: 2, y: 2, z: 4, core: 2. Of those that a mesh axis runs over, the one named last changes fastest.
Arguments:
- patches: bfloat16 [18432, 768], P(('dp', 'expert')), may hold values from -6 to 6
- padding: int32 [18432], P(('dp', 'expert')), may hold values from 0 to 1, as said below
- expert_ids: int32 [18432, 2], P(('dp', 'expert')), may hold values from 0 to 7, all different within a row; in each aligned block of 576 rows (0 to 575, 576 to 1151, ...) at most 192 rows name the same one
- priority: int32 [18432], P(('dp', 'expert')), may hold values from 0 to 18431, each once
- norm1_gain: float32 [768], replicated, may hold values from 0.5 to 1.5
- norm1_bias: float32 [768], replicated, may hold values from -0.875 to 0.875
- qkv_weight: bfloat16 [768, 2304], replicated, may hold values from -0.21875 to 0.21875
- qv_bias: float32 [1536], replicated, may hold values from -0.1875 to 0.1875
- out_weight: bfloat16 [768, 768], replicated, may hold values from -2.5 to 2.5
- out_bias: float32 [768], replicated, may hold values from -0.875 to 0.875
- norm2_gain: float32 [768], replicated, may hold values from 0.5 to 1.5
- norm2_bias: float32 [768], replicated, may hold values from -0.875 to 0.875
- router: bfloat16 [768, 8], replicated, may hold values from -0.15625 to 0.15625
- expert_in: bfloat16 [8, 768, 3072], P('expert'), may hold values from -0.21875 to 0.21875
- expert_in_bias: float32 [8, 3072], P('expert'), may hold values from -0.625 to 0.625
- expert_out: bfloat16 [8, 3072, 768], P('expert'), may hold values from -0.21875 to 0.21875
- expert_out_bias: float32 [8, 768], P('expert'), may hold values from -0.875 to 0.875
- cotangent: bfloat16 [18432, 768], P(('dp', 'expert')), may hold values from -6 to 6
Outputs:
- output: bfloat16 [18432, 768], P(('dp', 'expert'))
- grad_patches: bfloat16 [18432, 768], P(('dp', 'expert'))
- grad_norm1_gain: float32 [768], P('expert')
- grad_norm1_bias: float32 [768], P('expert')
- grad_qkv_weight: float32 [768, 2304], P('expert')
- grad_qv_bias: float32 [1536], P('expert')
- grad_out_weight: float32 [768, 768], P('expert')
- grad_out_bias: float32 [768], P('expert')
- grad_norm2_gain: float32 [768], P('expert')
- grad_norm2_bias: float32 [768], P('expert')
- grad_router: float32 [768, 8], P('expert')
- grad_expert_in: float32 [8, 768, 3072], P('expert', None, 'dp')
- grad_expert_in_bias: float32 [8, 3072], P('expert', 'dp')
- grad_expert_out: float32 [8, 3072, 768], P('expert', 'dp')
- grad_expert_out_bias: float32 [8, 768], P('expert', 'dp')
Inputs may be any that keep to these rules, and one draw needn't show every extreme that they name: `padding`: 1 marks a real patch; in each image of 576 patches the ones form a prefix of 504 patches or more. `expert_ids`: each patch names two different experts; among the patches of one device no expert is named by more than 192 of them, a bound that some block reaches. `priority`: every rank occurs once; a lower rank is served first.
All inputs are finite; a program needn't handle non-finite values.
Results may differ from a plain program's by a relative error of at most 0.02.
Values may be sent and summed in bfloat16 or wider, within the bound.
A program may use at most 384 MiB of HBM per device.

v0:
```python
from functools import partial

import jax
import jax.numpy as jnp
from jax import lax
from jax.sharding import PartitionSpec as P

HEADS = 12
HEAD_DIM = 64
SEQ_LEN = 576


def normalize(values, gain, shift):
    centred = values - jnp.mean(values, axis=-1, keepdims=True)
    inverse = lax.rsqrt(jnp.mean(centred * centred, axis=-1, keepdims=True) + 1e-06)
    return centred * inverse * gain + shift


def exact_gelu(values):
    return jax.nn.gelu(values, approximate=False)


def choose_gates(logits, expert_ids):
    row_peak = jnp.max(logits, axis=-1, keepdims=True)
    raised = jnp.exp(logits - row_peak)
    probabilities = raised / jnp.sum(raised, axis=-1, keepdims=True)
    matches = expert_ids[:, :, None] == jnp.arange(logits.shape[-1], dtype=jnp.int32)[None, None, :]
    picked = jnp.sum(jnp.where(matches, probabilities[:, None, :], 0.0), axis=-1)
    return picked / jnp.sum(picked, axis=1, keepdims=True)


def head_scores(queries, key_rows, key_valid):
    scores = jnp.einsum(
        "qhd,khd->hqk", queries, key_rows, preferred_element_type=jnp.float32
    ) * HEAD_DIM ** (-0.5)
    return jnp.where(key_valid[None, None, :], scores, -1000000000.0)


def attend_forward(pieces):
    queries, key_rows, value_rows, key_valid = pieces
    scores = head_scores(queries, key_rows, key_valid)
    row_peak = jnp.max(scores, axis=-1, keepdims=True)
    raised = jnp.exp(scores - row_peak)
    row_total = jnp.sum(raised, axis=-1, keepdims=True)
    weights = (raised / row_total).astype(jnp.bfloat16)
    attention_output = jnp.einsum(
        "hqk,khd->qhd", weights, value_rows, preferred_element_type=jnp.float32
    )
    return (attention_output.astype(jnp.bfloat16), row_peak, row_total)


def attend_backward(pieces):
    queries, key_rows, value_rows, key_valid, row_peak, row_total, d_attended = pieces
    scores = head_scores(queries, key_rows, key_valid)
    probabilities = jnp.exp(scores - row_peak) / row_total
    weights = probabilities.astype(jnp.bfloat16)
    d_values = jnp.einsum("hqk,qhd->khd", weights, d_attended, preferred_element_type=jnp.float32)
    d_weights = jnp.einsum(
        "qhd,khd->hqk", d_attended, value_rows, preferred_element_type=jnp.float32
    )
    centre = jnp.sum(probabilities * d_weights, axis=-1, keepdims=True)
    d_scores = (probabilities * (d_weights - centre)).astype(jnp.bfloat16)
    scaling = HEAD_DIM ** (-0.5)
    d_queries = (
        jnp.einsum("hqk,khd->qhd", d_scores, key_rows, preferred_element_type=jnp.float32) * scaling
    )
    d_keys = (
        jnp.einsum("hqk,qhd->khd", d_scores, queries, preferred_element_type=jnp.float32) * scaling
    )
    return (d_queries, d_keys, d_values)


def local(
    patches,
    padding,
    expert_ids,
    priority,
    norm1_gain,
    norm1_bias,
    qkv_weight,
    qv_bias,
    out_weight,
    out_bias,
    norm2_gain,
    norm2_bias,
    router,
    expert_in,
    expert_in_bias,
    expert_out,
    expert_out_bias,
    cotangent,
):
    row_count = patches.shape[0]
    model_width = patches.shape[1]
    image_count = row_count // SEQ_LEN
    expert_count = expert_in.shape[0] * lax.axis_size("expert")
    total_rows = row_count * lax.axis_size(("dp", "expert"))
    capacity = (210 * total_rows + 100 * expert_count - 1) // (100 * expert_count)
    most_rows = 8 * row_count // (3 * expert_count)
    slot_count = expert_count * most_rows
    valid_rows = padding > 0
    expert_range = jnp.arange(expert_count, dtype=jnp.int32)
    routing_rows = jnp.stack([priority, expert_ids[:, 0], expert_ids[:, 1], padding])
    table = lax.all_gather(routing_rows, ("dp", "expert"), axis=1, tiled=True)
    table_rank = table[0]
    pair_code = jnp.where(table[3][None, :] > 0, table[1:3], expert_count)
    by_rank = jnp.zeros((2, total_rows), jnp.int32).at[:, table_rank].set(pair_code)
    rank_blocks = by_rank.reshape(2, total_rows // 256, 256)
    block_counts = jnp.sum(
        rank_blocks[:, None, :, :] == expert_range[None, :, None, None], axis=-1, dtype=jnp.int32
    )
    block_start = jnp.cumsum(block_counts, axis=2) - block_counts
    slot_loads = jnp.sum(block_counts, axis=2)
    block_index = priority // 256
    inside_rows = rank_blocks[:, block_index]
    earlier = jnp.arange(256, dtype=jnp.int32)[None, :] < (priority % 256)[:, None]
    ids_by_choice = expert_ids.T
    same_before = jnp.sum(
        (inside_rows == ids_by_choice[:, :, None]) & earlier[None, :, :], axis=-1, dtype=jnp.int32
    )
    start_counts = block_start[
        jnp.arange(2, dtype=jnp.int32)[:, None], ids_by_choice, block_index[None, :]
    ]
    first_loads = jnp.sum(
        jnp.where(expert_ids[:, 1:2] == expert_range[None, :], slot_loads[0][None, :], 0), axis=1
    )
    shifted = jnp.concatenate([jnp.zeros((row_count, 1), jnp.int32), first_loads[:, None]], axis=1)
    position = (start_counts + same_before).T + shifted
    kept_pairs = valid_rows[:, None] & (position < capacity)
    inputs = patches.astype(jnp.float32)
    first_normed = normalize(inputs, norm1_gain, norm1_bias).astype(jnp.bfloat16)
    projection_bias = jnp.concatenate(
        [qv_bias[:model_width], jnp.zeros((model_width,), jnp.float32), qv_bias[model_width:]]
    )
    projected_output = (
        jnp.dot(first_normed, qkv_weight, preferred_element_type=jnp.float32) + projection_bias
    ).astype(jnp.bfloat16)
    split_heads = projected_output.reshape(image_count, SEQ_LEN, 3, HEADS, HEAD_DIM)
    queries = split_heads[:, :, 0]
    key_rows = split_heads[:, :, 1]
    value_rows = split_heads[:, :, 2]
    key_valid = valid_rows.reshape(image_count, SEQ_LEN)
    attention_output, row_peak, row_total = lax.map(
        attend_forward, (queries, key_rows, value_rows, key_valid)
    )
    attended_flat = attention_output.reshape(row_count, model_width)
    residual = (
        inputs + jnp.dot(attended_flat, out_weight, preferred_element_type=jnp.float32) + out_bias
    )
    second_normed = normalize(residual, norm2_gain, norm2_bias).astype(jnp.bfloat16)
    logits = jnp.dot(second_normed, router, preferred_element_type=jnp.float32)
    gate_values, gate_pull = jax.vjp(partial(choose_gates, expert_ids=expert_ids), logits)
    pair_expert = expert_ids.reshape(-1)
    pair_kept = kept_pairs.reshape(-1)
    expert_hits = ((pair_expert[:, None] == expert_range[None, :]) & pair_kept[:, None]).astype(
        jnp.int32
    )
    local_place = jnp.sum((jnp.cumsum(expert_hits, axis=0) - expert_hits) * expert_hits, axis=1)
    slot_index = pair_expert * most_rows + local_place
    slot_target = jnp.where(pair_kept, slot_index, slot_count)
    slot_pair = (
        jnp.zeros((slot_count,), jnp.int32)
        .at[slot_target]
        .set(jnp.arange(2 * row_count, dtype=jnp.int32), mode="drop")
    )
    slot_live = jnp.zeros((slot_count,), jnp.bool_).at[slot_target].set(True, mode="drop")
    pair_slot = jnp.where(pair_kept, slot_index, 0)
    sent_rows = jnp.where(
        slot_live[:, None],
        jnp.take(second_normed, slot_pair // 2, axis=0),
        jnp.zeros((), jnp.bfloat16),
    )
    received = lax.all_to_all(
        sent_rows.reshape(expert_count, most_rows, model_width),
        "expert",
        split_axis=0,
        concat_axis=1,
        tiled=True,
    )
    hidden_pre = (
        jnp.einsum("erd,edf->erf", received, expert_in, preferred_element_type=jnp.float32)
        + expert_in_bias[:, None, :]
    )
    hidden = exact_gelu(hidden_pre).astype(jnp.bfloat16)
    produced = (
        jnp.einsum("erf,efd->erd", hidden, expert_out, preferred_element_type=jnp.float32)
        + expert_out_bias[:, None, :]
    ).astype(jnp.bfloat16)
    returned = lax.all_to_all(produced, "expert", split_axis=1, concat_axis=0, tiled=True).reshape(
        slot_count, model_width
    )
    pair_keep = kept_pairs.astype(jnp.float32)
    chosen = (
        jnp.take(returned, pair_slot, axis=0).reshape(row_count, 2, model_width).astype(jnp.float32)
        * pair_keep[:, :, None]
    )
    combined = jnp.sum((gate_values * pair_keep)[:, :, None] * chosen, axis=1)
    output = (residual + combined).astype(jnp.bfloat16)
    d_out = cotangent.astype(jnp.float32)
    d_gate = jnp.sum(d_out[:, None, :] * chosen, axis=-1)
    pair_grad = (
        ((gate_values * pair_keep)[:, :, None] * d_out[:, None, :])
        .astype(jnp.bfloat16)
        .reshape(2 * row_count, model_width)
    )
    grad_slots = jnp.where(
        slot_live[:, None], jnp.take(pair_grad, slot_pair, axis=0), jnp.zeros((), jnp.bfloat16)
    )
    d_received = lax.all_to_all(
        grad_slots.reshape(expert_count, most_rows, model_width),
        "expert",
        split_axis=0,
        concat_axis=1,
        tiled=True,
    )
    d_hidden = jnp.einsum(
        "erd,efd->erf", d_received, expert_out, preferred_element_type=jnp.float32
    )
    gelu_value, gelu_pull = jax.vjp(exact_gelu, hidden_pre)
    d_pre = gelu_pull(d_hidden)[0].astype(jnp.bfloat16)
    d_rows = jnp.einsum(
        "erf,edf->erd", d_pre, expert_in, preferred_element_type=jnp.float32
    ).astype(jnp.bfloat16)
    d_returned = lax.all_to_all(d_rows, "expert", split_axis=1, concat_axis=0, tiled=True).reshape(
        slot_count, model_width
    )
    grad_in_local = jnp.einsum("erd,erf->edf", received, d_pre, preferred_element_type=jnp.float32)
    grad_in_bias_local = jnp.sum(d_pre.astype(jnp.float32), axis=1)
    grad_out_local = jnp.einsum(
        "erf,erd->efd", hidden, d_received, preferred_element_type=jnp.float32
    )
    grad_out_bias_local = jnp.sum(d_received.astype(jnp.float32), axis=1)
    grad_expert_in, grad_expert_in_bias, grad_expert_out, grad_expert_out_bias = (
        lax.psum_scatter(
            grad_in_local.astype(jnp.bfloat16), "dp", scatter_dimension=2, tiled=True
        ).astype(jnp.float32),
        lax.psum_scatter(
            grad_in_bias_local.astype(jnp.bfloat16), "dp", scatter_dimension=1, tiled=True
        ).astype(jnp.float32),
        lax.psum_scatter(
            grad_out_local.astype(jnp.bfloat16), "dp", scatter_dimension=1, tiled=True
        ).astype(jnp.float32),
        lax.psum_scatter(
            grad_out_bias_local.astype(jnp.bfloat16), "dp", scatter_dimension=1, tiled=True
        ).astype(jnp.float32),
    )
    d_logits = gate_pull(d_gate)[0].astype(jnp.bfloat16)
    grad_router = jnp.dot(second_normed.T, d_logits, preferred_element_type=jnp.float32)
    d_pairs = (
        jnp.take(d_returned, pair_slot, axis=0)
        .reshape(row_count, 2, model_width)
        .astype(jnp.float32)
        * pair_keep[:, :, None]
    )
    d_second = jnp.sum(d_pairs, axis=1) + jnp.dot(
        d_logits, router.T, preferred_element_type=jnp.float32
    )
    second_value, second_pull = jax.vjp(normalize, residual, norm2_gain, norm2_bias)
    d_residual_norm, grad_norm2_gain, grad_norm2_bias = second_pull(d_second)
    d_residual = d_out + d_residual_norm
    d_branch = d_residual.astype(jnp.bfloat16)
    grad_out_weight = jnp.dot(attended_flat.T, d_branch, preferred_element_type=jnp.float32)
    grad_out_bias = jnp.sum(d_branch.astype(jnp.float32), axis=0)
    d_attended = (
        jnp.dot(d_branch, out_weight.T, preferred_element_type=jnp.float32)
        .astype(jnp.bfloat16)
        .reshape(image_count, SEQ_LEN, HEADS, HEAD_DIM)
    )
    d_queries, d_keys, d_values = lax.map(
        attend_backward, (queries, key_rows, value_rows, key_valid, row_peak, row_total, d_attended)
    )
    d_projected = (
        jnp.stack([d_queries, d_keys, d_values], axis=2)
        .reshape(row_count, 3 * model_width)
        .astype(jnp.bfloat16)
    )
    grad_qkv_weight = jnp.dot(first_normed.T, d_projected, preferred_element_type=jnp.float32)
    column_sums = jnp.sum(d_projected.astype(jnp.float32), axis=0)
    grad_qv_bias = jnp.concatenate([column_sums[:model_width], column_sums[2 * model_width :]])
    d_first = jnp.dot(d_projected, qkv_weight.T, preferred_element_type=jnp.float32)
    first_value, first_pull = jax.vjp(normalize, inputs, norm1_gain, norm1_bias)
    d_inputs, grad_norm1_gain, grad_norm1_bias = first_pull(d_first)
    grad_patches = (d_residual + d_inputs).astype(jnp.bfloat16)
    part_n1g, part_n1b, part_qkv, part_qvb, part_wo, part_bo, part_n2g, part_n2b, part_router = (
        lax.psum_scatter(
            grad_norm1_gain.astype(jnp.bfloat16), "expert", scatter_dimension=0, tiled=True
        ).astype(jnp.float32),
        lax.psum_scatter(
            grad_norm1_bias.astype(jnp.bfloat16), "expert", scatter_dimension=0, tiled=True
        ).astype(jnp.float32),
        lax.psum_scatter(
            grad_qkv_weight.astype(jnp.bfloat16), "expert", scatter_dimension=0, tiled=True
        ).astype(jnp.float32),
        lax.psum_scatter(
            grad_qv_bias.astype(jnp.bfloat16), "expert", scatter_dimension=0, tiled=True
        ).astype(jnp.float32),
        lax.psum_scatter(
            grad_out_weight.astype(jnp.bfloat16), "expert", scatter_dimension=0, tiled=True
        ).astype(jnp.float32),
        lax.psum_scatter(
            grad_out_bias.astype(jnp.bfloat16), "expert", scatter_dimension=0, tiled=True
        ).astype(jnp.float32),
        lax.psum_scatter(
            grad_norm2_gain.astype(jnp.bfloat16), "expert", scatter_dimension=0, tiled=True
        ).astype(jnp.float32),
        lax.psum_scatter(
            grad_norm2_bias.astype(jnp.bfloat16), "expert", scatter_dimension=0, tiled=True
        ).astype(jnp.float32),
        lax.psum_scatter(
            grad_router.astype(jnp.bfloat16), "expert", scatter_dimension=0, tiled=True
        ).astype(jnp.float32),
    )
    sum_n1g, sum_n1b, sum_qkv, sum_qvb, sum_wo, sum_bo, sum_n2g, sum_n2b, sum_router = (
        lax.psum(part_n1g.astype(jnp.bfloat16), "dp").astype(jnp.float32),
        lax.psum(part_n1b.astype(jnp.bfloat16), "dp").astype(jnp.float32),
        lax.psum(part_qkv.astype(jnp.bfloat16), "dp").astype(jnp.float32),
        lax.psum(part_qvb.astype(jnp.bfloat16), "dp").astype(jnp.float32),
        lax.psum(part_wo.astype(jnp.bfloat16), "dp").astype(jnp.float32),
        lax.psum(part_bo.astype(jnp.bfloat16), "dp").astype(jnp.float32),
        lax.psum(part_n2g.astype(jnp.bfloat16), "dp").astype(jnp.float32),
        lax.psum(part_n2b.astype(jnp.bfloat16), "dp").astype(jnp.float32),
        lax.psum(part_router.astype(jnp.bfloat16), "dp").astype(jnp.float32),
    )
    return (
        output,
        grad_patches,
        sum_n1g,
        sum_n1b,
        sum_qkv,
        sum_qvb,
        sum_wo,
        sum_bo,
        sum_n2g,
        sum_n2b,
        sum_router,
        grad_expert_in,
        grad_expert_in_bias,
        grad_expert_out,
        grad_expert_out_bias,
    )


def solution(mesh):
    return jax.shard_map(
        local,
        mesh=mesh,
        in_specs=(
            P(("dp", "expert"), None),
            P(("dp", "expert")),
            P(("dp", "expert"), None),
            P(("dp", "expert")),
            P(),
            P(),
            P(),
            P(),
            P(),
            P(),
            P(),
            P(),
            P(),
            P("expert", None, None),
            P("expert", None),
            P("expert", None, None),
            P("expert", None),
            P(("dp", "expert"), None),
        ),
        out_specs=(
            P(("dp", "expert"), None),
            P(("dp", "expert"), None),
            P("expert"),
            P("expert"),
            P("expert", None),
            P("expert"),
            P("expert", None),
            P("expert"),
            P("expert"),
            P("expert"),
            P("expert", None),
            P("expert", None, "dp"),
            P("expert", "dp"),
            P("expert", "dp", None),
            P("expert", "dp"),
        ),
        check_vma=False,
    )
```

profile of v0, /device:TPU:0, one launch (start us, length us, event | category | flops | bytes accessed | tf_op | source)
XLA Modules:
  0.0 1247.5 jit_solution(1507527936059185390)
XLA Ops:
  11.4 71.6 %all-gather = s32[32,576,4]{1,2,0:T(4,128)S(1)} all-gather(s32[1,576,4]{1,2,0:T(4,128)S(1)} %add_bitcast_fusion.1), channel_id=1, replica_groups=mesh['dp'=4,'expert'=8] {'dp','expert'}, dimensions={0}, use_global_device_ids=true | all-gather | bytes 304128 | tf_op jit(solution)/shard_map/all_gather | solution.py:104
  95.0 5.9 copy.157
  100.8 50.0 %scatter_custom_fusion = s32[2,18432]{0,1:T(8,128)} fusion(s32[18432]{0:T(1024)} %bitcast.202, s32[18432,2]{1,0:T(8,128)} %copy.157, s32[]{:T(128)} %constant.117.clone.1), kind=kCustom, calls=%fused_computation.52 | custom fusion | bytes 147968 | tf_op jit(solution)/shard_map/scatter | solution.py:107
  150.9 6.5 copy.158
  164.2 9.6 gather_fusion
  175.2 32.1 %gather_fusion.1 = s32[576,2,256]{1,2,0:T(8,128)} fusion(s32[2,72,256]{0,2,1:T(8,128)} %bitcast.179, s32[1024]{0:T(1024)S(1)} %pad_clamp_fusion.3), kind=kCustom, calls=%fused_computation.3 | custom fusion | bytes 2361600 | tf_op jit(solution)/shard_map/gather | solution.py:115
  209.8 28.9 %convert_reduce_fusion = s32[2,576]{0,1:T(8,128)} fusion(s32[576,2,256]{1,2,0:T(8,128)} %gather_fusion.1, s32[2,576]{0,1:T(8,128)} %copy.159, pred[576,256]{1,0:T(8,128)(4,1)S(1)} %iota_compare_fusion.1), kind=kLoop, calls=%fused_computation.11 | loop fusion | flops 1178496 | bytes 1336320 | tf_op jit(solution)/shard_map/reduce_sum | solution.py:118
  265.1 10.1 fusion.57
  275.1 21.9 %fusion.99 = (f32[12,576]{1,0:T(8,128)}, f32[12,576,576]{1,2,0:T(8,128)}) fusion(f32[12,576,576]{1,2,0:T(8,128)} %fusion.57, pred[576]{0:T(1024)(128)(4,1)S(1)} %copy-done.51), kind=kOutput, calls=%fused_computation.224 | output fusion | flops 23888448 | bytes 31878720 | tf_op jit(solution)/shard_map/while/body/eval_jaxpr/sub | solution.py:43
  297.1 8.1 fusion.53
  324.9 6.6 scatter_custom_fusion.2
  334.7 12.1 scatter_custom_fusion.1
  350.9 8.1 gather_fusion.2
  367.6 49.6 %all-to-all-done = bf16[8,192,768]{2,1,0:T(8,128)(2,1)} async-done(((bf16[8,192,768]{2,1,0:T(8,128)(2,1)}), bf16[8,192,768]{2,1,0:T(8,128)(2,1)}, u32[]{:S(2)}, u32[]{:S(2)}) %all-to-all-start) | async-done | bytes 2359328 | tf_op jit(solution)/shard_map/all_to_all | solution.py:173
  417.2 49.7 %multiply_convert_fusion = (bf16[1536,3072]{1,0:T(8,128)(2,1)S(1)}, f32[1536,3072]{1,0:T(8,128)}, f32[1536,3072]{1,0:T(8,128)}) fusion(f32[3072]{0:T(1024)S(1)} %bitcast.205, bf16[1536,768]{1,0:T(8,128)(2,1)} %bitcast.22, bf16[1,768,3072]{2,1,0:T(8,128)(2,1)} %param.33), kind=kOutput, calls=%fused_computation.16 | convolution fusion | flops 7559184384 | bytes 54276096 | tf_op jit(solution)/shard_map/erd,edf->erf/dot_general | solution.py:181
  466.9 7.7 fusion.32
  474.6 33.9 %copy.200 = bf16[1,1536,768]{2,0,1:T(2,128)(2,1)} copy(bf16[1,1536,768]{2,1,0:T(8,128)(2,1)S(1)} %fusion.32) | data formatting | bytes 4718592 | tf_op jit(solution)/shard_map/convert_element_type | solution.py:188
  509.0 25.5 %reduce.22 = bf16[1536,768]{1,0:T(8,128)(2,1)} reduce(bf16[1536,1,768]{2,1,0:T(2,128)(2,1)} %bitcast.180, bf16[]{:T(256)} %broadcast.604), dimensions={1}, to_apply=%bitcast.174.reduce_sub_computation | reduce | bytes 4718594
  534.5 5.9 reshape.650
  548.9 5.5 mul.338
  570.1 28.1 %all-to-all-done.1 = bf16[8,2,73728]{2,1,0:T(2,128)(2,1)} async-done(((bf16[8,2,73728]{2,1,0:T(2,128)(2,1)}), bf16[8,2,73728]{2,1,0:T(2,128)(2,1)}, u32[]{:S(2)}, u32[]{:S(2)}) %all-to-all-start.1) | async-done | bytes 2359328 | tf_op jit(solution)/shard_map/all_to_all | solution.py:189
  598.2 7.1 reshape.651
  609.4 7.8 gather_fusion.4
  617.3 5.5 multiply_reduce_fusion.1
  622.8 8.5 gather_fusion.3
  633.3 57.7 %all_to_all.16 = bf16[8,192,768]{2,1,0:T(8,128)(2,1)S(1)} all-to-all(bf16[8,192,768]{2,1,0:T(8,128)(2,1)S(1)} %select_select_fusion), channel_id=1, replica_groups=mesh['dp'=4,'expert'=8] {'expert'}, dimensions={0} | all-to-all | bytes 4718592 | tf_op jit(solution)/shard_map/all_to_all | solution.py:209
  691.0 24.4 %fusion.102 = (bf16[3072]{0:T(1024)(128)(2,1)}, bf16[1536,3072]{1,0:T(8,128)(2,1)}) fusion(f32[1536,3072]{1,0:T(8,128)} %get-tuple-element.112, bf16[1536,768]{1,0:T(8,128)(2,1)S(1)} %bitcast.191, bf16[1,3072,768]{2,1,0:T(8,128)(2,1)} %param.35, f32[1536,3072]{1,0:T(8,128)} %get-tuple-element.140, f32[3072]{0:T(1024)S(1)} %bitcast.206), kind=kOutput, calls=%fused_computation.227 | convolution fusion | flops 7323251712 | bytes 54282240 | tf_op jit(solution)/shard_map/erd,efd->erf/dot_general | solution.py:216
  715.4 11.5 fusion.35
  726.9 33.8 %copy.199 = bf16[1,1536,768]{2,0,1:T(2,128)(2,1)} copy(bf16[1,1536,768]{2,1,0:T(8,128)(2,1)S(1)} %fusion.35) | data formatting | bytes 4718592 | tf_op jit(solution)/shard_map/convert_element_type | solution.py:223
  760.7 36.0 %reduce.23 = bf16[1536,768]{1,0:T(8,128)(2,1)} reduce(bf16[1536,1,768]{2,1,0:T(2,128)(2,1)} %bitcast.181, bf16[]{:T(256)} %broadcast.604), dimensions={1}, to_apply=%bitcast.173.reduce_sub_computation | reduce | bytes 4718594
  796.7 5.9 reshape.648
  823.4 38.4 %all-to-all-done.3 = bf16[8,2,73728]{2,1,0:T(2,128)(2,1)} async-done(((bf16[8,2,73728]{2,1,0:T(2,128)(2,1)}), bf16[8,2,73728]{2,1,0:T(2,128)(2,1)}, u32[]{:S(2)}, u32[]{:S(2)}) %all-to-all-start.3) | async-done | bytes 2359328 | tf_op jit(solution)/shard_map/all_to_all | solution.py:224
  861.8 7.0 reshape.649
  873.0 7.7 gather_fusion.5
  880.7 5.5 select_convert_fusion.1
  896.9 10.9 multiply_reduce_fusion.2
  918.6 15.5 %multiply_reduce_fusion = (f32[12,576]{1,0:T(8,128)S(1)}, f32[12,576,576]{1,2,0:T(8,128)}) fusion(f32[12,576,576]{1,2,0:T(8,128)} %get-tuple-element.137, f32[12,576]{1,0:T(8,128)} %get-tuple-element.136, bf16[576,12,64]{0,2,1:T(8,128)(2,1)} %bitcast.198, bf16[1,576,3,12,64]{1,4,3,2,0:T(8,128)(2,1)} %bitcast.186), kind=kOutput, calls=%fused_computation.31 | convolution fusion | flops 521544960 | bytes 35654656 | tf_op jit(solution)/shard_map/while/body/eval_jaxpr/qhd,khd->hqk/dot_general | solution.py:58
  934.0 12.2 multiply_convert_fusion.1
  954.8 9.2 fusion.50
  972.1 12.6 %fusion.21 = bf16[1,768,3072]{2,1,0:T(8,128)(2,1)} fusion(bf16[1536,768]{1,0:T(8,128)(2,1)} %bitcast.22, bf16[1536,3072]{1,0:T(8,128)(2,1)} %get-tuple-element.148), kind=kOutput, calls=%fused_computation.54 | convolution fusion | flops 7250116608 | bytes 16515072 | tf_op jit(solution)/shard_map/erd,erf->edf/dot_general | solution.py:227
  984.8 12.4 fusion.22
  1012.2 5.4 fusion.89
  1019.1 36.7 %all-reduce.7 = (bf16[768]{0:T(1024)(128)(2,1)}, bf16[768]{0:T(1024)(128)(2,1)}, bf16[1536]{0:T(1024)(128)(2,1)}, bf16[768]{0:T(1024)(128)(2,1)}, bf16[768]{0:T(1024)(128)(2,1)}, /*index=5*/bf16[768]{0:T(1024)(128)(2,1)}) all-reduce(bf16[768]{0:T(1024)(128)(2,1)} %get-tuple-element.64, ...), channel_id=2, replica_groups=mesh['dp'=4,'expert'=8] {'expert'}, use_global_device_ids=true, to_apply=%region_35.37.clone | all-reduce | flops 5376 | bytes 21504
  1063.3 6.5 all-reduce.8
  1079.4 20.9 %reduce-scatter.14.cloned.1.call-done = bf16[96,2304]{1,0:T(8,128)(2,1)} async-done(((bf16[768,2304]{1,0:T(8,128)(2,1)}), bf16[96,2304]{1,0:T(8,128)(2,1)}) %reduce-scatter.14.cloned.1.call-update) | async-done | bytes 442384 | tf_op jit(solution)/shard_map/reduce_scatter | solution.py:291
  1104.1 46.1 %reduce-scatter.18.cloned.1.call-done = bf16[1,768,768]{2,1,0:T(8,128)(2,1)} async-done(((bf16[1,768,3072]{2,1,0:T(8,128)(2,1)}), bf16[1,768,768]{2,1,0:T(8,128)(2,1)}) %reduce-scatter.18.cloned.1.call-update) | async-done | bytes 1179664 | tf_op jit(solution)/shard_map/reduce_scatter | solution.py:234
  1153.1 47.6 %reduce-scatter.20.cloned.1.call-done = bf16[1,768,768]{2,1,0:T(8,128)(2,1)} async-done(((bf16[1,3072,768]{2,1,0:T(8,128)(2,1)}), bf16[1,768,768]{2,1,0:T(8,128)(2,1)}) %reduce-scatter.20.cloned.1.call-update) | async-done | bytes 1179664 | tf_op jit(solution)/shard_map/reduce_scatter | solution.py:240
  1203.5 33.4 %all-reduce.12.cloned.1.call-done = (bf16[96,2304]{1,0:T(8,128)(2,1)}, bf16[96,768]{1,0:T(8,128)(2,1)}) async-done(((bf16[96,2304]{1,0:T(8,128)(2,1)}, bf16[96,768]{1,0:T(8,128)(2,1)}), (bf16[96,2304]{1,0:T(8,128)(2,1)}, bf16[96,768]{1,0:T(8,128)(2,1)})) %all-reduce.12.cloned.1.call-update) | async-done | bytes 589840 | tf_op jit(solution)/shard_map/psum | solution.py:316
  (294 shorter events, 227.6 us)
Async XLA Ops:
  7.2 248.3 %copy-start = (bf16[768,2304]{1,0:T(8,128)(2,1)S(1)}, bf16[768,2304]{1,0:T(8,128)(2,1)}, u32[]{:S(2)}) copy-start(bf16[768,2304]{1,0:T(8,128)(2,1)} %param.26) | copy-start | bytes 10616836
  150.9 11.2 copy-start.17
  209.8 45.7 %copy-start.47 = (f32[768]{0:T(1024)S(1)}, f32[768]{0:T(1024)}, u32[]{:S(2)}) copy-start(f32[768]{0:T(1024)} %param.24) | copy-start | bytes 9220
  241.7 18.9 %copy-start.44 = (pred[576,2]{0,1:T(4,128)(4,1)}, pred[576,2]{0,1:T(4,128)(4,1)S(1)}, u32[]{:S(2)}) copy-start(pred[576,2]{0,1:T(4,128)(4,1)S(1)} %get-tuple-element.114) | copy-start | bytes 3460
  248.8 73.5 %copy-start.26 = (s32[1152]{0:T(1024)}, s32[1152]{0:T(1024)S(1)}, u32[]{:S(2)}) copy-start(s32[1152]{0:T(1024)S(1)} %eq.97) | copy-start | bytes 13828
  265.1 10.1 copy-start.51
  297.1 8.1 copy-start.5
  297.1 8.1 copy-start.54
  297.1 8.1 copy-start.58
  306.3 52.7 %copy-start.21 = (f32[576]{0:T(1024)}, f32[576]{0:T(1024)S(1)}, u32[]{:S(2)}) copy-start(f32[576]{0:T(1024)S(1)} %broadcast_multiply_fusion.1) | copy-start | bytes 6916
  308.4 50.6 %copy-start.28 = (f32[576]{0:T(1024)}, f32[576]{0:T(1024)S(1)}, u32[]{:S(2)}) copy-start(f32[576]{0:T(1024)S(1)} %fusion.82) | copy-start | bytes 6916
  331.5 27.5 %copy-start.25 = (s32[1536]{0:T(1024)}, s32[1536]{0:T(1024)S(1)}, u32[]{:S(2)}) copy-start(s32[1536]{0:T(1024)S(1)} %scatter_custom_fusion.2) | copy-start | bytes 18436
  362.0 5.0 copy-start.52
  362.0 55.2 %copy-start.56 = (f32[1,3072]{1,0:T(1,128)S(1)}, f32[1,3072]{1,0:T(1,128)}, u32[]{:S(2)}) copy-start(f32[1,3072]{1,0:T(1,128)} %param.34) | copy-start | bytes 36868
  362.0 55.2 %all-to-all-start = ((bf16[8,192,768]{2,1,0:T(8,128)(2,1)}), bf16[8,192,768]{2,1,0:T(8,128)(2,1)}, u32[]{:S(2)}, u32[]{:S(2)}) async-start(bf16[8,192,768]{2,1,0:T(8,128)(2,1)} %select_select_fusion.1), calls=%async_computation | async-start | bytes 4718592 | tf_op jit(solution)/shard_map/all_to_all | solution.py:173
  417.2 49.7 %copy-start.50 = (f32[768]{0:T(1024)S(1)}, f32[768]{0:T(1024)}, u32[]{:S(2)}) copy-start(f32[768]{0:T(1024)} %reduce.16) | copy-start | bytes 9220
  417.2 49.7 %copy-start.53 = (bf16[1,3072,768]{2,1,0:T(8,128)(2,1)S(1)}, bf16[1,3072,768]{2,1,0:T(8,128)(2,1)}, u32[]{:S(2)}) copy-start(bf16[1,3072,768]{2,1,0:T(8,128)(2,1)} %param.35) | copy-start | bytes 14155780
  466.9 7.7 copy-start.62
  540.5 57.8 %all-to-all-start.1 = ((bf16[8,2,73728]{2,1,0:T(2,128)(2,1)}), bf16[8,2,73728]{2,1,0:T(2,128)(2,1)}, u32[]{:S(2)}, u32[]{:S(2)}) async-start(bf16[8,2,73728]{2,1,0:T(2,128)(2,1)} %reshape.650), calls=%async_computation.1 | async-start | bytes 4718592 | tf_op jit(solution)/shard_map/all_to_all | solution.py:189
  548.9 5.5 copy-start.45
  548.9 11.4 copy-start.18
  633.3 57.7 %copy-start.57 = (f32[1,3072]{1,0:T(1,128)S(1)}, f32[1,3072]{1,0:T(1,128)}, u32[]{:S(2)}) copy-start(f32[1,3072]{1,0:T(1,128)} %param.34) | copy-start | bytes 36868
  691.0 24.4 %copy-start.8 = (bf16[8,192,768]{2,1,0:T(8,128)(2,1)}, bf16[8,192,768]{2,1,0:T(8,128)(2,1)S(1)}, u32[]{:S(2)}) copy-start(bf16[8,192,768]{2,1,0:T(8,128)(2,1)S(1)} %all_to_all.16) | copy-start | bytes 7077892
  802.6 59.2 %all-to-all-start.3 = ((bf16[8,2,73728]{2,1,0:T(2,128)(2,1)}), bf16[8,2,73728]{2,1,0:T(2,128)(2,1)}, u32[]{:S(2)}, u32[]{:S(2)}) async-start(bf16[8,2,73728]{2,1,0:T(2,128)(2,1)} %reshape.648), calls=%async_computation.3 | async-start | bytes 4718592 | tf_op jit(solution)/shard_map/all_to_all | solution.py:224
  807.0 192.9 %reduce-scatter.22.cloned.1.call-start = ((), (), s32[]{:S(2)}) async-start(), calls=%async_computation.15 | async-start | bytes 221184
  818.2 183.1 %reduce-scatter.26.cloned.1.call-start = ((), (), s32[]{:S(2)}) async-start(), calls=%async_computation.17 | async-start | bytes 245760
  821.2 182.8 %reduce-scatter.24.cloned.1.call-start = ((), (), s32[]{:S(2)}) async-start(), calls=%async_computation.16 | async-start | bytes 983040
  823.3 256.1 %reduce-scatter.16.cloned.1.call-start = ((), (), s32[]{:S(2)}) async-start(), calls=%async_computation.12 | async-start | bytes 1327104 | tf_op jit(solution)/shard_map/reduce_scatter | solution.py:297
  868.8 4.2 copy-start.23
  873.0 7.7 copy-start.46
  896.8 11.0 copy-start.2
  896.8 11.0 copy-start.20
  896.8 11.0 copy-start.22
  896.8 11.0 copy-start.29
  896.8 11.0 copy-start.33
  896.8 11.0 copy-start.34
  896.9 11.0 copy-start.37
  918.6 15.5 %copy-start.36 = (f32[12,576]{1,0:T(8,128)S(1)}, f32[12,576]{1,0:T(8,128)}, u32[]{:S(2)}) copy-start(f32[12,576]{1,0:T(8,128)} %get-tuple-element.136) | copy-start | bytes 82948
  934.0 12.2 copy-start.3
  954.8 145.5 %reduce-scatter.14.cloned.1.call-start = ((), (), s32[]{:S(2)}) async-start(), calls=%async_computation.11 | async-start | bytes 3981312 | tf_op jit(solution)/shard_map/reduce_scatter | solution.py:291
  954.8 9.2 copy-start.11
  954.8 9.2 copy-start.12
  972.1 178.1 %reduce-scatter.18.cloned.1.call-start = ((), (), s32[]{:S(2)}) async-start(), calls=%async_computation.13 | async-start | bytes 5898240 | tf_op jit(solution)/shard_map/reduce_scatter | solution.py:234
  984.8 215.8 %reduce-scatter.20.cloned.1.call-start = ((), (), s32[]{:S(2)}) async-start(), calls=%async_computation.14 | async-start | bytes 5898240 | tf_op jit(solution)/shard_map/reduce_scatter | solution.py:240
  997.3 239.6 %all-reduce.12.cloned.1.call-start = ((), (), s32[]{:S(2)}) async-start(), calls=%async_computation.18 | async-start | bytes 1179648 | tf_op jit(solution)/shard_map/psum | solution.py:316
  1012.2 5.4 copy-start.41
  1012.2 5.5 copy-start.7
  1012.2 5.5 copy-start.49
  (26 other events, 43.9 us)
Sparse Core Ops, SparseCore 0:
  818.3 75.7 reduce-scatter.21
  896.5 18.7 reduce-scatter.25
  917.9 23.2 reduce-scatter.23
  954.9 62.9 reduce-scatter.15
  1021.8 78.4 reduce-scatter.13
  1102.8 47.3 reduce-scatter.17
  1152.7 47.8 reduce-scatter.19
  1203.3 33.5 all-reduce.11
where the time goes:
time: 1250 us
  local copies, waits for them, and re-layouts  355 us (28%)
  waiting for transfers between devices  264 us (21%)
  other arithmetic  233 us (19%)
  matrix products  192 us (15%)
  blocking collectives  172 us (14%)
  between operations  16.4 us (1%)
  starting transfers between devices  14.3 us (1%)
    all_gather x1, blocking collectives, local(): table = lax.all_gather(routing_rows, ('dp', 'expert'), axis=1, tiled=True)  71.6 us
    unnamed x148, local copies, waits for them, and re-layouts  63.2 us
    unnamed x5, other arithmetic  63.1 us
    all_to_all x1, blocking collectives, local(): lax.all_to_all(grad_slots.reshape(expert_count, most_rows, model_width),...  57.7 us
    scatter x1, local copies, waits for them, and re-layouts, local(): jnp.zeros((2, total_rows), jnp.int32).at[:, table_rank].set(pair_code)  50 us
    dot_general x1, matrix products, local(): jnp.einsum('erd,edf->erf', received, expert_in, preferred_element_type=jn...  49.7 us
    all_to_all x1, waiting for transfers between devices, local(): lax.all_to_all(sent_rows.reshape(expert_count, most_rows, model_width), '...  49.6 us
    reduce_scatter x1, waiting for transfers between devices, local(): lax.psum_scatter(grad_out_local.astype(jnp.bfloat16), 'dp', scatter_dimen...  47.6 us
  transfers between devices with their start and end apart: 11, of which 7 were waited for; matrix products, arithmetic and copies ran while one was open for 18% of the time, Pallas kernels for 0%

commit v1 on v0

v1 whole, which is shorter than its diff:
```python
from functools import partial

import jax
import jax.numpy as jnp
from jax import lax
from jax.experimental import pallas as pl
from jax.experimental.pallas import tpu as pltpu
from jax.sharding import PartitionSpec as P

HEADS = 12
HEAD_DIM = 64
SEQ_LEN = 576
LOG2E = 1.4426950408889634
EPS = 1e-06
MESH = pl.DeviceIdType.MESH
NN = (((1,), (0,)), ((), ()))
NT = (((1,), (1,)), ((), ()))
TN = (((0,), (0,)), ((), ()))
VMEM_BYTES = 60 << 20
bf16 = jnp.bfloat16
f32 = jnp.float32
i32 = jnp.int32


def dot(a, b, dims=NN):
    return lax.dot_general(a, b, dims, preferred_element_type=f32)


def iota(shape, axis):
    return lax.broadcasted_iota(i32, shape, axis)


def ones_where(mask):
    return jnp.where(mask, 1.0, 0.0).astype(bf16)


def standardize(values):
    centred = values - jnp.mean(values, axis=-1, keepdims=True)
    inverse = lax.rsqrt(jnp.mean(centred * centred, axis=-1, keepdims=True) + EPS)
    return centred * inverse, inverse


def greet(peers):
    barrier = pltpu.get_barrier_semaphore()
    for peer in peers:
        pl.semaphore_signal(barrier, inc=1, device_id=peer, device_id_type=MESH)
    pl.semaphore_wait(barrier, len(peers))


def send(src, dst, send_sem, recv_sem, peer):
    copy = pltpu.make_async_remote_copy(
        src_ref=src, dst_ref=dst, send_sem=send_sem, recv_sem=recv_sem,
        device_id=peer, device_id_type=MESH,
    )
    copy.start()
    return copy


def front_kernel(
    copies, experts, most, capacity,
    patches_ref, cot_ref, rows_ref, cols_ref, gain1_ref, bias1_ref, qkv_w_ref, qv_bias_ref,
    out_w_ref, out_bias_ref, gain2_ref, bias2_ref, router_ref,
    recv_cot_ref, x_slots_ref, gate_slots_ref, qkv_ref, att_t_ref, lse_ref, residual_ref,
    second_ref, first_ref, pairs_ref, probs_ref,
    cot_send, table, counts, cot_ss, cot_rs, near_ss, near_rs, far_ss, far_rs,
):
    me_dp = lax.axis_index("dp")
    me = lax.axis_index("expert")
    rows, width = patches_ref.shape
    greet(
        [(me_dp, me ^ o) for o in range(1, experts)]
        + [(me_dp ^ p, me) for p in range(1, copies)]
    )
    near = [
        send(rows_ref, table.at[0, o], near_ss.at[o], near_rs.at[o], (me_dp, me ^ o))
        for o in range(1, experts)
    ]
    table[0, 0] = rows_ref[...]
    id0_row, id1_row = rows_ref[1:2, :] ^ me, rows_ref[2:3, :] ^ me
    expert_rows = iota((experts, rows), 0)
    named_t = ones_where((expert_rows == id0_row) | (expert_rows == id1_row))
    before_t = ones_where(iota((rows, rows), 0) < iota((rows, rows), 1))
    place_t = dot(named_t, before_t).astype(i32) + expert_rows * most
    slot0_row = jnp.sum(jnp.where(expert_rows == id0_row, place_t, 0), axis=0, keepdims=True)
    slot1_row = jnp.sum(jnp.where(expert_rows == id1_row, place_t, 0), axis=0, keepdims=True)
    id0_col, id1_col = cols_ref[:, 1:2], cols_ref[:, 2:3]
    rel0_col, rel1_col = id0_col ^ me, id1_col ^ me
    expert_cols = iota((rows, experts), 1)
    named = ones_where((expert_cols == rel0_col) | (expert_cols == rel1_col))
    before = ones_where(iota((rows, rows), 1) < iota((rows, rows), 0))
    place = dot(before, named).astype(i32) + expert_cols * most
    slot0_col = jnp.sum(jnp.where(expert_cols == rel0_col, place, 0), axis=1, keepdims=True)
    slot1_col = jnp.sum(jnp.where(expert_cols == rel1_col, place, 0), axis=1, keepdims=True)

    def taken(o):
        slots = iota((most, rows), 0) + o * most
        return ones_where((slots == slot0_row) | (slots == slot1_row))

    cot_value = cot_ref[...]
    cots = []
    for o in [*range(1, experts), 0]:
        picked = dot(taken(o), cot_value).astype(bf16)
        if o == 0:
            recv_cot_ref[0:most, :] = picked
            continue
        part = pl.ds(o * most, most)
        cot_send[part, :] = picked
        cots.append(
            send(cot_send.at[part], recv_cot_ref.at[part], cot_ss.at[o], cot_rs.at[o], (me_dp, me ^ o))
        )
    inputs = patches_ref[...].astype(f32)
    first = (standardize(inputs)[0] * gain1_ref[...] + bias1_ref[...]).astype(bf16)
    first_ref[...] = first
    qkv_ref[:, :width] = (dot(first, qkv_w_ref[:, :width]) + qv_bias_ref[:, :width]).astype(bf16)
    qkv_ref[:, width : 2 * width] = dot(first, qkv_w_ref[:, width : 2 * width]).astype(bf16)
    qkv_ref[:, 2 * width :] = (
        dot(first, qkv_w_ref[:, 2 * width :]) + qv_bias_ref[:, width:]
    ).astype(bf16)
    key_bias = jnp.where(cols_ref[:, 3:4] > 0, 0.0, -1e30)
    scale = LOG2E * HEAD_DIM ** (-0.5)
    pair_width = 2 * HEAD_DIM

    for near_copy in near:
        near_copy.wait_recv()
    far = [
        send(table.at[0], table.at[p], far_ss.at[p], far_rs.at[p], (me_dp ^ p, me))
        for p in range(1, copies)
    ]

    def attend(pair, _):
        base = pl.multiple_of(pair * pair_width, pair_width)
        q = qkv_ref[:, pl.ds(base, pair_width)]
        k = qkv_ref[:, pl.ds(base + width, pair_width)]
        v_t = qkv_ref[:, pl.ds(base + 2 * width, pair_width)].T
        lanes = iota((rows, pair_width), 1)
        outs, stats = [], []
        for a in range(2):
            k_a = jnp.where((lanes >= HEAD_DIM) == (a == 1), k, jnp.zeros((), bf16))
            scores = dot(k_a, q, NT) + key_bias
            peak = jnp.max(scores, axis=0, keepdims=True)
            raised = jnp.exp2(scores * scale - peak * scale)
            total = jnp.sum(raised, axis=0, keepdims=True)
            out = dot(v_t[a * HEAD_DIM : (a + 1) * HEAD_DIM, :], raised.astype(bf16))
            outs.append(out / total)
            stats.append(peak * scale + jnp.log2(total))
        att_t_ref[pl.ds(base, pair_width), :] = jnp.concatenate(outs, axis=0).astype(bf16)
        lse_ref[pair] = jnp.concatenate(stats + [jnp.zeros((6, rows), f32)], axis=0)
        return 0

    lax.fori_loop(0, HEADS // 2, attend, 0)
    residual = inputs + dot(att_t_ref[...], out_w_ref[...], TN) + out_bias_ref[...]
    residual_ref[...] = residual
    second = (standardize(residual)[0] * gain2_ref[...] + bias2_ref[...]).astype(bf16)
    second_ref[...] = second
    for o in range(experts):
        x_slots_ref[pl.ds(o * most, most), :] = dot(taken(o), second).astype(bf16)
    logits = dot(second, router_ref[...])
    raised = jnp.exp(logits - jnp.max(logits, axis=-1, keepdims=True))
    probs = raised / jnp.sum(raised, axis=-1, keepdims=True)
    probs_ref[...] = probs
    prob0 = jnp.sum(jnp.where(expert_cols == id0_col, probs, 0.0), axis=1, keepdims=True)
    prob1 = jnp.sum(jnp.where(expert_cols == id1_col, probs, 0.0), axis=1, keepdims=True)
    both = prob0 + prob1
    gate0, gate1 = prob0 / both, prob1 / both
    for far_copy in far:
        far_copy.wait_recv()
    counts[...] = jnp.zeros_like(counts)
    rank_col = cols_ref[:, 0:1]

    def count(block, _):
        entry = table[block // experts, block % experts]
        real = entry[3:4, :] > 0
        hits = jnp.concatenate(
            [
                ones_where((expert_rows == entry[1:2, :]) & real),
                ones_where((expert_rows == entry[2:3, :]) & real),
            ],
            axis=0,
        )
        lower = ones_where(entry[0:1, :] < rank_col)
        counts[:rows, :] += dot(lower, hits, NT)
        counts[rows:, :] += dot(jnp.ones((8, rows), bf16), hits, NT)
        return 0

    lax.fori_loop(0, copies * experts, count, 0)
    both_cols = iota((rows, 2 * experts), 1)
    ahead = counts[:rows, :]
    loads = counts[rows : rows + 1, :]
    position0 = jnp.sum(jnp.where(both_cols == id0_col, ahead, 0.0), axis=1, keepdims=True)
    position1 = jnp.sum(
        jnp.where(both_cols == id1_col + experts, ahead, 0.0)
        + jnp.where(both_cols == id1_col, loads, 0.0),
        axis=1,
        keepdims=True,
    )
    real_col = cols_ref[:, 3:4] > 0
    kept0 = jnp.where(real_col & (position0 < capacity), 1.0, 0.0)
    kept1 = jnp.where(real_col & (position1 < capacity), 1.0, 0.0)
    gate0, gate1 = gate0 * kept0, gate1 * kept1
    for o in range(experts):
        slots = iota((rows, most), 1) + o * most
        gates = jnp.where(slots == slot0_col, gate0, 0.0) + jnp.where(slots == slot1_col, gate1, 0.0)
        gate_slots_ref[o] = jnp.broadcast_to(jnp.sum(gates, axis=0, keepdims=True), (8, most))
    lanes = iota((rows, 8), 1)
    columns = [slot0_col.astype(f32), slot1_col.astype(f32), gate0, gate1, kept0, kept1, both]
    packed = jnp.zeros((rows, 8), f32)
    for i, column in enumerate(columns):
        packed = jnp.where(lanes == i, column, packed)
    pairs_ref[...] = packed
    for copy in near + far:
        copy.wait_send()
    for copy in cots:
        copy.wait()


VMEM = pl.BlockSpec(memory_space=pltpu.VMEM)
HBM = pl.BlockSpec(memory_space=pl.ANY)
DMA = pltpu.SemaphoreType.DMA


def run_front(copies, experts, most, capacity, *operands):
    rows, width = operands[0].shape
    slots = experts * most
    shape = jax.ShapeDtypeStruct
    return pl.pallas_call(
        partial(front_kernel, copies, experts, most, capacity),
        out_shape=(
            shape((slots, width), bf16),
            shape((slots, width), bf16),
            shape((experts, 8, most), f32),
            shape((rows, 3 * width), bf16),
            shape((width, rows), bf16),
            shape((HEADS // 2, 8, rows), f32),
            shape((rows, width), f32),
            shape((rows, width), bf16),
            shape((rows, width), bf16),
            shape((rows, 8), f32),
            shape((rows, experts), f32),
        ),
        in_specs=[VMEM] * 13,
        out_specs=(VMEM,) * 11,
        scratch_shapes=[
            pltpu.VMEM((slots, width), bf16),
            pltpu.VMEM((copies, experts, 8, rows), i32),
            pltpu.VMEM((rows + 8, 2 * experts), f32),
            DMA((experts,)), DMA((experts,)),
            DMA((experts,)), DMA((experts,)),
            DMA((copies,)), DMA((copies,)),
        ],
        compiler_params=pltpu.CompilerParams(
            collective_id=0, has_side_effects=True, vmem_limit_bytes=VMEM_BYTES
        ),
        name="front",
    )(*operands)


def exact_gelu(values):
    return jax.nn.gelu(values, approximate=False)


def normalize(values, gain, shift):
    return standardize(values)[0] * gain + shift


def attend_backward(pieces):
    queries, key_rows, value_rows, key_valid, lse2, d_attended = pieces
    scores = jnp.einsum("qhd,khd->hqk", queries, key_rows, preferred_element_type=f32) * HEAD_DIM ** (-0.5)
    scores = jnp.where(key_valid[None, None, :], scores, -1000000000.0)
    probabilities = jnp.exp2(scores * LOG2E - lse2[:, :, None])
    weights = probabilities.astype(jnp.bfloat16)
    d_values = jnp.einsum("hqk,qhd->khd", weights, d_attended, preferred_element_type=jnp.float32)
    d_weights = jnp.einsum("qhd,khd->hqk", d_attended, value_rows, preferred_element_type=jnp.float32)
    centre = jnp.sum(probabilities * d_weights, axis=-1, keepdims=True)
    d_scores = (probabilities * (d_weights - centre)).astype(jnp.bfloat16)
    scaling = HEAD_DIM ** (-0.5)
    d_queries = jnp.einsum("hqk,khd->qhd", d_scores, key_rows, preferred_element_type=jnp.float32) * scaling
    d_keys = jnp.einsum("hqk,qhd->khd", d_scores, queries, preferred_element_type=jnp.float32) * scaling
    return (d_queries, d_keys, d_values)


def local(
    patches, padding, expert_ids, priority, norm1_gain, norm1_bias, qkv_weight, qv_bias, out_weight,
    out_bias, norm2_gain, norm2_bias, router, expert_in, expert_in_bias, expert_out, expert_out_bias,
    cotangent,
):
    row_count, width = patches.shape
    copies, experts = lax.axis_size("dp"), lax.axis_size("expert")
    total_rows = row_count * copies * experts
    capacity = (210 * total_rows + 100 * experts - 1) // (100 * experts)
    most = 8 * row_count // (3 * experts)
    me = lax.axis_index("expert")
    facts = [priority, expert_ids[:, 0], expert_ids[:, 1], padding]
    facts = facts + [jnp.zeros_like(padding)] * 4
    (recv_cot, x_slots, gate_slots, qkv, att_t, lse, residual, second, first, pairs, probs) = run_front(
        copies, experts, most, capacity,
        patches, cotangent, jnp.stack(facts), jnp.stack(facts, axis=1),
        norm1_gain[None, :], norm1_bias[None, :], qkv_weight, qv_bias[None, :],
        out_weight, out_bias[None, :], norm2_gain[None, :], norm2_bias[None, :], router,
    )
    order = jnp.arange(experts) ^ me

    def exchange(block):
        block = jnp.take(block.reshape(experts, -1, block.shape[-1]), order, axis=0)
        out = lax.all_to_all(block, "expert", split_axis=0, concat_axis=0, tiled=True)
        return jnp.take(out, order, axis=0)

    received = exchange(x_slots).reshape(-1, width)
    gates = exchange(gate_slots[:, :1, :].reshape(experts, most, 1)).reshape(-1, 1)
    w1, w2 = expert_in[0], expert_out[0]
    hidden_pre = jnp.dot(received, w1, preferred_element_type=f32) + expert_in_bias
    hidden = exact_gelu(hidden_pre).astype(bf16)
    produced = (jnp.dot(hidden, w2, preferred_element_type=f32) + expert_out_bias).astype(bf16)
    d_gate_slots = jnp.sum(produced.astype(f32) * recv_cot.astype(f32), axis=-1, keepdims=True)
    d_produced = (gates * recv_cot.astype(f32)).astype(bf16)
    d_hidden = lax.dot_general(d_produced, w2, NT, preferred_element_type=f32)
    gelu_value, gelu_pull = jax.vjp(exact_gelu, hidden_pre)
    d_pre = gelu_pull(d_hidden)[0].astype(jnp.bfloat16)
    d_rows = lax.dot_general(d_pre, w1, NT, preferred_element_type=f32).astype(bf16)
    g1 = lax.dot_general(received, d_pre, TN, preferred_element_type=f32)
    gb1 = jnp.sum(d_pre.astype(f32), axis=0)
    g2 = lax.dot_general(hidden, d_produced, TN, preferred_element_type=f32)
    gb2 = jnp.sum(d_produced.astype(f32), axis=0)
    scatter = lambda v, d: lax.psum_scatter(v.astype(bf16), "dp", scatter_dimension=d, tiled=True).astype(f32)[None]
    grad_expert_in, grad_expert_in_bias = scatter(g1, 1), scatter(gb1, 0)
    grad_expert_out, grad_expert_out_bias = scatter(g2, 0), scatter(gb2, 0)
    ret_produced = exchange(produced).reshape(-1, width)
    ret_rows = exchange(d_rows).reshape(-1, width)
    ret_gate = exchange(d_gate_slots).reshape(-1, 1)
    slot = pairs[:, :2].astype(i32)
    gk, kept, both = pairs[:, 2:4], pairs[:, 4:6], pairs[:, 6:7]
    chosen = jnp.take(ret_produced, slot.reshape(-1), axis=0).reshape(row_count, 2, width).astype(f32)
    output = (residual + jnp.sum(gk[:, :, None] * chosen, axis=1)).astype(bf16)
    d_gate = jnp.take(ret_gate[:, 0], slot.reshape(-1), axis=0).reshape(row_count, 2) * kept
    matches = expert_ids[:, :, None] == jnp.arange(experts)[None, None, :]
    picked = jnp.sum(jnp.where(matches, probs[:, None, :], 0.0), axis=-1)
    gate = picked / both
    d_picked = (d_gate - jnp.sum(d_gate * gate, axis=1, keepdims=True)) / both
    d_probs = jnp.sum(jnp.where(matches, d_picked[:, :, None], 0.0), axis=1)
    d_logits = (probs * (d_probs - jnp.sum(probs * d_probs, axis=1, keepdims=True))).astype(bf16)
    grad_router = jnp.dot(second.T, d_logits, preferred_element_type=jnp.float32)
    d_pairs = jnp.take(ret_rows, slot.reshape(-1), axis=0).reshape(row_count, 2, width).astype(f32)
    d_second = jnp.sum(d_pairs * kept[:, :, None], axis=1) + jnp.dot(d_logits, router.T, preferred_element_type=f32)
    second_value, second_pull = jax.vjp(normalize, residual, norm2_gain, norm2_bias)
    d_residual_norm, grad_norm2_gain, grad_norm2_bias = second_pull(d_second)
    d_residual = cotangent.astype(f32) + d_residual_norm
    d_branch = d_residual.astype(jnp.bfloat16)
    grad_out_weight = jnp.dot(att_t, d_branch, preferred_element_type=jnp.float32)
    grad_out_bias = jnp.sum(d_branch.astype(jnp.float32), axis=0)
    d_att = jnp.dot(d_branch, out_weight.T, preferred_element_type=jnp.float32).astype(bf16)
    d_att = d_att.reshape(SEQ_LEN, HEADS, HEAD_DIM)
    heads = qkv.reshape(SEQ_LEN, 3, HEADS, HEAD_DIM)
    lse2 = lse[:, :2].reshape(HEADS, row_count)
    d_q, d_k, d_v = attend_backward((heads[:, 0], heads[:, 1], heads[:, 2], padding > 0, lse2, d_att))
    d_projected = jnp.stack([d_q, d_k, d_v], axis=1).reshape(row_count, 3 * width).astype(bf16)
    grad_qkv_weight = jnp.dot(first.T, d_projected, preferred_element_type=jnp.float32)
    column_sums = jnp.sum(d_projected.astype(jnp.float32), axis=0)
    grad_qv_bias = jnp.concatenate([column_sums[:width], column_sums[2 * width :]])
    d_first = jnp.dot(d_projected, qkv_weight.T, preferred_element_type=jnp.float32)
    first_value, first_pull = jax.vjp(normalize, patches.astype(f32), norm1_gain, norm1_bias)
    d_inputs, grad_norm1_gain, grad_norm1_bias = first_pull(d_first)
    grad_patches = (d_residual + d_inputs).astype(jnp.bfloat16)
    dense = [grad_norm1_gain, grad_norm1_bias, grad_qkv_weight, grad_qv_bias, grad_out_weight, grad_out_bias,
             grad_norm2_gain, grad_norm2_bias, grad_router]
    dense = [lax.psum_scatter(g.astype(bf16), "expert", scatter_dimension=0, tiled=True) for g in dense]
    dense = [lax.psum(g, "dp").astype(f32) for g in dense]
    return (output, grad_patches, *dense, grad_expert_in, grad_expert_in_bias, grad_expert_out, grad_expert_out_bias)


def solution(mesh):
    tokens = P(("dp", "expert"))
    wide = P(("dp", "expert"), None)
    return jax.shard_map(
        local,
        mesh=mesh,
        in_specs=(
            wide, tokens, wide, tokens, P(), P(), P(), P(), P(), P(), P(), P(), P(),
            P("expert", None, None), P("expert", None), P("expert", None, None), P("expert", None), wide,
        ),
        out_specs=(
            wide, wide, P("expert"), P("expert"), P("expert", None), P("expert"), P("expert", None),
            P("expert"), P("expert"), P("expert"), P("expert", None), P("expert", None, "dp"),
            P("expert", "dp"), P("expert", "dp", None), P("expert", "dp"),
        ),
        check_vma=False,
    )
```

time: 1250 us -> 700 us (0.56)
  local copies, waits for them, and re-layouts: 355 us -> 94 us
  other arithmetic: 233 us -> 82 us
  blocking collectives: 172 us -> 48.1 us
  waiting for transfers between devices: 264 us -> 184 us
  Pallas kernels: 0 us -> 57.1 us
  starting transfers between devices: 14.3 us -> 31.7 us
  matrix products: 192 us -> 179 us
    reduce_scatter x4, waiting for transfers between devices: 115 us -> 33 us  [the longest x2 33 us: local(): lax.psum_scatter(v.astype(bf16), 'dp', scatter_dimension=d, tiled=True)]
    convert_element_type x7 -> x3, local copies, waits for them, and re-layouts: 86.3 us -> 10.9 us  [the longest x1 5.35 us: local(): jnp.take(ret_produced, slot.reshape(-1), axis=0)]
    all_gather x1 -> x0, blocking collectives: 71.6 us -> none  [local(): table = lax.all_gather(routing_rows, ('dp', 'expert'), axis=1, tiled=True)]
    scatter x3 -> x0, local copies, waits for them, and re-layouts: 68.8 us -> none  [the longest x1 50 us: local(): jnp.zeros((2, total_rows), jnp.int32).at[:, table_rank].set(pair_code)]
    unnamed x5 -> x1, other arithmetic: 63.1 us -> 0.63 us
    all_to_all x1 -> x0, blocking collectives: 57.7 us -> none  [local(): lax.all_to_all(grad_slots.reshape(expert_count, most_rows, model_width),...]
    pallas_call x0 -> x1, Pallas kernels: none -> 57.1 us  [run_front(): pl.pallas_call(partial(front_kernel, copies, experts, most, capacity), ou...]
    unnamed x148 -> x104, local copies, waits for them, and re-layouts: 63.2 us -> 17.6 us
  transfers between devices with their start and end apart: 11 -> 11, of which waited for: 7 -> 7; matrix products, arithmetic and copies ran while one was open for 18% -> 32% of each run, Pallas kernels for 0% -> 0%
where the time goes in v1:
time: 700 us; the launch traced here: 694 us
  waiting for transfers between devices  184 us (26%)
  matrix products  179 us (26%)
  local copies, waits for them, and re-layouts  94 us (13%)
  other arithmetic  82 us (12%)
  Pallas kernels  57.1 us (8%)
  blocking collectives  48.1 us (7%)
  starting transfers between devices  31.7 us (5%)
  between operations  17.6 us (3%)
    all_to_all x5, waiting for transfers between devices, exchange(): lax.all_to_all(block, 'expert', split_axis=0, concat_axis=0, tiled=True)  118 us
    pallas_call x1, Pallas kernels, run_front(): pl.pallas_call(partial(front_kernel, copies, experts, most, capacity), ou...  57.1 us
    dot_general x1, matrix products, local(): jnp.dot(received, w1, preferred_element_type=f32) + expert_in_bias  49.6 us
    unnamed x1, blocking collectives  36 us
    psum x1, waiting for transfers between devices, local(): dense = [lax.psum(g, 'dp').astype(f32) for g in dense]  33.2 us
    reduce_scatter x2, waiting for transfers between devices, local(): lax.psum_scatter(v.astype(bf16), 'dp', scatter_dimension=d, tiled=True)  33 us
    all_to_all x5, starting transfers between devices, exchange(): lax.all_to_all(block, 'expert', split_axis=0, concat_axis=0, tiled=True)  31.3 us
    dot_general x1, matrix products, local(): d_hidden = lax.dot_general(d_produced, w2, NT, preferred_element_type=f32)  23.6 us
  transfers between devices with their start and end apart: 11, of which 7 were waited for; matrix products, arithmetic and copies ran while one was open for 32% of the time, Pallas kernels for 0%

profile of v1, /device:TPU:0, one launch (start us, length us, event | category | flops | bytes accessed | tf_op | source)
XLA Modules:
  0.0 693.6 jit_solution(4437137920336018122)
XLA Ops:
  22.3 57.1 %front.1 = (bf16[1536,768]{1,0:T(8,128)(2,1)}, bf16[1536,768]{1,0:T(8,128)(2,1)}, f32[8,8,192]{2,1,0:T(8,128)}, bf16[576,2304]{1,0:T(8,128)(2,1)}, bf16[768,576]...) custom-call(bf16[576,768]{1,0:T(8,128)(2,1)} %patches_ref.1, ...), custom_call_target="tpu_custom_call" | custom-call | tf_op jit(solution)/shard_map/front/pallas_call | solution.py:225
  79.4 2.4 gather_fusion.1
  83.5 16.1 %all-to-all-start = ((bf16[8,192,768]{2,1,0:T(8,128)(2,1)}), bf16[8,192,768]{2,1,0:T(8,128)(2,1)S(1)}, u32[]{:S(2)}, u32[]{:S(2)}) async-start(bf16[8,192,768]{2,1,0:T(8,128)(2,1)} %broadcast_select_fusion.2), calls=%async_computation | async-start | bytes 4718592 | tf_op jit(solution)/shard_map/all_to_all | solution.py:304
  104.0 49.1 %all-to-all-done = bf16[8,192,768]{2,1,0:T(8,128)(2,1)S(1)} async-done(((bf16[8,192,768]{2,1,0:T(8,128)(2,1)}), bf16[8,192,768]{2,1,0:T(8,128)(2,1)S(1)}, u32[]{:S(2)}, u32[]{:S(2)}) %all-to-all-start) | async-done | bytes 2359328 | tf_op jit(solution)/shard_map/all_to_all | solution.py:304
  157.2 49.6 %multiply_convert_fusion = (bf16[1536,3072]{1,0:T(8,128)(2,1)S(1)}, f32[1536,3072]{1,0:T(8,128)}, f32[1536,3072]{1,0:T(8,128)}) fusion(f32[3072]{0:T(1024)S(1)} %bitcast.135, bf16[1536,768]{1,0:T(8,128)(2,1)S(1)} %bitcast.126, bf16[1,768,3072]{2,1,0:T(8,128)(2,1)} %param.37), kind=kOutput, calls=%fused_computation.16 | convolution fusion | flops 7559184384 | bytes 54276096 | tf_op jit(solution)/shard_map/dot_general | solution.py:310
  207.0 8.8 %fusion.9 = (f32[1536]{0:T(1024)S(1)}, bf16[1536,768]{1,0:T(8,128)(2,1)}) fusion(bf16[1536,768]{1,0:T(8,128)(2,1)S(1)} %copy-done.12, f32[768]{0:T(1024)S(1)} %copy-done.36, bf16[1536,3072]{1,0:T(8,128)(2,1)S(1)} %get-tuple-element.71, bf16[1,3072,768]{2,1,0:T(8,128)(2,1)S(1)} %copy-done.39), kind=kOutput, calls=%fused_computation.42 | convolution fusion | flops 7254833664 | bytes 18883584 | tf_op jit(solution)/shard_map/dot_general | solution.py:312
  217.2 3.6 all-to-all-start.4
  221.6 5.7 all-to-all-done.4
  228.6 3.6 all-to-all-start.2
  233.0 5.5 all-to-all-done.2
  239.3 23.6 %fusion.49 = (bf16[3072]{0:T(1024)(128)(2,1)}, bf16[1536,3072]{1,0:T(8,128)(2,1)}) fusion(f32[1536,3072]{1,0:T(8,128)} %get-tuple-element.72, bf16[1,3072,768]{2,1,0:T(8,128)(2,1)} %param.39, bf16[1536,768]{1,0:T(8,128)(2,1)S(1)} %copy-done.12, f32[1536]{0:T(1024)S(1)} %mul.202, f32[1536,3072]{1,0:T(8,128)} %get-tuple-element.89, f32[3072]{0:T(1024)S(1)} %bitcast.136), kind=kOutput, calls=%fused_computation.148 | convolution fusion | flops 7326790656 | bytes 54288384 | tf_op jit(solution)/shard_map/dot_general | solution.py:315
  262.9 12.5 %fusion.19 = bf16[1536,768]{1,0:T(8,128)(2,1)} fusion(bf16[1536,3072]{1,0:T(8,128)(2,1)} %get-tuple-element.97, bf16[1,768,3072]{2,1,0:T(8,128)(2,1)} %param.37), kind=kOutput, calls=%fused_computation.53 | convolution fusion | flops 7248936960 | bytes 16515072 | tf_op jit(solution)/shard_map/dot_general | solution.py:318
  275.4 2.4 gather_fusion.8
  279.4 3.6 all-to-all-start.3
  283.2 9.3 %gather_fusion = f32[1152]{0:T(1024)} fusion(f32[1536]{0:T(1024)S(1)} %squeeze_reshape.3, s32[2048]{0:T(1024)S(1)} %pad_clamp_fusion), kind=kCustom, calls=%fused_computation.12 | custom fusion | bytes 13824 | tf_op jit(solution)/shard_map/jit(_take)/gather | solution.py:333
  300.7 12.7 %convolution_convert_fusion = bf16[3072,768]{1,0:T(8,128)(2,1)} fusion(bf16[1536,3072]{1,0:T(8,128)(2,1)} %copy-done.44, bf16[1536,768]{1,0:T(8,128)(2,1)} %get-tuple-element.33, f32[1536]{0:T(1024)S(1)} %copy-done.30), kind=kOutput, calls=%fused_computation.38 | convolution fusion | flops 7253655552 | bytes 16521216 | tf_op jit(solution)/shard_map/dot_general | solution.py:321
  313.3 3.9 gather_fusion.3
  317.2 19.2 %all-to-all-done.3 = bf16[8,192,768]{2,1,0:T(8,128)(2,1)S(1)} async-done(((bf16[8,192,768]{2,1,0:T(8,128)(2,1)}), bf16[8,192,768]{2,1,0:T(8,128)(2,1)S(1)}, u32[]{:S(2)}, u32[]{:S(2)}) %all-to-all-start.3) | async-done | bytes 2359328 | tf_op jit(solution)/shard_map/all_to_all | solution.py:304
  336.4 2.2 gather_fusion.9
  338.7 4.3 broadcast_select_fusion.1
  342.9 4.4 all-to-all-start.1
  349.1 5.0 copy.90
  358.2 4.8 gather_fusion.10
  363.0 38.6 %all-to-all-done.1 = bf16[8,192,768]{2,1,0:T(8,128)(2,1)} async-done(((bf16[8,192,768]{2,1,0:T(8,128)(2,1)}), bf16[8,192,768]{2,1,0:T(8,128)(2,1)}, u32[]{:S(2)}, u32[]{:S(2)}) %all-to-all-start.1) | async-done | bytes 2359328 | tf_op jit(solution)/shard_map/all_to_all | solution.py:304
  401.6 3.9 gather_fusion.4
  405.5 2.7 broadcast_select_fusion.5
  408.2 4.8 gather_fusion.5
  413.0 5.7 select_convert_fusion
  418.7 4.0 reshape.243
  422.7 5.3 reshape.242
  428.1 10.1 %multiply_reduce_fusion.1 = (f32[576,768]{1,0:T(8,128)S(1)}, f32[576,768]{1,0:T(8,128)S(1)}) fusion(f32[576,2,768]{2,1,0:T(2,128)S(1)} %reshape.243, f32[576,2]{1,0:T(8,128)} %get-tuple-element.75, f32[576,2,768]{2,1,0:T(2,128)} %reshape.242, f32[576,2]{1,0:T(8,128)} %get-tuple-element.76), kind=kLoop, calls=%fused_computation.51 | loop fusion | flops 2654208 | bytes 10626048 | tf_op jit(solution)/shard_map/reduce_sum | solution.py:342
  446.6 3.6 convolution_convert_fusion.3
  450.5 9.9 %fusion.34 = f32[12,576,576]{1,2,0:T(8,128)} fusion(bf16[576,12,64]{0,2,1:T(8,128)(2,1)S(1)} %bitcast.122, bf16[576,3,12,64]{0,3,2,1:T(8,128)(2,1)} %bitcast.118), kind=kOutput, calls=%fused_computation.91 | convolution fusion | flops 509607936 | bytes 17793024 | tf_op jit(solution)/shard_map/qhd,khd->hqk/dot_general | solution.py:272
  460.4 16.8 %multiply_reduce_fusion = (f32[12,576]{1,0:T(8,128)S(1)}, f32[12,576,576]{1,2,0:T(8,128)}) fusion(f32[12,576,576]{1,2,0:T(8,128)} %fusion.34, f32[12,576]{1,0:T(8,128)S(1)} %copy-done.21, bf16[576,3,12,64]{0,3,2,1:T(8,128)(2,1)S(1)} %bitcast.119, pred[576]{0:T(1024)(128)(4,1)S(1)} %copy-done.38), kind=kOutput, calls=%fused_computation.31 | convolution fusion | flops 537470208 | bytes 33886208 | tf_op jit(solution)/shard_map/qhd,khd->hqk/dot_general | solution.py:267
  477.2 12.1 %multiply_convert_fusion.1 = bf16[12,576,576]{1,2,0:T(8,128)(2,1)S(1)} fusion(f32[12,576,576]{1,2,0:T(8,128)} %get-tuple-element.94, f32[12,576,576]{1,2,0:T(8,128)} %fusion.34, f32[12,576]{1,0:T(8,128)S(1)} %get-tuple-element.93), kind=kLoop, calls=%fused_computation.30 | loop fusion | flops 11943936 | bytes 39840768 | tf_op jit(solution)/shard_map/convert_element_type | solution.py:274
  489.3 2.7 multiply_bitcast_fusion
  493.6 8.7 %fusion.30 = bf16[576,1,12,64]{0,3,2,1:T(8,128)(2,1)S(1)} fusion(bf16[576,12,64]{0,2,1:T(8,128)(2,1)S(1)} %bitcast.123, f32[12,576,576]{1,2,0:T(8,128)} %get-tuple-element.94), kind=kOutput, calls=%fused_computation.82 | convolution fusion | flops 513589248 | bytes 17694720 | tf_op jit(solution)/shard_map/hqk,qhd->khd/dot_general | solution.py:271
  504.7 4.6 convolution_convert_fusion.1
  509.3 12.6 %convolution_convert_fusion.2 = bf16[768,3072]{1,0:T(8,128)(2,1)} fusion(bf16[1536,768]{1,0:T(8,128)(2,1)} %bitcast.127, bf16[1536,3072]{1,0:T(8,128)(2,1)} %get-tuple-element.97), kind=kOutput, calls=%fused_computation.40 | convolution fusion | flops 7250116608 | bytes 16515072 | tf_op jit(solution)/shard_map/dot_general | solution.py:319
  526.6 2.8 fusion.38
  531.6 6.3 fusion.42
  540.6 36.0 %all-reduce.8 = (bf16[768]{0:T(1024)(128)(2,1)}, bf16[768]{0:T(1024)(128)(2,1)}, bf16[1536]{0:T(1024)(128)(2,1)}, bf16[768]{0:T(1024)(128)(2,1)}, bf16[768]{0:T(1024)(128)(2,1)}, /*index=5*/bf16[768]{0:T(1024)(128)(2,1)}) all-reduce(bf16[768]{0:T(1024)(128)(2,1)} %get-tuple-element.42, ...), channel_id=2, replica_groups=mesh['dp'=4,'expert'=8] {'expert'}, use_global_device_ids=true, to_apply=%region_17.21.clone | all-reduce | flops 5376 | bytes 21504
  584.1 12.1 %all-reduce.9 = (bf16[96]{0:T(256)(128)(2,1)}, bf16[96]{0:T(256)(128)(2,1)}, bf16[192]{0:T(256)(128)(2,1)}, bf16[96]{0:T(256)(128)(2,1)}, bf16[96]{0:T(256)(128)...) all-reduce(bf16[96]{0:T(256)(128)(2,1)} %dynamic-slice.1, ...), channel_id=1, replica_groups=mesh['dp'=4,'expert'=8] {'dp'}, use_global_device_ids=true, to_apply=%region_18.22 | all-reduce | flops 5280 | bytes 21120 | tf_op jit(solution)/shard_map/psum | solution.py:365
  607.9 3.1 add_convert_fusion.2
  611.0 2.8 bitcast_convert_fusion
  613.9 33.0 %reduce-scatter.12.cloned.1.call-done = bf16[768,768]{1,0:T(8,128)(2,1)} async-done(((bf16[768,3072]{1,0:T(8,128)(2,1)}), bf16[768,768]{1,0:T(8,128)(2,1)}) %reduce-scatter.12.cloned.1.call-update) | async-done | bytes 1179664 | tf_op jit(solution)/shard_map/reduce_scatter | solution.py:323
  646.9 2.8 bitcast_convert_fusion.1
  649.8 33.2 %all-reduce.13.cloned.1.call-done = (bf16[96,2304]{1,0:T(8,128)(2,1)}, bf16[96,768]{1,0:T(8,128)(2,1)}) async-done(((bf16[96,2304]{1,0:T(8,128)(2,1)}, bf16[96,768]{1,0:T(8,128)(2,1)}), (bf16[96,2304]{1,0:T(8,128)(2,1)}, bf16[96,768]{1,0:T(8,128)(2,1)})) %all-reduce.13.cloned.1.call-update) | async-done | bytes 589840 | tf_op jit(solution)/shard_map/psum | solution.py:365
  (219 shorter events, 88.4 us)
Async XLA Ops:
  7.2 148.0 %copy-start.27 = (pred[8]{0:T(512)(128)(4,1)}, pred[8]{0:T(512)(128)(4,1)S(1)}, u32[]{:S(2)}) copy-start(pred[8]{0:T(512)(128)(4,1)S(1)} %compare_and_fusion.1) | copy-start | bytes 28
  16.4 136.7 %copy-start.33 = (s32[1024]{0:T(1024)}, s32[1024]{0:T(1024)S(1)}, u32[]{:S(2)}) copy-start(s32[1024]{0:T(1024)S(1)} %pad_clamp_fusion.2) | copy-start | bytes 12292
  83.5 16.2 %copy-start.10 = (f32[576,8]{1,0:T(8,128)S(1)}, f32[576,8]{1,0:T(8,128)}, u32[]{:S(2)}) copy-start(f32[576,8]{1,0:T(8,128)} %get-tuple-element.34) | copy-start | bytes 55300
  83.5 16.3 %copy-start.37 = (f32[1,768]{1,0:T(1,128)S(1)}, f32[1,768]{1,0:T(1,128)}, u32[]{:S(2)}) copy-start(f32[1,768]{1,0:T(1,128)} %param.40) | copy-start | bytes 9220
  83.5 16.9 %copy-start.18 = (s32[576,2]{0,1:T(2,128)S(1)}, s32[576,2]{0,1:T(2,128)}, u32[]{:S(2)}) copy-start(s32[576,2]{0,1:T(2,128)} %param.26) | copy-start | bytes 13828
  83.5 17.5 %copy-start.1 = (f32[576,8]{1,0:T(8,128)S(1)}, f32[576,8]{1,0:T(8,128)}, u32[]{:S(2)}) copy-start(f32[576,8]{1,0:T(8,128)} %get-tuple-element.30) | copy-start | bytes 55300
  83.5 69.6 %all-to-all-start = ((bf16[8,192,768]{2,1,0:T(8,128)(2,1)}), bf16[8,192,768]{2,1,0:T(8,128)(2,1)S(1)}, u32[]{:S(2)}, u32[]{:S(2)}) async-start(bf16[8,192,768]{2,1,0:T(8,128)(2,1)} %broadcast_select_fusion.2), calls=%async_computation | async-start | bytes 4718592 | tf_op jit(solution)/shard_map/all_to_all | solution.py:304
  155.2 2.0 copy-start.41
  157.2 49.7 %copy-start.13 = (bf16[8,192,768]{2,1,0:T(8,128)(2,1)}, bf16[8,192,768]{2,1,0:T(8,128)(2,1)S(1)}, u32[]{:S(2)}) copy-start(bf16[8,192,768]{2,1,0:T(8,128)(2,1)S(1)} %broadcast_select_fusion.3) | copy-start | bytes 7077892
  157.2 49.7 %copy-start.12 = (bf16[1536,768]{1,0:T(8,128)(2,1)S(1)}, bf16[1536,768]{1,0:T(8,128)(2,1)}, u32[]{:S(2)}) copy-start(bf16[1536,768]{1,0:T(8,128)(2,1)} %get-tuple-element.33) | copy-start | bytes 7077892
  157.2 49.7 %copy-start.36 = (f32[768]{0:T(1024)S(1)}, f32[768]{0:T(1024)}, u32[]{:S(2)}) copy-start(f32[768]{0:T(1024)} %reduce.5) | copy-start | bytes 9220
  157.2 49.7 %copy-start.39 = (bf16[1,3072,768]{2,1,0:T(8,128)(2,1)S(1)}, bf16[1,3072,768]{2,1,0:T(8,128)(2,1)}, u32[]{:S(2)}) copy-start(bf16[1,3072,768]{2,1,0:T(8,128)(2,1)} %param.39) | copy-start | bytes 14155780
  206.9 9.0 %copy-start.44 = (bf16[1536,3072]{1,0:T(8,128)(2,1)}, bf16[1536,3072]{1,0:T(8,128)(2,1)S(1)}, u32[]{:S(2)}) copy-start(bf16[1536,3072]{1,0:T(8,128)(2,1)S(1)} %get-tuple-element.71) | copy-start | bytes 28311556
  206.9 9.0 %copy-start.34 = (s32[1024]{0:T(1024)S(1)}, s32[1024]{0:T(1024)}, u32[]{:S(2)}) copy-start(s32[1024]{0:T(1024)} %copy-done.33) | copy-start | bytes 12292
  206.9 9.6 %copy-start.28 = (pred[8]{0:T(512)(128)(4,1)S(1)}, pred[8]{0:T(512)(128)(4,1)}, u32[]{:S(2)}) copy-start(pred[8]{0:T(512)(128)(4,1)} %copy-done.27) | copy-start | bytes 28
  206.9 13.9 %copy-start.24 = (f32[576]{0:T(1024)S(1)}, f32[576]{0:T(1024)}, u32[]{:S(2)}) copy-start(f32[576]{0:T(1024)} %slice_reduce_fusion) | copy-start | bytes 6916
  206.9 13.9 %copy-start.35 = (f32[576,2]{0,1:T(2,128)S(1)}, f32[576,2]{0,1:T(2,128)}, u32[]{:S(2)}) copy-start(f32[576,2]{0,1:T(2,128)} %select_reduce_fusion.1) | copy-start | bytes 13828
  207.0 13.9 %copy-start.32 = (f32[8,192,1]{1,2,0:T(1,128)S(1)}, f32[8,192,1]{1,2,0:T(1,128)}, u32[]{:S(2)}) copy-start(f32[8,192,1]{1,2,0:T(1,128)} %slice_bitcast_fusion.8) | copy-start | bytes 18436
  207.0 14.5 %copy-start.9 = (s32[576,2]{1,0:T(8,128)S(1)}, s32[576,2]{1,0:T(8,128)}, u32[]{:S(2)}) copy-start(s32[576,2]{1,0:T(8,128)} %slice_convert_fusion) | copy-start | bytes 13828
  217.2 10.2 %all-to-all-start.4 = ((f32[8,192,1]{1,2,0:T(1,128)}), f32[8,192,1]{1,2,0:T(1,128)S(1)}, u32[]{:S(2)}, u32[]{:S(2)}) async-start(f32[8,192,1]{1,2,0:T(1,128)} %copy.83), calls=%async_computation.4 | async-start | bytes 16384 | tf_op jit(solution)/shard_map/all_to_all | solution.py:304
  228.6 10.0 %all-to-all-start.2 = ((f32[8,192,1]{1,2,0:T(1,128)}), f32[8,192,1]{1,2,0:T(1,128)S(1)}, u32[]{:S(2)}, u32[]{:S(2)}) async-start(f32[8,192,1]{1,2,0:T(1,128)} %copy.82), calls=%async_computation.2 | async-start | bytes 16384 | tf_op jit(solution)/shard_map/all_to_all | solution.py:304
  239.3 23.6 %copy-start.29 = (f32[1536]{0:T(1024)}, f32[1536]{0:T(1024)S(1)}, u32[]{:S(2)}) copy-start(f32[1536]{0:T(1024)S(1)} %mul.202) | copy-start | bytes 18436
  279.4 57.0 %all-to-all-start.3 = ((bf16[8,192,768]{2,1,0:T(8,128)(2,1)}), bf16[8,192,768]{2,1,0:T(8,128)(2,1)S(1)}, u32[]{:S(2)}, u32[]{:S(2)}) async-start(bf16[8,192,768]{2,1,0:T(8,128)(2,1)} %broadcast_select_fusion), calls=%async_computation.3 | async-start | bytes 4718592 | tf_op jit(solution)/shard_map/all_to_all | solution.py:304
  283.1 246.3 %reduce-scatter.16.cloned.1.call-start = ((), (), s32[]{:S(2)}) async-start(), calls=%async_computation.14 | async-start | bytes 221184
  283.2 10.3 %copy-start.2 = (f32[576,8]{1,0:T(8,128)S(1)}, f32[576,8]{1,0:T(8,128)}, u32[]{:S(2)}) copy-start(f32[576,8]{1,0:T(8,128)} %get-tuple-element.30) | copy-start | bytes 55300
  292.5 4.6 copy-start.19
  292.5 4.8 copy-start.11
  296.0 4.7 copy-start.30
  300.6 310.5 %reduce-scatter.14.cloned.1.call-start = ((), (), s32[]{:S(2)}) async-start(), calls=%async_computation.13 | async-start | bytes 5898240 | tf_op jit(solution)/shard_map/reduce_scatter | solution.py:323
  342.9 58.7 %all-to-all-start.1 = ((bf16[8,192,768]{2,1,0:T(8,128)(2,1)}), bf16[8,192,768]{2,1,0:T(8,128)(2,1)}, u32[]{:S(2)}, u32[]{:S(2)}) async-start(bf16[8,192,768]{2,1,0:T(8,128)(2,1)} %get-tuple-element.88), calls=%async_computation.1 | async-start | bytes 4718592 | tf_op jit(solution)/shard_map/all_to_all | solution.py:304
  347.3 266.6 %reduce-scatter.10.cloned.1.call-start = ((), (), s32[]{:S(2)}) async-start(), calls=%async_computation.11 | async-start | bytes 1327104 | tf_op jit(solution)/shard_map/reduce_scatter | solution.py:364
  354.1 3.5 copy-start.25
  428.1 10.2 %copy-start = (f32[576,768]{1,0:T(8,128)S(1)}, f32[576,768]{1,0:T(8,128)}, u32[]{:S(2)}) copy-start(f32[576,768]{1,0:T(8,128)} %get-tuple-element.29) | copy-start | bytes 5308420
  428.1 10.2 %copy-start.15 = (bf16[576,8]{1,0:T(8,128)(2,1)S(1)}, bf16[576,8]{1,0:T(8,128)(2,1)}, u32[]{:S(2)}) copy-start(bf16[576,8]{1,0:T(8,128)(2,1)} %copy-done.14) | copy-start | bytes 27652
  428.1 10.2 %copy-start.20 = (bf16[768,8]{0,1:T(8,128)(2,1)S(1)}, bf16[768,8]{0,1:T(8,128)(2,1)}, u32[]{:S(2)}) copy-start(bf16[768,8]{0,1:T(8,128)(2,1)} %param.36) | copy-start | bytes 36868
  428.1 10.2 %copy-start.22 = (f32[768]{0:T(1024)S(1)}, f32[768]{0:T(1024)}, u32[]{:S(2)}) copy-start(f32[768]{0:T(1024)} %param.34) | copy-start | bytes 9220
  450.2 163.7 %reduce-scatter.8.cloned.1.call-start = ((), (), s32[]{:S(2)}) async-start(), calls=%async_computation.10 | async-start | bytes 3981312 | tf_op jit(solution)/shard_map/reduce_scatter | solution.py:364
  450.4 9.9 %copy-start.4 = (bf16[576,2304]{0,1:T(8,128)(2,1)S(1)}, bf16[576,2304]{0,1:T(8,128)(2,1)}, u32[]{:S(2)}) copy-start(bf16[576,2304]{0,1:T(8,128)(2,1)} %copy.90) | copy-start | bytes 7962628
  450.5 9.9 %copy-start.21 = (f32[12,576]{1,0:T(8,128)S(1)}, f32[12,576]{1,0:T(8,128)}, u32[]{:S(2)}) copy-start(f32[12,576]{1,0:T(8,128)} %sub.56) | copy-start | bytes 82948
  450.5 9.9 %copy-start.38 = (pred[576]{0:T(1024)(128)(4,1)S(1)}, pred[576]{0:T(1024)(128)(4,1)}, u32[]{:S(2)}) copy-start(pred[576]{0:T(1024)(128)(4,1)} %broadcast_compare_fusion) | copy-start | bytes 1732
  502.4 2.3 copy-start.40
  509.3 137.6 %reduce-scatter.12.cloned.1.call-start = ((), (), s32[]{:S(2)}) async-start(), calls=%async_computation.12 | async-start | bytes 5898240 | tf_op jit(solution)/shard_map/reduce_scatter | solution.py:323
  522.0 2.5 copy-start.42
  522.0 4.4 copy-start.3
  522.0 4.7 copy-start.31
  522.0 9.6 %copy-start.23 = (f32[768]{0:T(1024)S(1)}, f32[768]{0:T(1024)}, u32[]{:S(2)}) copy-start(f32[768]{0:T(1024)} %param.28) | copy-start | bytes 9220
  522.0 160.9 %all-reduce.13.cloned.1.call-start = ((), (), s32[]{:S(2)}) async-start(), calls=%async_computation.15 | async-start | bytes 1179648 | tf_op jit(solution)/shard_map/psum | solution.py:365
  537.9 70.0 %copy-start.6 = (bf16[576,768]{1,0:T(8,128)(2,1)S(1)}, bf16[576,768]{1,0:T(8,128)(2,1)}, u32[]{:S(2)}) copy-start(bf16[576,768]{1,0:T(8,128)(2,1)} %cot_ref.1) | copy-start | bytes 2654212
  (8 other events, 9.6 us)
Sparse Core Ops, SparseCore 0:
  300.7 96.7 reduce-scatter.15
  400.0 45.9 reduce-scatter.13
  450.3 64.0 reduce-scatter.9
  518.4 78.5 reduce-scatter.7
  599.5 47.3 reduce-scatter.11
  649.3 33.6 all-reduce.12

commit v2 on v1

--- a/solution.py
+++ b/solution.py
@@ -254,6 +254,209 @@
     )(*operands)
 
 
+def gelu_parts(values):
+    bell = jnp.exp2(values * values * (-0.5 * LOG2E))
+    t = 1.0 / (1.0 + (0.3275911 * 0.5**0.5) * jnp.abs(values))
+    tail = t * (0.1274147959 + t * (-0.142248368 + t * (0.7107068705 + t * (-0.7265760135 + t * 0.5307027145))))
+    tail = tail * bell
+    share = jnp.where(values >= 0, 1.0 - tail, tail)
+    return values * share, share + values * bell * 0.3989422804014327
+
+
+def to_column(row):
+    n = row.shape[1]
+    return jnp.sum(jnp.where(iota((n, n), 0) == iota((n, n), 1), row, 0.0), axis=1, keepdims=True)
+
+
+def to_row(column):
+    n = column.shape[0]
+    return jnp.sum(jnp.where(iota((n, n), 0) == iota((n, n), 1), column, 0.0), axis=0, keepdims=True)
+
+
+def expert_kernel(
+    copies, experts, most, chunks, tile,
+    x_ref, gates_ref, cot_ref, in_w_ref, in_bias_ref, out_w_ref, out_bias_ref,
+    d_rows_ref, d_gates_ref, produced_ref, grads_ref,
+    recv_x, recv_g, send_d, send_g, hidden, d_pre, x_t, d_t, bias_sum, total_p, total_d, stage,
+    x_ss, x_rs, g_ss, g_rs, d_ss, d_rs, dg_ss, dg_rs, own_sem, own_d_sem, stage_sem,
+):
+    me_dp = lax.axis_index("dp")
+    me = lax.axis_index("expert")
+    width, hidden_width = in_w_ref.shape
+    rows = chunks * most
+    block = hidden_width // copies
+
+    def chunk(o):
+        return pl.ds(pl.multiple_of(o * most, most), most)
+
+    def move_x(o):
+        return pltpu.make_async_remote_copy(
+            x_ref.at[chunk(o)], recv_x.at[chunk(o)], x_ss.at[o], x_rs.at[o], (me_dp, me ^ o), MESH
+        )
+
+    def move_g(o):
+        return pltpu.make_async_remote_copy(
+            gates_ref.at[o], recv_g.at[o], g_ss.at[o], g_rs.at[o], (me_dp, me ^ o), MESH
+        )
+
+    def move_d(o):
+        return pltpu.make_async_remote_copy(
+            send_d.at[chunk(o)], d_rows_ref.at[chunk(o)], d_ss.at[o], d_rs.at[o], (me_dp, me ^ o), MESH
+        )
+
+    def move_dg(o):
+        return pltpu.make_async_remote_copy(
+            send_g.at[o], d_gates_ref.at[o], dg_ss.at[o], dg_rs.at[o], (me_dp, me ^ o), MESH
+        )
+
+    own = pltpu.make_async_copy(x_ref.at[chunk(0)], recv_x.at[chunk(0)], own_sem)
+    own.start()
+    greet([(me_dp, me ^ o) for o in range(1, experts)])
+    for o in range(1, experts):
+        move_g(o).start()
+        move_x(o).start()
+    recv_g[0] = gates_ref[0]
+    bias_sum[...] = jnp.zeros_like(bias_sum)
+    x_t[width:, :] = jnp.ones_like(x_t[width:, :])
+    own.wait()
+    own_d = pltpu.make_async_copy(send_d.at[chunk(0)], d_rows_ref.at[chunk(0)], own_d_sem)
+
+    def work(g, _):
+        for j in range(chunks):
+            o = g * chunks + j
+
+            @pl.when(o > 0)
+            def _():
+                move_g(o).wait_recv()
+                move_x(o).wait_recv()
+
+        at = pl.multiple_of(g * rows, rows)
+        here = pl.ds(at, rows)
+        gate = jnp.concatenate([to_column(recv_g[g * chunks + j][0:1, :]) for j in range(chunks)], axis=0)
+        x = recv_x[here, :]
+        cot = cot_ref[here, :].astype(f32)
+        d_produced = (cot * gate).astype(bf16)
+        bias_sum[0:1, :] += jnp.sum(d_produced.astype(f32), axis=0, keepdims=True)
+        x_t[:width, here] = x.T
+        d_t[:, here] = d_produced.T
+        total_p[...] = jnp.zeros_like(total_p)
+        total_d[...] = jnp.zeros_like(total_d)
+
+        def step(n, _):
+            cols = pl.ds(pl.multiple_of(n * tile, tile), tile)
+            pre = dot(x, in_w_ref[:, cols]) + in_bias_ref[:, cols]
+            value, slope = gelu_parts(pre)
+            value = value.astype(bf16)
+            hidden[here, cols] = value
+            total_p[...] += dot(value, out_w_ref[cols, :])
+            d_value = (dot(d_produced, out_w_ref[cols, :], NT) * slope).astype(bf16)
+            d_pre[here, cols] = d_value
+            total_d[...] += dot(d_value, in_w_ref[:, cols], NT)
+            return 0
+
+        lax.fori_loop(0, hidden_width // tile, step, 0)
+        send_d[here, :] = total_d[...].astype(bf16)
+        produced = (total_p[...] + out_bias_ref[...]).astype(bf16)
+        produced_ref[here, :] = produced
+        d_gate = jnp.sum(produced.astype(f32) * cot, axis=1, keepdims=True)
+        for j in range(chunks):
+            o = g * chunks + j
+            d_gate_row = jnp.broadcast_to(to_row(d_gate[j * most : (j + 1) * most, :]), (8, most))
+            send_g[o] = d_gate_row
+
+            @pl.when(o > 0)
+            def _():
+                move_d(o).start()
+                move_dg(o).start()
+
+            @pl.when(o == 0)
+            def _():
+                own_d.start()
+                d_gates_ref[0] = d_gate_row
+
+        return 0
+
+    lax.fori_loop(0, experts // chunks, work, 0)
+
+    def store(w, p):
+        return pltpu.make_async_copy(stage.at[w], grads_ref.at[w, p], stage_sem.at[w])
+
+    def weigh(p, _):
+        cols = pl.ds(pl.multiple_of((me_dp ^ p) * block, block), block)
+
+        @pl.when(p > 0)
+        def _():
+            store(0, p - 1).wait()
+
+        total = dot(x_t[...], d_pre[:, cols])
+        stage[0, :width, :] = total[:width, :].astype(bf16)
+        tail = total[width:, :]
+        lines = iota((16, block), 0)
+        for i in range(-(-width // block)):
+            tail = jnp.where(lines == 8 + i, bias_sum[0:1, i * block : (i + 1) * block], tail)
+        stage[0, width:, :] = tail.astype(bf16)
+        store(0, p).start()
+
+        @pl.when(p > 0)
+        def _():
+            store(1, p - 1).wait()
+
+        stage[1, :width, :] = dot(d_t[...], hidden[:, cols]).astype(bf16)
+        stage[1, width:, :] = jnp.zeros((16, block), bf16)
+        store(1, p).start()
+        return 0
+
+    lax.fori_loop(0, copies, weigh, 0)
+    store(0, copies - 1).wait()
+    store(1, copies - 1).wait()
+    own_d.wait()
+    for o in range(1, experts):
+        move_g(o).wait_send()
+        move_x(o).wait_send()
+        move_d(o).wait()
+        move_dg(o).wait()
+
+
+def run_experts(copies, experts, most, *operands):
+    slots, width = operands[0].shape
+    hidden_width = operands[3].shape[1]
+    chunks = max(1, min(experts, 384 // most))
+    rows = chunks * most
+    block = hidden_width // copies
+    shape = jax.ShapeDtypeStruct
+    return pl.pallas_call(
+        partial(expert_kernel, copies, experts, most, chunks, 512),
+        out_shape=(
+            shape((slots, width), bf16),
+            shape((experts, 8, most), f32),
+            shape((slots, width), bf16),
+            shape((2, copies, width + 16, block), bf16),
+        ),
+        in_specs=[HBM] + [VMEM] * 6,
+        out_specs=(HBM, VMEM, VMEM, HBM),
+        scratch_shapes=[
+            pltpu.VMEM((slots, width), bf16),
+            pltpu.VMEM((experts, 8, most), f32),
+            pltpu.VMEM((slots, width), bf16),
+            pltpu.VMEM((experts, 8, most), f32),
+            pltpu.VMEM((slots, hidden_width), bf16),
+            pltpu.VMEM((slots, hidden_width), bf16),
+            pltpu.VMEM((width + 16, slots), bf16),
+            pltpu.VMEM((width, slots), bf16),
+            pltpu.VMEM((8, width), f32),
+            pltpu.VMEM((rows, width), f32),
+            pltpu.VMEM((rows, width), f32),
+            pltpu.VMEM((2, width + 16, block), bf16),
+        ]
+        + [DMA((experts,))] * 8
+        + [DMA(()), DMA(()), DMA((2,))],
+        compiler_params=pltpu.CompilerParams(
+            collective_id=1, has_side_effects=True, vmem_limit_bytes=VMEM_BYTES
+        ),
+        name="experts",
+    )(*operands)
+
+
 def exact_gelu(values):
     return jax.nn.gelu(values, approximate=False)
 
@@ -304,28 +507,23 @@
         out = lax.all_to_all(block, "expert", split_axis=0, concat_axis=0, tiled=True)
         return jnp.take(out, order, axis=0)
 
-    received = exchange(x_slots).reshape(-1, width)
-    gates = exchange(gate_slots[:, :1, :].reshape(experts, most, 1)).reshape(-1, 1)
-    w1, w2 = expert_in[0], expert_out[0]
-    hidden_pre = jnp.dot(received, w1, preferred_element_type=f32) + expert_in_bias
-    hidden = exact_gelu(hidden_pre).astype(bf16)
-    produced = (jnp.dot(hidden, w2, preferred_element_type=f32) + expert_out_bias).astype(bf16)
-    d_gate_slots = jnp.sum(produced.astype(f32) * recv_cot.astype(f32), axis=-1, keepdims=True)
-    d_produced = (gates * recv_cot.astype(f32)).astype(bf16)
-    d_hidden = lax.dot_general(d_produced, w2, NT, preferred_element_type=f32)
-    gelu_value, gelu_pull = jax.vjp(exact_gelu, hidden_pre)
-    d_pre = gelu_pull(d_hidden)[0].astype(jnp.bfloat16)
-    d_rows = lax.dot_general(d_pre, w1, NT, preferred_element_type=f32).astype(bf16)
-    g1 = lax.dot_general(received, d_pre, TN, preferred_element_type=f32)
-    gb1 = jnp.sum(d_pre.astype(f32), axis=0)
-    g2 = lax.dot_general(hidden, d_produced, TN, preferred_element_type=f32)
-    gb2 = jnp.sum(d_produced.astype(f32), axis=0)
-    scatter = lambda v, d: lax.psum_scatter(v.astype(bf16), "dp", scatter_dimension=d, tiled=True).astype(f32)[None]
-    grad_expert_in, grad_expert_in_bias = scatter(g1, 1), scatter(gb1, 0)
-    grad_expert_out, grad_expert_out_bias = scatter(g2, 0), scatter(gb2, 0)
+    ret_rows, ret_gate, produced, grads = run_experts(
+        copies, experts, most,
+        x_slots, gate_slots, recv_cot, expert_in[0], expert_in_bias, expert_out[0], expert_out_bias,
+    )
+    me_dp = lax.axis_index("dp")
+    grads = jnp.take(grads, jnp.arange(copies) ^ me_dp, axis=1)
+    block = grads.shape[-1]
+    g1 = grads[0].transpose(1, 0, 2).reshape(width + 16, -1)
+    g2 = grads[1].transpose(1, 0, 2).reshape(width + 16, -1)
+    g1 = lax.psum_scatter(g1, "dp", scatter_dimension=1, tiled=True).astype(f32)
+    g2 = lax.psum_scatter(g2, "dp", scatter_dimension=1, tiled=True).astype(f32)
+    grad_expert_in, grad_expert_in_bias = g1[:width][None], g1[width][None]
+    grad_expert_out = g2[:width].T[None]
+    gb2 = g1[width + 8 :].reshape(-1)[:width]
+    grad_expert_out_bias = lax.dynamic_slice(gb2, (me_dp * (width // copies),), (width // copies,))[None]
     ret_produced = exchange(produced).reshape(-1, width)
-    ret_rows = exchange(d_rows).reshape(-1, width)
-    ret_gate = exchange(d_gate_slots).reshape(-1, 1)
+    ret_gate = ret_gate[:, 0].reshape(-1, 1)
     slot = pairs[:, :2].astype(i32)
     gk, kept, both = pairs[:, 2:4], pairs[:, 4:6], pairs[:, 6:7]
     chosen = jnp.take(ret_produced, slot.reshape(-1), axis=0).reshape(row_count, 2, width).astype(f32)

time: 700 us -> 605 us (0.86)
  matrix products: 179 us -> 57.9 us
  Pallas kernels: 57.1 us -> 174 us
  waiting for transfers between devices: 184 us -> 111 us
  local copies, waits for them, and re-layouts: 94 us -> 111 us
  starting transfers between devices: 31.7 us -> 15.9 us
  other arithmetic: 82 us -> 71 us
    dot_general x6 -> x0, matrix products: 120 us -> none  [the longest x1 49.6 us: local(): jnp.dot(received, w1, preferred_element_type=f32) + expert_in_bias]
    pallas_call x0 -> x1, Pallas kernels: none -> 117 us  [run_experts(): pl.pallas_call(partial(expert_kernel, copies, experts, most, chunks, 512)...]
    all_to_all x5 -> x1, waiting for transfers between devices: 118 us -> 38.8 us  [exchange(): lax.all_to_all(block, 'expert', split_axis=0, concat_axis=0, tiled=True)]
    reduce_scatter x2, waiting for transfers between devices: 0.01 us -> 37.8 us  [local(): lax.psum_scatter(g.astype(bf16), 'expert', scatter_dimension=0, tiled=True)]
    reduce_scatter x2, waiting for transfers between devices: 33 us -> 0.01 us  [the longest x1 0.01 us: local(): g2 = lax.psum_scatter(g2, 'dp', scatter_dimension=1, tiled=True).astype(f32)]
    gather x0 -> x4, local copies, waits for them, and re-layouts: none -> 16.9 us  [local(): grads = jnp.take(grads, jnp.arange(copies) ^ me_dp, axis=1)]
    all_to_all x5 -> x1, starting transfers between devices: 31.3 us -> 15.1 us  [exchange(): lax.all_to_all(block, 'expert', split_axis=0, concat_axis=0, tiled=True)]
    select_n x0 -> x2, other arithmetic: none -> 8.6 us  [local(): grads = jnp.take(grads, jnp.arange(copies) ^ me_dp, axis=1)]
  transfers between devices with their start and end apart: 11 -> 7, of which waited for: 7 -> 3; matrix products, arithmetic and copies ran while one was open for 32% -> 34% of each run, Pallas kernels for 0% -> 0%
where the time goes in v2:
time: 605 us; the launch traced here: 599 us
  Pallas kernels  174 us (29%)
  local copies, waits for them, and re-layouts  111 us (18%)
  waiting for transfers between devices  111 us (18%)
  other arithmetic  71 us (12%)
  matrix products  57.9 us (10%)
  blocking collectives  42.7 us (7%)
  between operations  16.1 us (3%)
  starting transfers between devices  15.9 us (3%)
    pallas_call x1, Pallas kernels, run_experts(): pl.pallas_call(partial(expert_kernel, copies, experts, most, chunks, 512)...  117 us
    pallas_call x1, Pallas kernels, run_front(): pl.pallas_call(partial(front_kernel, copies, experts, most, capacity), ou...  57.1 us
    all_to_all x1, waiting for transfers between devices, exchange(): lax.all_to_all(block, 'expert', split_axis=0, concat_axis=0, tiled=True)  38.8 us
    reduce_scatter x2, waiting for transfers between devices, local(): lax.psum_scatter(g.astype(bf16), 'expert', scatter_dimension=0, tiled=True)  37.8 us
    unnamed x1, blocking collectives  35.8 us
    psum x1, waiting for transfers between devices, local(): dense = [lax.psum(g, 'dp').astype(f32) for g in dense]  33.9 us
    unnamed x64, local copies, waits for them, and re-layouts  25.5 us
    gather x4, local copies, waits for them, and re-layouts, local(): grads = jnp.take(grads, jnp.arange(copies) ^ me_dp, axis=1)  16.9 us
  transfers between devices with their start and end apart: 7, of which 3 were waited for; matrix products, arithmetic and copies ran while one was open for 34% of the time, Pallas kernels for 0%

profile of v2, /device:TPU:0, one launch (start us, length us, event | category | flops | bytes accessed | tf_op | source)
XLA Modules:
  0.0 599.1 jit_solution(11987009757945662995)
XLA Ops:
  22.3 57.1 %front.1 = (bf16[1536,768]{1,0:T(8,128)(2,1)}, bf16[1536,768]{1,0:T(8,128)(2,1)}, f32[8,8,192]{2,1,0:T(8,128)}, bf16[576,2304]{1,0:T(8,128)(2,1)}, bf16[768,576]...) custom-call(bf16[576,768]{1,0:T(8,128)(2,1)} %patches_ref.1, ...), custom_call_target="tpu_custom_call" | custom-call | tf_op jit(solution)/shard_map/front/pallas_call | solution.py:225
  83.3 116.9 %experts.1 = (bf16[1536,768]{1,0:T(8,128)(2,1)}, f32[8,8,192]{2,1,0:T(8,128)}, bf16[1536,768]{1,0:T(8,128)(2,1)}, bf16[2,4,784,768]{3,2,1,0:T(8,128)(2,1)}) custom-call(bf16[1536,768]{1,0:T(8,128)(2,1)} %get-tuple-element.34.x_ref, f32[8,8,192]{2,1,0:T(8,128)} %get-tuple-element.35.gates_ref, bf16[1536,768]{1,0:T(8,128)(2,1)} %get-tuple-element.36.cot_ref, ...), custom_call_target="tpu_custom_call" | custom-call | tf_op jit(solution)/shard_map/experts/pallas_call | solution.py:427
  201.1 6.5 %gather_fusion = f32[1152]{0:T(1024)S(1)} fusion(f32[1536]{0:T(1024)S(1)} %squeeze_reshape_squeeze.3, s32[2048]{0:T(1024)S(1)} %pad_clamp_fusion), kind=kCustom, calls=%fused_computation.4 | custom fusion | bytes 13824 | tf_op jit(solution)/shard_map/jit(_take)/gather | solution.py:531
  211.9 2.2 mini-gather-slice.1
  214.0 5.8 mini-gather-slice
  219.9 6.4 %gather_fusion.1 = bf16[4,2,512,768]{3,2,1,0:T(8,128)(2,1)} fusion(bf16[2,4,512,768]{3,2,1,0:T(8,128)(2,1)} %mini-gather-slice, s32[1024]{0:T(1024)S(1)} %pad_clamp_fusion.2), kind=kCustom, calls=%fused_computation.5 | custom fusion | bytes 12582928 | tf_op jit(solution)/shard_map/jit(_take)/gather | solution.py:515
  226.3 2.5 gather_fusion.2
  228.7 8.6 %maximum_select_fusion = bf16[2,4,784,768]{3,2,0,1:T(8,128)(2,1)} fusion(bf16[2,4,272,768]{3,2,0,1:T(8,128)(2,1)} %bitcast.86, bf16[2,4,512,768]{3,2,0,1:T(8,128)(2,1)} %bitcast.79, pred[4]{0:T(512)(128)(4,1)S(1)} %compare_and_fusion.2), kind=kLoop, calls=%fused_computation.10 | loop fusion | flops 24084480 | bytes 19267588 | tf_op jit(solution)/shard_map/jit(_take)/select_n | solution.py:515
  237.3 6.8 %slice_bitcast_fusion = (bf16[4,98,8,768]{3,2,1,0:T(8,128)(2,1)S(1)}, bf16[4,98,8,768]{3,2,1,0:T(8,128)(2,1)}) fusion(bf16[2,4,784,768]{3,2,0,1:T(8,128)(2,1)} %maximum_select_fusion), kind=kLoop, calls=%fused_computation.15 | loop fusion | bytes 19267584
  244.1 2.8 copy.107
  247.0 5.2 copy.106
  252.3 2.4 gather_fusion.3
  254.7 1.7 broadcast_select_fusion
  256.4 15.1 %all-to-all-start = ((bf16[8,192,768]{2,1,0:T(8,128)(2,1)}), bf16[8,192,768]{2,1,0:T(8,128)(2,1)}, u32[]{:S(2)}, u32[]{:S(2)}) async-start(bf16[8,192,768]{2,1,0:T(8,128)(2,1)} %broadcast_select_fusion), calls=%async_computation | async-start | bytes 4718592 | tf_op jit(solution)/shard_map/all_to_all | solution.py:507
  273.2 4.9 copy.93
  278.1 1.7 reduce_sum.198
  279.8 4.8 gather_fusion.6
  284.6 1.8 multiply_reduce_fusion.5
  286.5 38.8 %all-to-all-done = bf16[8,192,768]{2,1,0:T(8,128)(2,1)} async-done(((bf16[8,192,768]{2,1,0:T(8,128)(2,1)}), bf16[8,192,768]{2,1,0:T(8,128)(2,1)}, u32[]{:S(2)}, u32[]{:S(2)}) %all-to-all-start) | async-done | bytes 2359328 | tf_op jit(solution)/shard_map/all_to_all | solution.py:507
  325.2 3.8 gather_fusion.4
  329.0 2.0 broadcast_select_fusion.1
  331.0 4.8 gather_fusion.5
  335.8 5.4 select_convert_fusion
  341.2 4.0 reshape.220
  345.2 5.4 reshape.219
  350.6 10.2 %multiply_reduce_fusion.1 = (f32[576,768]{1,0:T(8,128)S(1)}, f32[576,768]{1,0:T(8,128)S(1)}) fusion(f32[576,2,768]{2,1,0:T(2,128)S(1)} %reshape.220, f32[576,2]{1,0:T(8,128)} %get-tuple-element.142, f32[576,2,768]{2,1,0:T(2,128)} %reshape.219, f32[576,2]{1,0:T(8,128)} %get-tuple-element.143), kind=kLoop, calls=%fused_computation.17 | loop fusion | flops 2654208 | bytes 10626048 | tf_op jit(solution)/shard_map/reduce_sum | solution.py:540
  362.3 1.7 fusion.24
  365.9 1.8 convolution_convert_fusion.2
  367.7 1.5 copy.94
  369.2 3.6 convolution_convert_fusion.1
  373.3 10.1 %fusion.14 = f32[12,576,576]{1,2,0:T(8,128)} fusion(bf16[576,12,64]{0,2,1:T(8,128)(2,1)S(1)} %bitcast.87, bf16[576,3,12,64]{0,3,2,1:T(8,128)(2,1)} %bitcast.82), kind=kOutput, calls=%fused_computation.52 | convolution fusion | flops 509607936 | bytes 17793024 | tf_op jit(solution)/shard_map/qhd,khd->hqk/dot_general | solution.py:475
  383.4 16.8 %multiply_reduce_fusion = (f32[12,576]{1,0:T(8,128)S(1)}, f32[12,576,576]{1,2,0:T(8,128)}) fusion(f32[12,576,576]{1,2,0:T(8,128)} %fusion.14, f32[12,576]{1,0:T(8,128)S(1)} %copy-done.19, bf16[576,3,12,64]{0,3,2,1:T(8,128)(2,1)S(1)} %bitcast.83, pred[576]{0:T(1024)(128)(4,1)S(1)} %broadcast_compare_fusion), kind=kOutput, calls=%fused_computation.8 | convolution fusion | flops 537470208 | bytes 33886208 | tf_op jit(solution)/shard_map/qhd,khd->hqk/dot_general | solution.py:470
  400.2 12.0 %multiply_convert_fusion = bf16[12,576,576]{1,2,0:T(8,128)(2,1)S(1)} fusion(f32[12,576,576]{1,2,0:T(8,128)} %get-tuple-element.154, f32[12,576,576]{1,2,0:T(8,128)} %fusion.14, f32[12,576]{1,0:T(8,128)S(1)} %get-tuple-element.153), kind=kLoop, calls=%fused_computation.7 | loop fusion | flops 11943936 | bytes 39840768 | tf_op jit(solution)/shard_map/convert_element_type | solution.py:477
  412.2 2.7 multiply_bitcast_fusion
  414.9 1.7 multiply_bitcast_fusion.1
  416.6 8.8 %fusion.10 = bf16[576,1,12,64]{0,3,2,1:T(8,128)(2,1)S(1)} fusion(bf16[576,12,64]{0,2,1:T(8,128)(2,1)S(1)} %bitcast.88, f32[12,576,576]{1,2,0:T(8,128)} %get-tuple-element.154), kind=kOutput, calls=%fused_computation.45 | convolution fusion | flops 513589248 | bytes 17694720 | tf_op jit(solution)/shard_map/hqk,qhd->khd/dot_general | solution.py:474
  426.1 1.6 copy-done.8
  427.7 4.5 convolution_convert_fusion
  437.1 6.3 %fusion.20 = (bf16[768]{0:T(1024)(128)(2,1)}, f32[576]{0:T(1024)S(1)}, f32[576]{0:T(1024)S(1)}, f32[576,768]{1,0:T(8,128)S(1)}) fusion(f32[768]{0:T(1024)S(1)} %copy-done.21, f32[576]{0:T(1024)S(1)} %broadcast_multiply_fusion, bf16[576,768]{1,0:T(8,128)(2,1)S(1)} %copy-done.3, bf16[576,2304]{0,1:T(8,128)(2,1)} %bitcast.92, bf16[768,2304]{1,0:T(8,128)(2,1)} %qkv_w_ref.1), kind=kOutput, calls=%fused_computation.100 | convolution fusion | flops 2041968896 | bytes 8858880 | tf_op jit(solution)/shard_map/dot_general | solution.py:556
  446.1 35.8 %all-reduce.6 = (bf16[768]{0:T(1024)(128)(2,1)}, bf16[768]{0:T(1024)(128)(2,1)}, bf16[1536]{0:T(1024)(128)(2,1)}, bf16[768]{0:T(1024)(128)(2,1)}, bf16[768]{0:T(1024)(128)(2,1)}, /*index=5*/bf16[768]{0:T(1024)(128)(2,1)}) all-reduce(bf16[768]{0:T(1024)(128)(2,1)} %get-tuple-element.109, ...), channel_id=2, replica_groups=mesh['dp'=4,'expert'=8] {'expert'}, use_global_device_ids=true, to_apply=%region_16.19.clone | all-reduce | flops 5376 | bytes 21504
  489.6 6.9 %all-reduce.7 = (bf16[96]{0:T(256)(128)(2,1)}, bf16[96]{0:T(256)(128)(2,1)}, bf16[192]{0:T(256)(128)(2,1)}, bf16[96]{0:T(256)(128)(2,1)}, bf16[96]{0:T(256)(128)...) all-reduce(bf16[96]{0:T(256)(128)(2,1)} %dynamic-slice.2, ...), channel_id=1, replica_groups=mesh['dp'=4,'expert'=8] {'dp'}, use_global_device_ids=true, to_apply=%region_17.20 | all-reduce | flops 1440 | bytes 5760 | tf_op jit(solution)/shard_map/psum | solution.py:563
  505.4 2.9 add_convert_fusion
  509.8 2.0 copy.100
  515.2 37.8 %reduce-scatter.8.cloned.1.call-done = bf16[96,2304]{1,0:T(8,128)(2,1)} async-done(((bf16[768,2304]{1,0:T(8,128)(2,1)}), bf16[96,2304]{1,0:T(8,128)(2,1)}) %reduce-scatter.8.cloned.1.call-update) | async-done | bytes 442384 | tf_op jit(solution)/shard_map/reduce_scatter | solution.py:562
  553.0 1.6 slice_bitcast_fusion.2
  554.5 33.9 %all-reduce.11.cloned.1.call-done = (bf16[96,2304]{1,0:T(8,128)(2,1)}, bf16[96,768]{1,0:T(8,128)(2,1)}) async-done(((bf16[96,2304]{1,0:T(8,128)(2,1)}, bf16[96,768]{1,0:T(8,128)(2,1)}), (bf16[96,2304]{1,0:T(8,128)(2,1)}, bf16[96,768]{1,0:T(8,128)(2,1)})) %all-reduce.11.cloned.1.call-update) | async-done | bytes 589840 | tf_op jit(solution)/shard_map/psum | solution.py:563
  588.5 1.6 convert_element_type.133
  590.1 2.0 convert_element_type.129
  (156 shorter events, 58.2 us)
Async XLA Ops:
  7.2 427.8 %reduce-scatter.16.cloned.1.call-start = ((), (), s32[]{:S(2)}) async-start(), calls=%async_computation.10 | async-start | bytes 221184
  22.2 60.5 %copy-start.17 = (s32[576,2]{0,1:T(2,128)S(1)}, s32[576,2]{0,1:T(2,128)}, u32[]{:S(2)}) copy-start(s32[576,2]{0,1:T(2,128)} %param.24) | copy-start | bytes 13828
  81.6 118.6 %copy-start.9 = (s32[576,2]{1,0:T(8,128)}, s32[576,2]{1,0:T(8,128)S(1)}, u32[]{:S(2)}) copy-start(s32[576,2]{1,0:T(8,128)S(1)} %slice_convert_fusion) | copy-start | bytes 13828
  201.1 6.7 %copy-start.2 = (f32[576,8]{1,0:T(8,128)S(1)}, f32[576,8]{1,0:T(8,128)}, u32[]{:S(2)}) copy-start(f32[576,8]{1,0:T(8,128)} %get-tuple-element.33) | copy-start | bytes 55300
  207.6 2.0 copy-start.11
  208.1 2.5 copy-start.15
  210.0 0.7 copy-start.12
  211.8 296.6 %reduce-scatter.14.cloned.1.call-start = ((), (), s32[]{:S(2)}) async-start(), calls=%async_computation.9 | async-start | bytes 6021120 | tf_op jit(solution)/shard_map/reduce_scatter | solution.py:520
  247.0 264.8 %reduce-scatter.12.cloned.1.call-start = ((), (), s32[]{:S(2)}) async-start(), calls=%async_computation.8 | async-start | bytes 6021120 | tf_op jit(solution)/shard_map/reduce_scatter | solution.py:519
  256.4 15.1 %copy-start.10 = (s32[576,2]{1,0:T(8,128)S(1)}, s32[576,2]{1,0:T(8,128)}, u32[]{:S(2)}) copy-start(s32[576,2]{1,0:T(8,128)} %copy-done.9) | copy-start | bytes 13828
  256.4 68.9 %all-to-all-start = ((bf16[8,192,768]{2,1,0:T(8,128)(2,1)}), bf16[8,192,768]{2,1,0:T(8,128)(2,1)}, u32[]{:S(2)}, u32[]{:S(2)}) async-start(bf16[8,192,768]{2,1,0:T(8,128)(2,1)} %broadcast_select_fusion), calls=%async_computation | async-start | bytes 4718592 | tf_op jit(solution)/shard_map/all_to_all | solution.py:507
  271.4 243.8 %reduce-scatter.10.cloned.1.call-start = ((), (), s32[]{:S(2)}) async-start(), calls=%async_computation.7 | async-start | bytes 1327104 | tf_op jit(solution)/shard_map/reduce_scatter | solution.py:562
  273.2 6.6 %copy-start = (bf16[1536,768]{1,0:T(8,128)(2,1)S(1)}, bf16[1536,768]{1,0:T(8,128)(2,1)}, u32[]{:S(2)}) copy-start(bf16[1536,768]{1,0:T(8,128)(2,1)} %get-tuple-element.38) | copy-start | bytes 7077892
  279.8 6.7 %copy-start.22 = (s32[576]{0:T(1024)S(1)}, s32[576]{0:T(1024)}, u32[]{:S(2)}) copy-start(s32[576]{0:T(1024)} %param.23) | copy-start | bytes 6916
  350.6 10.3 %copy-start.1 = (f32[576,768]{1,0:T(8,128)S(1)}, f32[576,768]{1,0:T(8,128)}, u32[]{:S(2)}) copy-start(f32[576,768]{1,0:T(8,128)} %get-tuple-element.32) | copy-start | bytes 5308420
  350.6 10.3 %copy-start.13 = (bf16[576,8]{1,0:T(8,128)(2,1)S(1)}, bf16[576,8]{1,0:T(8,128)(2,1)}, u32[]{:S(2)}) copy-start(bf16[576,8]{1,0:T(8,128)(2,1)} %copy-done.12) | copy-start | bytes 27652
  350.6 10.3 %copy-start.18 = (bf16[768,8]{0,1:T(8,128)(2,1)S(1)}, bf16[768,8]{0,1:T(8,128)(2,1)}, u32[]{:S(2)}) copy-start(bf16[768,8]{0,1:T(8,128)(2,1)} %param.34) | copy-start | bytes 36868
  350.6 10.3 %copy-start.20 = (f32[768]{0:T(1024)S(1)}, f32[768]{0:T(1024)}, u32[]{:S(2)}) copy-start(f32[768]{0:T(1024)} %param.32) | copy-start | bytes 9220
  362.3 1.7 copy-start.5
  364.1 1.8 copy-start.14
  364.1 0.9 copy-start.23
  365.0 0.9 copy-start.16
  372.8 180.1 %reduce-scatter.8.cloned.1.call-start = ((), (), s32[]{:S(2)}) async-start(), calls=%async_computation.6 | async-start | bytes 3981312 | tf_op jit(solution)/shard_map/reduce_scatter | solution.py:562
  373.3 10.2 %copy-start.4 = (bf16[576,2304]{0,1:T(8,128)(2,1)S(1)}, bf16[576,2304]{0,1:T(8,128)(2,1)}, u32[]{:S(2)}) copy-start(bf16[576,2304]{0,1:T(8,128)(2,1)} %copy.93) | copy-start | bytes 7962628
  373.3 10.1 %copy-start.19 = (f32[12,576]{1,0:T(8,128)S(1)}, f32[12,576]{1,0:T(8,128)}, u32[]{:S(2)}) copy-start(f32[12,576]{1,0:T(8,128)} %sub.56) | copy-start | bytes 82948
  425.4 2.3 copy-start.24
  426.1 1.6 copy-start.8
  432.2 0.7 copy-start.25
  432.2 2.5 copy-start.3
  432.2 4.9 copy-start.21
  432.2 156.2 %all-reduce.11.cloned.1.call-start = ((), (), s32[]{:S(2)}) async-start(), calls=%async_computation.11 | async-start | bytes 1179648 | tf_op jit(solution)/shard_map/psum | solution.py:563
  443.5 1.2 copy-start.7
  443.5 62.0 %copy-start.6 = (bf16[576,768]{1,0:T(8,128)(2,1)S(1)}, bf16[576,768]{1,0:T(8,128)(2,1)}, u32[]{:S(2)}) copy-start(bf16[576,768]{1,0:T(8,128)(2,1)} %cot_ref.1) | copy-start | bytes 2654212
Sparse Core Ops, SparseCore 0:
  211.9 76.0 reduce-scatter.15
  290.6 61.0 reduce-scatter.13
  354.4 48.4 reduce-scatter.11
  406.8 64.0 reduce-scatter.9
  474.3 78.5 reduce-scatter.7
  555.3 33.1 all-reduce.10

commit v3 on v2

--- a/solution.py
+++ b/solution.py
@@ -457,28 +457,390 @@
     )(*operands)
 
 
-def exact_gelu(values):
-    return jax.nn.gelu(values, approximate=False)
-
-
-def normalize(values, gain, shift):
-    return standardize(values)[0] * gain + shift
-
-
-def attend_backward(pieces):
-    queries, key_rows, value_rows, key_valid, lse2, d_attended = pieces
-    scores = jnp.einsum("qhd,khd->hqk", queries, key_rows, preferred_element_type=f32) * HEAD_DIM ** (-0.5)
-    scores = jnp.where(key_valid[None, None, :], scores, -1000000000.0)
-    probabilities = jnp.exp2(scores * LOG2E - lse2[:, :, None])
-    weights = probabilities.astype(jnp.bfloat16)
-    d_values = jnp.einsum("hqk,qhd->khd", weights, d_attended, preferred_element_type=jnp.float32)
-    d_weights = jnp.einsum("qhd,khd->hqk", d_attended, value_rows, preferred_element_type=jnp.float32)
-    centre = jnp.sum(probabilities * d_weights, axis=-1, keepdims=True)
-    d_scores = (probabilities * (d_weights - centre)).astype(jnp.bfloat16)
-    scaling = HEAD_DIM ** (-0.5)
-    d_queries = jnp.einsum("hqk,khd->qhd", d_scores, key_rows, preferred_element_type=jnp.float32) * scaling
-    d_keys = jnp.einsum("hqk,qhd->khd", d_scores, queries, preferred_element_type=jnp.float32) * scaling
-    return (d_queries, d_keys, d_values)
+def back_kernel(
+    copies, experts, most,
+    d_rows_ref, d_gates_ref, produced_ref, grads_ref, pairs_ref, probs_ref, cols_ref,
+    second_ref, residual_ref, patches_ref, cot_ref, qkv_ref, att_t_ref, lse_ref, first_ref,
+    gain1_ref, gain2_ref, qkv_w_ref, out_w_ref, router_ref,
+    output_ref, grad_patches_ref, dense_ref, small_ref, kept_grads_ref, far_grads_ref,
+    recv_p, own_grads, near_grads, d_qkv, d_att, d_att_t, d_residual_ref,
+    p_ss, p_rs, n_ss, n_rs, f_ss, f_rs, own_sem,
+):
+    me_dp = lax.axis_index("dp")
+    me = lax.axis_index("expert")
+    rows, width = patches_ref.shape
+    slots = experts * most
+    chips = copies // 2
+    greet(
+        [(me_dp, me ^ o) for o in range(1, experts)]
+        + [(me_dp ^ 1, me)]
+        + [(me_dp ^ (2 * q), me) for q in range(1, chips)]
+    )
+    near = [
+        send(grads_ref.at[w, 2 * q + 1], near_grads.at[w, q], n_ss.at[w, q], n_rs.at[w, q], (me_dp ^ 1, me))
+        for q in range(chips)
+        for w in range(2)
+    ]
+    own = [
+        pltpu.make_async_copy(grads_ref.at[w, 2 * q], own_grads.at[w, q], own_sem.at[w, q])
+        for q in range(chips)
+        for w in range(2)
+    ]
+    for copy in own:
+        copy.start()
+    returns = []
+    for o in range(1, experts):
+        part = pl.ds(o * most, most)
+        returns.append(
+            send(produced_ref.at[part], recv_p.at[part], p_ss.at[o], p_rs.at[o], (me_dp, me ^ o))
+        )
+    own_p = pltpu.make_async_copy(
+        produced_ref.at[pl.ds(0, most)], recv_p.at[pl.ds(0, most)], p_rs.at[0]
+    )
+    own_p.start()
+    slot0, slot1 = pairs_ref[:, 0:1].astype(i32), pairs_ref[:, 1:2].astype(i32)
+    gate0, gate1 = pairs_ref[:, 2:3], pairs_ref[:, 3:4]
+    kept0, kept1, both = pairs_ref[:, 4:5], pairs_ref[:, 5:6], pairs_ref[:, 6:7]
+    places = iota((rows, slots), 1)
+    d_second = dot(ones_where((places == slot0) | (places == slot1)), d_rows_ref[...])
+    d_gate0 = jnp.zeros((rows, 1), f32)
+    d_gate1 = jnp.zeros((rows, 1), f32)
+    for o in range(experts):
+        part = iota((rows, most), 1) + o * most
+        line = d_gates_ref[o][0:1, :]
+        d_gate0 += jnp.sum(jnp.where(part == slot0, line, 0.0), axis=1, keepdims=True)
+        d_gate1 += jnp.sum(jnp.where(part == slot1, line, 0.0), axis=1, keepdims=True)
+    d_gate0, d_gate1 = d_gate0 * kept0, d_gate1 * kept1
+    probs = probs_ref[...]
+    names = iota((rows, experts), 1)
+    is0, is1 = names == cols_ref[:, 1:2], names == cols_ref[:, 2:3]
+    share0 = jnp.sum(jnp.where(is0, probs, 0.0), axis=1, keepdims=True) / both
+    share1 = jnp.sum(jnp.where(is1, probs, 0.0), axis=1, keepdims=True) / both
+    centre = d_gate0 * share0 + d_gate1 * share1
+    d_probs = jnp.where(is0, (d_gate0 - centre) / both, 0.0) + jnp.where(is1, (d_gate1 - centre) / both, 0.0)
+    d_logits = (probs * (d_probs - jnp.sum(probs * d_probs, axis=1, keepdims=True))).astype(bf16)
+    small_ref[8:, :] = jnp.zeros_like(small_ref[8:, :])
+    small_ref[8 : 8 + experts, :] = dot(d_logits, second_ref[...], TN)
+    d_second += dot(d_logits, router_ref[...], NT)
+    n, inverse = standardize(residual_ref[...])
+    small_ref[5:6, :] = jnp.sum(d_second * n, axis=0, keepdims=True)
+    small_ref[6:7, :] = jnp.sum(d_second, axis=0, keepdims=True)
+    m = d_second * gain2_ref[...]
+    d_residual = cot_ref[...].astype(f32) + inverse * (
+        m - jnp.mean(m, axis=-1, keepdims=True) - n * jnp.mean(m * n, axis=-1, keepdims=True)
+    )
+    d_residual_ref[...] = d_residual
+    d_branch = d_residual.astype(bf16)
+    small_ref[4:5, :] = jnp.sum(d_branch.astype(f32), axis=0, keepdims=True)
+    small_ref[7:8, :] = jnp.zeros((1, width), f32)
+    for copy in own:
+        copy.wait()
+    for copy in near:
+        copy.wait_recv()
+    far = []
+    for q in range(chips):
+        for w in range(2):
+            total = own_grads[w, q].astype(f32) + near_grads[w, q].astype(f32)
+            if q == 0:
+                kept_grads_ref[w] = total.astype(bf16)
+                continue
+            own_grads[w, q] = total.astype(bf16)
+            far.append(
+                send(
+                    own_grads.at[w, q], far_grads_ref.at[w, q - 1], f_ss.at[w, q], f_rs.at[w, q],
+                    (me_dp ^ (2 * q), me),
+                )
+            )
+    per = width // experts
+    group = experts // chips
+    half = width // 2
+
+    def keep(matrix, value):
+        for e in range(experts):
+            at = (e // 2) % chips * group + e // (2 * chips) * 2 + e % 2
+            for h in range(2):
+                dense_ref[matrix, h, at] = value[e * per : (e + 1) * per, h * half : (h + 1) * half].astype(bf16)
+
+    keep(3, dot(att_t_ref[...], d_branch))
+    d_att[...] = dot(d_branch, out_w_ref[...], NT).astype(bf16)
+    d_att_t[...] = dot(out_w_ref[...], d_branch, NT).astype(bf16)
+    key_bias = jnp.where(cols_ref[:, 3:4] > 0, 0.0, -1e30)
+    scale = LOG2E * HEAD_DIM ** (-0.5)
+    pair_width = 2 * HEAD_DIM
+
+    def attend(pair, _):
+        base = pl.multiple_of(pair * pair_width, pair_width)
+        here = pl.ds(base, pair_width)
+        q = qkv_ref[:, here]
+        k = qkv_ref[:, pl.ds(base + width, pair_width)]
+        v = qkv_ref[:, pl.ds(base + 2 * width, pair_width)]
+        k_t = k.T
+        d_out = d_att[:, here]
+        products = att_t_ref[here, :].astype(f32) * d_att_t[here, :].astype(f32)
+        lanes = iota((rows, pair_width), 1)
+        d_q, d_k, d_v = [], [], []
+        for a in range(2):
+            mine = (lanes >= HEAD_DIM) == (a == 1)
+            k_a = jnp.where(mine, k, jnp.zeros((), bf16))
+            v_a = jnp.where(mine, v, jnp.zeros((), bf16))
+            part = slice(a * HEAD_DIM, (a + 1) * HEAD_DIM)
+            delta = jnp.sum(products[part, :], axis=0, keepdims=True)
+            weights = jnp.exp2((dot(k_a, q, NT) + key_bias) * scale - lse_ref[pair][a : a + 1, :])
+            d_scores = (weights * (dot(v_a, d_out, NT) - delta)).astype(bf16)
+            d_v.append(dot(weights.astype(bf16), d_out))
+            d_k.append(dot(d_scores, q))
+            d_q.append(dot(k_t[part, :], d_scores))
+        low = lanes < HEAD_DIM
+        down = HEAD_DIM ** (-0.5)
+        d_qkv[:, here] = (jnp.concatenate(d_q, axis=0).T * down).astype(bf16)
+        d_qkv[:, pl.ds(base + width, pair_width)] = (jnp.where(low, d_k[0], d_k[1]) * down).astype(bf16)
+        d_qkv[:, pl.ds(base + 2 * width, pair_width)] = jnp.where(low, d_v[0], d_v[1]).astype(bf16)
+        return 0
+
+    lax.fori_loop(0, HEADS // 2, attend, 0)
+    first_t = first_ref[...].T
+    d_first = jnp.zeros((rows, width), f32)
+    ones = jnp.ones((8, rows), bf16)
+    for i in range(3):
+        part = slice(i * width, (i + 1) * width)
+        d_part = d_qkv[:, part]
+        keep(i, dot(first_t, d_part))
+        if i != 1:
+            small_ref[2 + i // 2 : 3 + i // 2, :] = dot(ones, d_part)[0:1, :]
+        d_first += dot(d_part, qkv_w_ref[:, part], NT)
+    n, inverse = standardize(patches_ref[...].astype(f32))
+    small_ref[0:1, :] = jnp.sum(d_first * n, axis=0, keepdims=True)
+    small_ref[1:2, :] = jnp.sum(d_first, axis=0, keepdims=True)
+    m = d_first * gain1_ref[...]
+    grad_patches_ref[...] = (
+        d_residual_ref[...]
+        + inverse * (m - jnp.mean(m, axis=-1, keepdims=True) - n * jnp.mean(m * n, axis=-1, keepdims=True))
+    ).astype(bf16)
+    own_p.wait()
+    for copy in returns:
+        copy.wait()
+    produced = recv_p[...]
+    output_ref[...] = (
+        residual_ref[...]
+        + gate0 * dot(ones_where(places == slot0), produced)
+        + gate1 * dot(ones_where(places == slot1), produced)
+    ).astype(bf16)
+    for copy in near:
+        copy.wait_send()
+    for copy in far:
+        copy.wait()
+
+
+def run_back(copies, experts, most, *operands):
+    rows, width = operands[9].shape
+    slots = experts * most
+    chips = copies // 2
+    block = operands[3].shape[-1]
+    shape = jax.ShapeDtypeStruct
+    smalls = -(-(8 + experts) // 16) * 16
+    return pl.pallas_call(
+        partial(back_kernel, copies, experts, most),
+        out_shape=(
+            shape((rows, width), bf16),
+            shape((rows, width), bf16),
+            shape((4, 2, experts, width // experts, width // 2), bf16),
+            shape((smalls, width), f32),
+            shape((2, width + 16, block), bf16),
+            shape((2, chips - 1, width + 16, block), bf16),
+        ),
+        in_specs=[VMEM] * 2 + [HBM] * 2 + [VMEM] * 16,
+        out_specs=(VMEM,) * 5 + (HBM,),
+        scratch_shapes=[
+            pltpu.VMEM((slots, width), bf16),
+            pltpu.VMEM((2, chips, width + 16, block), bf16),
+            pltpu.VMEM((2, chips, width + 16, block), bf16),
+            pltpu.VMEM((rows, 3 * width), bf16),
+            pltpu.VMEM((rows, width), bf16),
+            pltpu.VMEM((width, rows), bf16),
+            pltpu.VMEM((rows, width), f32),
+            DMA((experts,)), DMA((experts,)),
+            DMA((2, chips)), DMA((2, chips)),
+            DMA((2, chips)), DMA((2, chips)),
+            DMA((2, chips)),
+        ],
+        compiler_params=pltpu.CompilerParams(
+            collective_id=2, has_side_effects=True, vmem_limit_bytes=VMEM_BYTES
+        ),
+        name="back",
+    )(*operands)
+
+
+def reduce_kernel(
+    copies, experts,
+    dense_ref, small_ref, out_ref, small_out_ref,
+    near, summed, far, chip_sum, gathered, tiny,
+    a_ss, a_rs, b_ss, b_rs, c_ss, c_rs, d_ss, d_rs, e_ss, e_rs, t_ss, t_rs,
+):
+    me_dp = lax.axis_index("dp")
+    me = lax.axis_index("expert")
+    core, chip = me_dp % 2, me_dp // 2
+    chips = copies // 2
+    group = experts // chips
+    matrices = dense_ref.shape[0]
+    inside = (me // 2) % chips == chip
+    over_copies = [(me_dp ^ (1 << i), me) for i in range(copies.bit_length() - 1)]
+    over_experts = [(me_dp, me ^ (1 << i)) for i in range(experts.bit_length() - 1)]
+    steps = over_copies + over_experts
+    greet(
+        [(me_dp, me ^ o) for o in range(1, experts)]
+        + [(me_dp ^ 1, me)]
+        + [(me_dp ^ (2 * q), me) for q in range(1, chips)]
+    )
+
+    def place(k):
+        return k // 2 * (2 * chips) + chip * 2 + k % 2
+
+    def copy_a(m):
+        return pltpu.make_async_remote_copy(
+            dense_ref.at[m, 1 - core], near.at[m], a_ss.at[m], a_rs.at[m], (me_dp ^ 1, me), MESH
+        )
+
+    def copy_b(m, q):
+        return pltpu.make_async_remote_copy(
+            summed.at[m, chip ^ q], far.at[m, q - 1], b_ss.at[m, q], b_rs.at[m, q],
+            (me_dp ^ (2 * q), me), MESH,
+        )
+
+    def copy_c(m, k, o, peer):
+        return pltpu.make_async_remote_copy(
+            chip_sum.at[m, k], gathered.at[m, o], c_ss.at[m, k], c_rs.at[m, o], (me_dp, peer), MESH
+        )
+
+    def copy_d(m, q):
+        return pltpu.make_async_remote_copy(
+            out_ref.at[m, core], out_ref.at[m, core], d_ss.at[m, q], d_rs.at[m],
+            (me_dp ^ (2 * q), me), MESH,
+        )
+
+    def copy_e(m):
+        return pltpu.make_async_remote_copy(
+            out_ref.at[m, core], out_ref.at[m, core], e_ss.at[m], e_rs.at[m], (me_dp ^ 1, me), MESH
+        )
+
+    def copy_t(i):
+        src = small_ref if i == 0 else tiny.at[0, i - 1]
+        return pltpu.make_async_remote_copy(src, tiny.at[1, i], t_ss.at[i], t_rs.at[i], steps[i], MESH)
+
+    def end_t(i):
+        copy_t(i).wait_recv()
+        mine = small_ref[...] if i == 0 else tiny[0, i - 1]
+        tiny[0, i] = mine + tiny[1, i]
+        if i + 1 < len(steps):
+            copy_t(i + 1).start()
+
+    todo = list(range(len(steps)))
+
+    def advance():
+        if todo:
+            end_t(todo.pop(0))
+
+    order = [3, 0, 1, 2][-matrices:] if matrices < 4 else [3, 0, 1, 2]
+    for m in order:
+        copy_a(m).start()
+    copy_t(0).start()
+    for m in order:
+        copy_a(m).wait_recv()
+        total = dense_ref[m, core].astype(f32) + near[m].astype(f32)
+        summed[m] = total.astype(bf16).reshape(summed.shape[1:])
+        for q in range(1, chips):
+            copy_b(m, q).start()
+    advance()
+    for m in order:
+        total = summed[m, chip].astype(f32)
+        for q in range(1, chips):
+            copy_b(m, q).wait_recv()
+            total += far[m, q - 1].astype(f32)
+        chip_sum[m] = total.astype(bf16)
+        for k in range(group):
+            peer = place(k)
+
+            @pl.when(peer != me)
+            def _():
+                copy_c(m, k, me ^ peer, peer).start()
+
+        advance()
+    for m in order:
+
+        @pl.when(inside)
+        def _():
+            total = chip_sum[m, me // (2 * chips) * 2 + me % 2].astype(f32)
+            for o in range(1, experts):
+                copy_c(m, 0, o, me ^ o).wait_recv()
+                total += gathered[m, o].astype(f32)
+            out_ref[m, core] = total.astype(bf16)
+            for q in range(1, chips):
+                copy_d(m, q).start()
+
+        advance()
+    for m in order:
+
+        @pl.when(jnp.logical_not(inside))
+        def _():
+            copy_d(m, 1).wait_recv()
+
+        copy_e(m).start()
+        advance()
+    while todo:
+        advance()
+    small_out_ref[...] = tiny[0, len(steps) - 1]
+    for m in order:
+        copy_a(m).wait_send()
+        for q in range(1, chips):
+            copy_b(m, q).wait_send()
+        for k in range(group):
+
+            @pl.when(place(k) != me)
+            def _():
+                copy_c(m, k, 1, place(k)).wait_send()
+
+        @pl.when(inside)
+        def _():
+            for q in range(1, chips):
+                copy_d(m, q).wait_send()
+
+        pltpu.make_async_remote_copy(
+            out_ref.at[m, core], out_ref.at[m, 1 - core], e_ss.at[m], e_rs.at[m], (me_dp ^ 1, me), MESH
+        ).wait()
+    for i in range(len(steps)):
+        copy_t(i).wait_send()
+
+
+def run_reduce(copies, experts, *operands):
+    matrices, _, _, per, half = operands[0].shape
+    smalls, width = operands[1].shape
+    chips = copies // 2
+    group = experts // chips
+    steps = copies.bit_length() - 1 + experts.bit_length() - 1
+    shape = jax.ShapeDtypeStruct
+    return pl.pallas_call(
+        partial(reduce_kernel, copies, experts),
+        out_shape=(shape((matrices, 2, per, half), bf16), shape((smalls, width), f32)),
+        in_specs=[VMEM] * 2,
+        out_specs=(VMEM,) * 2,
+        scratch_shapes=[
+            pltpu.VMEM((matrices, experts, per, half), bf16),
+            pltpu.VMEM((matrices, chips, group, per, half), bf16),
+            pltpu.VMEM((matrices, chips - 1, group, per, half), bf16),
+            pltpu.VMEM((matrices, group, per, half), bf16),
+            pltpu.VMEM((matrices, experts, per, half), bf16),
+            pltpu.VMEM((2, steps, smalls, width), f32),
+            DMA((matrices,)), DMA((matrices,)),
+            DMA((matrices, chips)), DMA((matrices, chips)),
+            DMA((matrices, group)), DMA((matrices, experts)),
+            DMA((matrices, chips)), DMA((matrices,)),
+            DMA((matrices,)), DMA((matrices,)),
+            DMA((steps,)), DMA((steps,)),
+        ],
+        compiler_params=pltpu.CompilerParams(
+            collective_id=3, has_side_effects=True, vmem_limit_bytes=VMEM_BYTES
+        ),
+        name="reduce",
+    )(*operands)
 
 
 def local(
@@ -491,77 +853,44 @@
     total_rows = row_count * copies * experts
     capacity = (210 * total_rows + 100 * experts - 1) // (100 * experts)
     most = 8 * row_count // (3 * experts)
-    me = lax.axis_index("expert")
+    me_dp, me = lax.axis_index("dp"), lax.axis_index("expert")
     facts = [priority, expert_ids[:, 0], expert_ids[:, 1], padding]
     facts = facts + [jnp.zeros_like(padding)] * 4
+    columns = jnp.stack(facts, axis=1)
+    gain1, gain2 = norm1_gain[None, :], norm2_gain[None, :]
     (recv_cot, x_slots, gate_slots, qkv, att_t, lse, residual, second, first, pairs, probs) = run_front(
         copies, experts, most, capacity,
-        patches, cotangent, jnp.stack(facts), jnp.stack(facts, axis=1),
-        norm1_gain[None, :], norm1_bias[None, :], qkv_weight, qv_bias[None, :],
-        out_weight, out_bias[None, :], norm2_gain[None, :], norm2_bias[None, :], router,
-    )
-    order = jnp.arange(experts) ^ me
-
-    def exchange(block):
-        block = jnp.take(block.reshape(experts, -1, block.shape[-1]), order, axis=0)
-        out = lax.all_to_all(block, "expert", split_axis=0, concat_axis=0, tiled=True)
-        return jnp.take(out, order, axis=0)
-
-    ret_rows, ret_gate, produced, grads = run_experts(
+        patches, cotangent, jnp.stack(facts), columns,
+        gain1, norm1_bias[None, :], qkv_weight, qv_bias[None, :],
+        out_weight, out_bias[None, :], gain2, norm2_bias[None, :], router,
+    )
+    d_rows, d_gates, produced, grads = run_experts(
         copies, experts, most,
         x_slots, gate_slots, recv_cot, expert_in[0], expert_in_bias, expert_out[0], expert_out_bias,
     )
-    me_dp = lax.axis_index("dp")
-    grads = jnp.take(grads, jnp.arange(copies) ^ me_dp, axis=1)
-    block = grads.shape[-1]
-    g1 = grads[0].transpose(1, 0, 2).reshape(width + 16, -1)
-    g2 = grads[1].transpose(1, 0, 2).reshape(width + 16, -1)
-    g1 = lax.psum_scatter(g1, "dp", scatter_dimension=1, tiled=True).astype(f32)
-    g2 = lax.psum_scatter(g2, "dp", scatter_dimension=1, tiled=True).astype(f32)
-    grad_expert_in, grad_expert_in_bias = g1[:width][None], g1[width][None]
-    grad_expert_out = g2[:width].T[None]
-    gb2 = g1[width + 8 :].reshape(-1)[:width]
-    grad_expert_out_bias = lax.dynamic_slice(gb2, (me_dp * (width // copies),), (width // copies,))[None]
-    ret_produced = exchange(produced).reshape(-1, width)
-    ret_gate = ret_gate[:, 0].reshape(-1, 1)
-    slot = pairs[:, :2].astype(i32)
-    gk, kept, both = pairs[:, 2:4], pairs[:, 4:6], pairs[:, 6:7]
-    chosen = jnp.take(ret_produced, slot.reshape(-1), axis=0).reshape(row_count, 2, width).astype(f32)
-    output = (residual + jnp.sum(gk[:, :, None] * chosen, axis=1)).astype(bf16)
-    d_gate = jnp.take(ret_gate[:, 0], slot.reshape(-1), axis=0).reshape(row_count, 2) * kept
-    matches = expert_ids[:, :, None] == jnp.arange(experts)[None, None, :]
-    picked = jnp.sum(jnp.where(matches, probs[:, None, :], 0.0), axis=-1)
-    gate = picked / both
-    d_picked = (d_gate - jnp.sum(d_gate * gate, axis=1, keepdims=True)) / both
-    d_probs = jnp.sum(jnp.where(matches, d_picked[:, :, None], 0.0), axis=1)
-    d_logits = (probs * (d_probs - jnp.sum(probs * d_probs, axis=1, keepdims=True))).astype(bf16)
-    grad_router = jnp.dot(second.T, d_logits, preferred_element_type=jnp.float32)
-    d_pairs = jnp.take(ret_rows, slot.reshape(-1), axis=0).reshape(row_count, 2, width).astype(f32)
-    d_second = jnp.sum(d_pairs * kept[:, :, None], axis=1) + jnp.dot(d_logits, router.T, preferred_element_type=f32)
-    second_value, second_pull = jax.vjp(normalize, residual, norm2_gain, norm2_bias)
-    d_residual_norm, grad_norm2_gain, grad_norm2_bias = second_pull(d_second)
-    d_residual = cotangent.astype(f32) + d_residual_norm
-    d_branch = d_residual.astype(jnp.bfloat16)
-    grad_out_weight = jnp.dot(att_t, d_branch, preferred_element_type=jnp.float32)
-    grad_out_bias = jnp.sum(d_branch.astype(jnp.float32), axis=0)
-    d_att = jnp.dot(d_branch, out_weight.T, preferred_element_type=jnp.float32).astype(bf16)
-    d_att = d_att.reshape(SEQ_LEN, HEADS, HEAD_DIM)
-    heads = qkv.reshape(SEQ_LEN, 3, HEADS, HEAD_DIM)
-    lse2 = lse[:, :2].reshape(HEADS, row_count)
-    d_q, d_k, d_v = attend_backward((heads[:, 0], heads[:, 1], heads[:, 2], padding > 0, lse2, d_att))
-    d_projected = jnp.stack([d_q, d_k, d_v], axis=1).reshape(row_count, 3 * width).astype(bf16)
-    grad_qkv_weight = jnp.dot(first.T, d_projected, preferred_element_type=jnp.float32)
-    column_sums = jnp.sum(d_projected.astype(jnp.float32), axis=0)
-    grad_qv_bias = jnp.concatenate([column_sums[:width], column_sums[2 * width :]])
-    d_first = jnp.dot(d_projected, qkv_weight.T, preferred_element_type=jnp.float32)
-    first_value, first_pull = jax.vjp(normalize, patches.astype(f32), norm1_gain, norm1_bias)
-    d_inputs, grad_norm1_gain, grad_norm1_bias = first_pull(d_first)
-    grad_patches = (d_residual + d_inputs).astype(jnp.bfloat16)
-    dense = [grad_norm1_gain, grad_norm1_bias, grad_qkv_weight, grad_qv_bias, grad_out_weight, grad_out_bias,
-             grad_norm2_gain, grad_norm2_bias, grad_router]
-    dense = [lax.psum_scatter(g.astype(bf16), "expert", scatter_dimension=0, tiled=True) for g in dense]
-    dense = [lax.psum(g, "dp").astype(f32) for g in dense]
-    return (output, grad_patches, *dense, grad_expert_in, grad_expert_in_bias, grad_expert_out, grad_expert_out_bias)
+    output, grad_patches, dense, small, kept_grads, far_grads = run_back(
+        copies, experts, most,
+        d_rows, d_gates, produced, grads, pairs, probs, columns,
+        second, residual, patches, cotangent, qkv, att_t, lse, first,
+        gain1, gain2, qkv_weight, out_weight, router,
+    )
+    reduced, small = run_reduce(copies, experts, dense, small)
+    expert_grads = kept_grads.astype(f32) + jnp.sum(far_grads.astype(f32), axis=1)
+    grad_expert_in = expert_grads[0, :width][None]
+    grad_expert_in_bias = expert_grads[0, width][None]
+    grad_expert_out = expert_grads[1, :width].T[None]
+    out_bias_grad = expert_grads[0, width + 8 :].reshape(-1)[:width]
+    share = width // copies
+    grad_expert_out_bias = lax.dynamic_slice(out_bias_grad, (me_dp * share,), (share,))[None]
+    weights = reduced.astype(f32).transpose(2, 0, 1, 3).reshape(width // experts, 4 * width)
+    per = width // experts
+    mine = lax.dynamic_slice(small, (0, me * per), (small.shape[0], per))
+    value_bias = lax.dynamic_slice(small[2:4].reshape(-1), (me * 2 * per,), (2 * per,))
+    return (
+        output, grad_patches, mine[0], mine[1], weights[:, : 3 * width], value_bias, weights[:, 3 * width :],
+        mine[4], mine[5], mine[6], mine[8 : 8 + experts].T,
+        grad_expert_in, grad_expert_in_bias, grad_expert_out, grad_expert_out_bias,
+    )
 
 
 def solution(mesh):

time: 605 us -> 376 us (0.62)
  the two profiles are of different devices: /device:TPU:0 before, /device:TPU:9 now
where the time goes in v3:
time: 376 us; the launch traced here: 371 us
  Pallas kernels  334 us (89%)
  local copies, waits for them, and re-layouts  30.7 us (8%)
  other arithmetic  4.78 us (1%)
    pallas_call x1, Pallas kernels, run_experts(): pl.pallas_call(partial(expert_kernel, copies, experts, most, chunks, 512)...  116 us
    pallas_call x1, Pallas kernels, run_back(): pl.pallas_call(partial(back_kernel, copies, experts, most), out_shape=(sh...  76.6 us
    pallas_call x1, Pallas kernels, run_reduce(): pl.pallas_call(partial(reduce_kernel, copies, experts), out_shape=(shape(...  74.8 us
    pallas_call x1, Pallas kernels, run_front(): pl.pallas_call(partial(front_kernel, copies, experts, most, capacity), ou...  67.1 us

profile of v3, /device:TPU:9, one launch (start us, length us, event | category | flops | bytes accessed | tf_op | source)
XLA Modules:
  0.0 370.8 jit_solution(514466678270168178)
XLA Ops:
  0.6 0.8 slice_bitcast_fusion.2
  1.4 0.7 stack.24
  2.1 0.7 stack.25
  2.8 0.6 stack.27.rows_ref
  3.4 0.7 stack.28
  4.1 0.7 stack.29
  4.8 0.1 pad.3.clone
  4.9 0.8 add_add_fusion
  5.7 0.9 copy.44.cols_ref
  6.5 1.5 copy.45.router_ref
  8.0 1.3 broadcast_in_dim.24.gain1_ref
  9.3 1.3 broadcast_in_dim.28.gain2_ref
  10.6 1.3 broadcast_in_dim.26.qv_bias_ref
  11.9 1.3 broadcast_in_dim.25.bias1_ref
  13.1 1.3 broadcast_in_dim.27.out_bias_ref
  14.4 1.3 broadcast_in_dim.29.bias2_ref
  15.7 67.1 %front.1 = (bf16[1536,768]{1,0:T(8,128)(2,1)}, bf16[1536,768]{1,0:T(8,128)(2,1)}, f32[8,8,192]{2,1,0:T(8,128)}, bf16[576,2304]{1,0:T(8,128)(2,1)}, bf16[768,576]...) custom-call(bf16[576,768]{1,0:T(8,128)(2,1)} %patches_ref.3, ...), custom_call_target="tpu_custom_call" | custom-call | tf_op jit(solution)/shard_map/front/pallas_call | solution.py:225
  82.8 115.9 %experts.1 = (bf16[1536,768]{1,0:T(8,128)(2,1)}, f32[8,8,192]{2,1,0:T(8,128)}, bf16[1536,768]{1,0:T(8,128)(2,1)}, bf16[2,4,784,768]{3,2,1,0:T(8,128)(2,1)}) custom-call(bf16[1536,768]{1,0:T(8,128)(2,1)} %get-tuple-element.38.x_ref, f32[8,8,192]{2,1,0:T(8,128)} %get-tuple-element.39.gates_ref, bf16[1536,768]{1,0:T(8,128)(2,1)} %get-tuple-element.40.cot_ref, ...), custom_call_target="tpu_custom_call" | custom-call | tf_op jit(solution)/shard_map/experts/pallas_call | solution.py:427
  198.6 76.6 %back.1 = (bf16[576,768]{1,0:T(8,128)(2,1)}, bf16[576,768]{1,0:T(8,128)(2,1)}, bf16[4,2,8,96,384]{4,3,2,1,0:T(8,128)(2,1)}, f32[16,768]{1,0:T(8,128)}, bf16[2,78...) custom-call(bf16[1536,768]{1,0:T(8,128)(2,1)} %get-tuple-element.41.d_rows_ref, ...), custom_call_target="tpu_custom_call" | custom-call | tf_op jit(solution)/shard_map/back/pallas_call | solution.py:641
  275.3 2.9 convert_add_fusion
  278.2 0.0 copy-start
  278.2 2.0 slice_bitcast_fusion
  280.1 0.9 copy-done
  281.1 1.9 copy.49
  283.0 1.3 fusion
  284.3 0.6 dynamic-slice_bitcast_fusion.1
  285.0 74.8 %reduce.1 = (bf16[4,2,96,384]{3,2,1,0:T(8,128)(2,1)}, f32[16,768]{1,0:T(8,128)}) custom-call(bf16[4,2,8,96,384]{4,3,2,1,0:T(8,128)(2,1)} %get-tuple-element.55.dense_ref, f32[16,768]{1,0:T(8,128)} %get-tuple-element.56.small_ref), custom_call_target="tpu_custom_call" | custom-call | tf_op jit(solution)/shard_map/reduce/pallas_call | solution.py:820
  359.8 1.1 convert_bitcast_fusion
  360.9 0.9 copy.48
  361.8 0.0 copy-start.2
  361.8 0.9 reshape.48
  362.8 0.0 copy-start.1
  362.8 1.0 slice.64
  363.8 0.7 slice.65
  364.5 0.7 slice.54
  365.3 0.6 dynamic_slice.10
  365.9 1.4 dynamic-slice_bitcast_fusion
  367.3 1.5 dynamic-slice_bitcast_fusion.2
  368.7 0.0 copy-done.2
  368.8 0.9 copy.52
  369.7 0.0 copy-done.1
  369.7 0.9 copy.53
  (3 shorter events, 0.0 us)
Async XLA Ops:
  278.2 2.9 copy-start
  361.8 6.9 %copy-start.2 = (bf16[576,768]{1,0:T(8,128)(2,1)S(1)}, bf16[576,768]{1,0:T(8,128)(2,1)}, u32[]{:S(2)}) copy-start(bf16[576,768]{1,0:T(8,128)(2,1)} %get-tuple-element.132) | copy-start | bytes 2654212
  362.8 6.9 %copy-start.1 = (bf16[576,768]{1,0:T(8,128)(2,1)S(1)}, bf16[576,768]{1,0:T(8,128)(2,1)}, u32[]{:S(2)}) copy-start(bf16[576,768]{1,0:T(8,128)(2,1)} %get-tuple-element.133) | copy-start | bytes 2654212

commit v4 on v2

--- a/solution.py
+++ b/solution.py
@@ -16,7 +16,7 @@
 NN = (((1,), (0,)), ((), ()))
 NT = (((1,), (1,)), ((), ()))
 TN = (((0,), (0,)), ((), ()))
-VMEM_BYTES = 60 << 20
+VMEM_BYTES = 63 << 20
 bf16 = jnp.bfloat16
 f32 = jnp.float32
 i32 = jnp.int32
@@ -28,6 +28,10 @@
 
 def iota(shape, axis):
     return lax.broadcasted_iota(i32, shape, axis)
+
+
+def flat(ref):
+    return ref[...].reshape(1, ref.shape[0])
 
 
 def ones_where(mask):
@@ -58,15 +62,20 @@
 
 def front_kernel(
     copies, experts, most, capacity,
-    patches_ref, cot_ref, rows_ref, cols_ref, gain1_ref, bias1_ref, qkv_w_ref, qv_bias_ref,
+    patches_ref, cot_ref, priority_ref, ids_ref, padding_ref, gain1_ref, bias1_ref, qkv_w_ref, qv_bias_ref,
     out_w_ref, out_bias_ref, gain2_ref, bias2_ref, router_ref,
     recv_cot_ref, x_slots_ref, gate_slots_ref, qkv_ref, att_t_ref, lse_ref, residual_ref,
     second_ref, first_ref, pairs_ref, probs_ref,
-    cot_send, table, counts, cot_ss, cot_rs, near_ss, near_rs, far_ss, far_rs,
+    cot_send, rows_ref, table, counts, cot_ss, cot_rs, near_ss, near_rs, far_ss, far_rs,
 ):
     me_dp = lax.axis_index("dp")
     me = lax.axis_index("expert")
     rows, width = patches_ref.shape
+    rows_ref[0:1, :] = priority_ref[...].reshape(1, rows)
+    rows_ref[1:3, :] = ids_ref[...]
+    rows_ref[3:4, :] = padding_ref[...].reshape(1, rows)
+    rows_ref[4:, :] = jnp.zeros((4, rows), i32)
+    cols = rows_ref[...].T
     greet(
         [(me_dp, me ^ o) for o in range(1, experts)]
         + [(me_dp ^ p, me) for p in range(1, copies)]
@@ -83,7 +92,7 @@
     place_t = dot(named_t, before_t).astype(i32) + expert_rows * most
     slot0_row = jnp.sum(jnp.where(expert_rows == id0_row, place_t, 0), axis=0, keepdims=True)
     slot1_row = jnp.sum(jnp.where(expert_rows == id1_row, place_t, 0), axis=0, keepdims=True)
-    id0_col, id1_col = cols_ref[:, 1:2], cols_ref[:, 2:3]
+    id0_col, id1_col = cols[:, 1:2], cols[:, 2:3]
     rel0_col, rel1_col = id0_col ^ me, id1_col ^ me
     expert_cols = iota((rows, experts), 1)
     named = ones_where((expert_cols == rel0_col) | (expert_cols == rel1_col))
@@ -109,14 +118,14 @@
             send(cot_send.at[part], recv_cot_ref.at[part], cot_ss.at[o], cot_rs.at[o], (me_dp, me ^ o))
         )
     inputs = patches_ref[...].astype(f32)
-    first = (standardize(inputs)[0] * gain1_ref[...] + bias1_ref[...]).astype(bf16)
+    first = (standardize(inputs)[0] * flat(gain1_ref) + flat(bias1_ref)).astype(bf16)
     first_ref[...] = first
-    qkv_ref[:, :width] = (dot(first, qkv_w_ref[:, :width]) + qv_bias_ref[:, :width]).astype(bf16)
+    qkv_ref[:, :width] = (dot(first, qkv_w_ref[:, :width]) + flat(qv_bias_ref)[:, :width]).astype(bf16)
     qkv_ref[:, width : 2 * width] = dot(first, qkv_w_ref[:, width : 2 * width]).astype(bf16)
     qkv_ref[:, 2 * width :] = (
-        dot(first, qkv_w_ref[:, 2 * width :]) + qv_bias_ref[:, width:]
+        dot(first, qkv_w_ref[:, 2 * width :]) + flat(qv_bias_ref)[:, width:]
     ).astype(bf16)
-    key_bias = jnp.where(cols_ref[:, 3:4] > 0, 0.0, -1e30)
+    key_bias = jnp.where(cols[:, 3:4] > 0, 0.0, -1e30)
     scale = LOG2E * HEAD_DIM ** (-0.5)
     pair_width = 2 * HEAD_DIM
 
@@ -148,13 +157,13 @@
         return 0
 
     lax.fori_loop(0, HEADS // 2, attend, 0)
-    residual = inputs + dot(att_t_ref[...], out_w_ref[...], TN) + out_bias_ref[...]
+    residual = inputs + dot(att_t_ref[...], out_w_ref[...], TN) + flat(out_bias_ref)
     residual_ref[...] = residual
-    second = (standardize(residual)[0] * gain2_ref[...] + bias2_ref[...]).astype(bf16)
+    second = (standardize(residual)[0] * flat(gain2_ref) + flat(bias2_ref)).astype(bf16)
     second_ref[...] = second
     for o in range(experts):
         x_slots_ref[pl.ds(o * most, most), :] = dot(taken(o), second).astype(bf16)
-    logits = dot(second, router_ref[...])
+    logits = dot(second, router_ref[...], NT)
     raised = jnp.exp(logits - jnp.max(logits, axis=-1, keepdims=True))
     probs = raised / jnp.sum(raised, axis=-1, keepdims=True)
     probs_ref[...] = probs
@@ -165,7 +174,7 @@
     for far_copy in far:
         far_copy.wait_recv()
     counts[...] = jnp.zeros_like(counts)
-    rank_col = cols_ref[:, 0:1]
+    rank_col = cols[:, 0:1]
 
     def count(block, _):
         entry = table[block // experts, block % experts]
@@ -193,7 +202,7 @@
         axis=1,
         keepdims=True,
     )
-    real_col = cols_ref[:, 3:4] > 0
+    real_col = cols[:, 3:4] > 0
     kept0 = jnp.where(real_col & (position0 < capacity), 1.0, 0.0)
     kept1 = jnp.where(real_col & (position1 < capacity), 1.0, 0.0)
     gate0, gate1 = gate0 * kept0, gate1 * kept1
@@ -201,9 +210,10 @@
         slots = iota((rows, most), 1) + o * most
         gates = jnp.where(slots == slot0_col, gate0, 0.0) + jnp.where(slots == slot1_col, gate1, 0.0)
         gate_slots_ref[o] = jnp.broadcast_to(jnp.sum(gates, axis=0, keepdims=True), (8, most))
-    lanes = iota((rows, 8), 1)
-    columns = [slot0_col.astype(f32), slot1_col.astype(f32), gate0, gate1, kept0, kept1, both]
-    packed = jnp.zeros((rows, 8), f32)
+    lanes = iota((rows, 16), 1)
+    columns = [slot0_col, slot1_col, gate0, gate1, kept0, kept1, both, cols[:, 3:4], id0_col, id1_col]
+    columns = [column.astype(f32) for column in columns]
+    packed = jnp.zeros((rows, 16), f32)
     for i, column in enumerate(columns):
         packed = jnp.where(lanes == i, column, packed)
     pairs_ref[...] = packed
@@ -234,13 +244,14 @@
             shape((rows, width), f32),
             shape((rows, width), bf16),
             shape((rows, width), bf16),
-            shape((rows, 8), f32),
+            shape((rows, 16), f32),
             shape((rows, experts), f32),
         ),
-        in_specs=[VMEM] * 13,
+        in_specs=[VMEM] * 14,
         out_specs=(VMEM,) * 11,
         scratch_shapes=[
             pltpu.VMEM((slots, width), bf16),
+            pltpu.VMEM((8, rows), i32),
             pltpu.VMEM((copies, experts, 8, rows), i32),
             pltpu.VMEM((rows + 8, 2 * experts), f32),
             DMA((experts,)), DMA((experts,)),
@@ -312,16 +323,24 @@
     own = pltpu.make_async_copy(x_ref.at[chunk(0)], recv_x.at[chunk(0)], own_sem)
     own.start()
     greet([(me_dp, me ^ o) for o in range(1, experts)])
-    for o in range(1, experts):
-        move_g(o).start()
-        move_x(o).start()
+
+    def begin(g):
+        for o in range(max(1, g * chunks), (g + 1) * chunks):
+            move_g(o).start()
+            move_x(o).start()
+
+    groups = experts // chunks
+    order = [0, *range(groups // 2, groups), *range(1, groups // 2)]
+    begin(order[0])
+    begin(order[1])
     recv_g[0] = gates_ref[0]
     bias_sum[...] = jnp.zeros_like(bias_sum)
     x_t[width:, :] = jnp.ones_like(x_t[width:, :])
     own.wait()
     own_d = pltpu.make_async_copy(send_d.at[chunk(0)], d_rows_ref.at[chunk(0)], own_d_sem)
 
-    def work(g, _):
+    def work(n, _):
+        g = n % 2 * (groups // 2) + n // 2
         for j in range(chunks):
             o = g * chunks + j
 
@@ -355,6 +374,12 @@
             return 0
 
         lax.fori_loop(0, hidden_width // tile, step, 0)
+
+        @pl.when(n == 0)
+        def _():
+            for later in order[2:]:
+                begin(later)
+
         send_d[here, :] = total_d[...].astype(bf16)
         produced = (total_p[...] + out_bias_ref[...]).astype(bf16)
         produced_ref[here, :] = produced
@@ -376,7 +401,7 @@
 
         return 0
 
-    lax.fori_loop(0, experts // chunks, work, 0)
+    lax.fori_loop(0, groups, work, 0)
 
     def store(w, p):
         return pltpu.make_async_copy(stage.at[w], grads_ref.at[w, p], stage_sem.at[w])
@@ -457,28 +482,421 @@
     )(*operands)
 
 
-def exact_gelu(values):
-    return jax.nn.gelu(values, approximate=False)
-
-
-def normalize(values, gain, shift):
-    return standardize(values)[0] * gain + shift
-
-
-def attend_backward(pieces):
-    queries, key_rows, value_rows, key_valid, lse2, d_attended = pieces
-    scores = jnp.einsum("qhd,khd->hqk", queries, key_rows, preferred_element_type=f32) * HEAD_DIM ** (-0.5)
-    scores = jnp.where(key_valid[None, None, :], scores, -1000000000.0)
-    probabilities = jnp.exp2(scores * LOG2E - lse2[:, :, None])
-    weights = probabilities.astype(jnp.bfloat16)
-    d_values = jnp.einsum("hqk,qhd->khd", weights, d_attended, preferred_element_type=jnp.float32)
-    d_weights = jnp.einsum("qhd,khd->hqk", d_attended, value_rows, preferred_element_type=jnp.float32)
-    centre = jnp.sum(probabilities * d_weights, axis=-1, keepdims=True)
-    d_scores = (probabilities * (d_weights - centre)).astype(jnp.bfloat16)
-    scaling = HEAD_DIM ** (-0.5)
-    d_queries = jnp.einsum("hqk,khd->qhd", d_scores, key_rows, preferred_element_type=jnp.float32) * scaling
-    d_keys = jnp.einsum("hqk,qhd->khd", d_scores, queries, preferred_element_type=jnp.float32) * scaling
-    return (d_queries, d_keys, d_values)
+def back_kernel(
+    copies, experts, most,
+    d_rows_ref, d_gates_ref, produced_ref, grads_ref, pairs_ref, probs_ref,
+    second_ref, residual_ref, patches_ref, cot_ref, qkv_ref, att_t_ref, lse_ref, first_ref,
+    gain1_ref, gain2_ref, qkv_w_ref, out_w_ref, router_ref,
+    output_ref, grad_patches_ref, sums_ref, small_sums_ref, kept_grads_ref, far_grads_ref,
+    recv_p, own_grads, near_grads, d_qkv, d_att, d_att_t, d_residual_ref,
+    dense, small, halves, landed, crossed, tiny,
+    p_ss, p_rs, n_ss, n_rs, f_ss, f_rs, own_sem, kept_sem,
+    a_ss, a_rs, b_ss, b_rs, c_ss, c_rs, e_ss, e_rs, t_ss, t_rs,
+):
+    me_dp = lax.axis_index("dp")
+    me = lax.axis_index("expert")
+    rows, width = patches_ref.shape
+    slots = experts * most
+    chips = copies // 2
+    core = me_dp % 2
+    per = width // experts
+    half = width // 2
+    partner = (me_dp ^ 1, me)
+    bits = [1, 0, *range(2, experts.bit_length() - 1)]
+    steps = [(me_dp ^ (1 << i), me) for i in range(copies.bit_length() - 1)]
+    steps += [(me_dp, me ^ (1 << i)) for i in range(experts.bit_length() - 1)]
+
+    def copy_a(m):
+        return pltpu.make_async_remote_copy(
+            dense.at[m, 1 - core], halves.at[m], a_ss.at[m], a_rs.at[m], partner, MESH
+        )
+
+    def copy_b(m, i):
+        part = pl.ds(experts >> (i + 1), experts >> (i + 1))
+        return pltpu.make_async_remote_copy(
+            dense.at[m, core, part], landed.at[m, part], b_ss.at[m, i], b_rs.at[m, i],
+            (me_dp, me ^ (1 << bits[i])), MESH,
+        )
+
+    def copy_c(m, q):
+        return pltpu.make_async_remote_copy(
+            dense.at[m, core, 0], crossed.at[m, q - 1], c_ss.at[m, q], c_rs.at[m, q],
+            (me_dp ^ (2 * q), me), MESH,
+        )
+
+    def copy_e(m):
+        return pltpu.make_async_remote_copy(
+            sums_ref.at[m, core], sums_ref.at[m, core], e_ss.at[m], e_rs.at[m], partner, MESH
+        )
+
+    def begin(m, k):
+        if k == 0:
+            copy_a(m).start()
+        elif k <= len(bits):
+            copy_b(m, k - 1).start()
+        elif k == len(bits) + 1:
+            for q in range(1, chips):
+                copy_c(m, q).start()
+        else:
+            copy_e(m).start()
+
+    def end(m, k):
+        if k == 0:
+            copy_a(m).wait_recv()
+            dense[m, core] = (dense[m, core].astype(f32) + halves[m].astype(f32)).astype(bf16)
+        elif k <= len(bits):
+            copy_b(m, k - 1).wait_recv()
+            n = experts >> k
+            total = dense[m, core, 0:n].astype(f32) + landed[m, n : 2 * n].astype(f32)
+            dense[m, core, 0:n] = total.astype(bf16)
+        elif k == len(bits) + 1:
+            total = dense[m, core, 0].astype(f32)
+            for q in range(1, chips):
+                copy_c(m, q).wait_recv()
+                total += crossed[m, q - 1].astype(f32)
+            sums_ref[m, core] = total.astype(bf16)
+
+    stages = [0] * 4
+
+    def advance(m):
+        if stages[m] < len(bits) + 2:
+            end(m, stages[m])
+            stages[m] += 1
+            begin(m, stages[m])
+
+    def copy_t(i):
+        src = small if i == 0 else tiny.at[0, i - 1]
+        return pltpu.make_async_remote_copy(src, tiny.at[1, i], t_ss.at[i], t_rs.at[i], steps[i], MESH)
+
+    todo = list(range(len(steps)))
+
+    def advance_small():
+        if todo:
+            i = todo.pop(0)
+            copy_t(i).wait_recv()
+            mine = small[...] if i == 0 else tiny[0, i - 1]
+            tiny[0, i] = mine + tiny[1, i]
+            if i + 1 < len(steps):
+                copy_t(i + 1).start()
+
+    def copy_f(w, q):
+        return pltpu.make_async_remote_copy(
+            near_grads.at[w, q], far_grads_ref.at[w, q - 1], f_ss.at[w, q], f_rs.at[w, q],
+            (me_dp ^ (2 * q), me), MESH,
+        )
+
+    greet(
+        [(me_dp, me ^ o) for o in range(1, experts)]
+        + [partner]
+        + [(me_dp ^ (2 * q), me) for q in range(1, chips)]
+    )
+    near = [
+        send(grads_ref.at[w, 2 * q + 1], near_grads.at[w, q], n_ss.at[w, q], n_rs.at[w, q], partner)
+        for q in range(chips)
+        for w in range(2)
+    ]
+    turns = [(w, q) for q in [*range(1, chips), 0] for w in range(2)]
+    own = [
+        pltpu.make_async_copy(grads_ref.at[w, 2 * q], own_grads.at[i % 2], own_sem.at[i % 2])
+        for i, (w, q) in enumerate(turns)
+    ]
+    for copy in own[:2]:
+        copy.start()
+    returns = []
+    for o in range(1, experts):
+        part = pl.ds(o * most, most)
+        returns.append(
+            send(produced_ref.at[part], recv_p.at[part], p_ss.at[o], p_rs.at[o], (me_dp, me ^ o))
+        )
+    own_p = pltpu.make_async_copy(
+        produced_ref.at[pl.ds(0, most)], recv_p.at[pl.ds(0, most)], p_rs.at[0]
+    )
+    own_p.start()
+    slot0, slot1 = pairs_ref[:, 0:1].astype(i32), pairs_ref[:, 1:2].astype(i32)
+    kept0, kept1, both = pairs_ref[:, 4:5], pairs_ref[:, 5:6], pairs_ref[:, 6:7]
+    places = iota((rows, slots), 1)
+    d_second = dot(ones_where((places == slot0) | (places == slot1)), d_rows_ref[...])
+    d_gate0 = jnp.zeros((rows, 1), f32)
+    d_gate1 = jnp.zeros((rows, 1), f32)
+    for o in range(experts):
+        part = iota((rows, most), 1) + o * most
+        line = d_gates_ref[o][0:1, :]
+        d_gate0 += jnp.sum(jnp.where(part == slot0, line, 0.0), axis=1, keepdims=True)
+        d_gate1 += jnp.sum(jnp.where(part == slot1, line, 0.0), axis=1, keepdims=True)
+    d_gate0, d_gate1 = d_gate0 * kept0, d_gate1 * kept1
+    probs = probs_ref[...]
+    names = iota((rows, experts), 1)
+    is0, is1 = names == pairs_ref[:, 8:9].astype(i32), names == pairs_ref[:, 9:10].astype(i32)
+    share0 = jnp.sum(jnp.where(is0, probs, 0.0), axis=1, keepdims=True) / both
+    share1 = jnp.sum(jnp.where(is1, probs, 0.0), axis=1, keepdims=True) / both
+    centre = d_gate0 * share0 + d_gate1 * share1
+    d_probs = jnp.where(is0, (d_gate0 - centre) / both, 0.0) + jnp.where(is1, (d_gate1 - centre) / both, 0.0)
+    d_logits = (probs * (d_probs - jnp.sum(probs * d_probs, axis=1, keepdims=True))).astype(bf16)
+    small[8:, :] = jnp.zeros_like(small[8:, :])
+    small[8 : 8 + experts, :] = dot(d_logits, second_ref[...], TN)
+    d_second += dot(d_logits, router_ref[...])
+    n, inverse = standardize(residual_ref[...])
+    small[5:6, :] = jnp.sum(d_second * n, axis=0, keepdims=True)
+    small[6:7, :] = jnp.sum(d_second, axis=0, keepdims=True)
+    m = d_second * flat(gain2_ref)
+    d_residual = cot_ref[...].astype(f32) + inverse * (
+        m - jnp.mean(m, axis=-1, keepdims=True) - n * jnp.mean(m * n, axis=-1, keepdims=True)
+    )
+    d_residual_ref[...] = d_residual
+    d_branch = d_residual.astype(bf16)
+    small[4:5, :] = jnp.sum(d_branch.astype(f32), axis=0, keepdims=True)
+    small[7:8, :] = jnp.zeros((1, width), f32)
+
+    def keep(matrix, value):
+        for e in range(experts):
+            r = e ^ me
+            at = 0
+            for bit in bits:
+                at = at * 2 + (r // (1 << bit)) % 2
+            for h in range(2):
+                dense[matrix, h, at] = value[e * per : (e + 1) * per, h * half : (h + 1) * half].astype(bf16)
+        begin(matrix, 0)
+
+    keep(3, dot(att_t_ref[...], d_branch))
+    for copy in near:
+        copy.wait_recv()
+    for i, (w, q) in enumerate(turns):
+        own[i].wait()
+        near_grads[w, q] = (own_grads[i % 2].astype(f32) + near_grads[w, q].astype(f32)).astype(bf16)
+        if i + 2 < len(turns):
+            own[i + 2].start()
+        if q > 0:
+            copy_f(w, q).start()
+    kept = pltpu.make_async_copy(near_grads.at[:, 0], kept_grads_ref, kept_sem)
+    kept.start()
+    advance(3)
+    d_att[...] = dot(d_branch, out_w_ref[...], NT).astype(bf16)
+    d_att_t[...] = dot(out_w_ref[...], d_branch, NT).astype(bf16)
+    key_bias = jnp.where(pairs_ref[:, 7:8] > 0, 0.0, -1e30)
+    scale = LOG2E * HEAD_DIM ** (-0.5)
+    pair_width = 2 * HEAD_DIM
+
+    def attend(pair, _):
+        base = pl.multiple_of(pair * pair_width, pair_width)
+        here = pl.ds(base, pair_width)
+        q = qkv_ref[:, here]
+        k = qkv_ref[:, pl.ds(base + width, pair_width)]
+        v = qkv_ref[:, pl.ds(base + 2 * width, pair_width)]
+        k_t = k.T
+        d_out = d_att[:, here]
+        products = att_t_ref[here, :].astype(f32) * d_att_t[here, :].astype(f32)
+        lanes = iota((rows, pair_width), 1)
+        d_q, d_k, d_v = [], [], []
+        for a in range(2):
+            mine = (lanes >= HEAD_DIM) == (a == 1)
+            k_a = jnp.where(mine, k, jnp.zeros((), bf16))
+            v_a = jnp.where(mine, v, jnp.zeros((), bf16))
+            part = slice(a * HEAD_DIM, (a + 1) * HEAD_DIM)
+            delta = jnp.sum(products[part, :], axis=0, keepdims=True)
+            weights = jnp.exp2((dot(k_a, q, NT) + key_bias) * scale - lse_ref[pair][a : a + 1, :])
+            d_scores = (weights * (dot(v_a, d_out, NT) - delta)).astype(bf16)
+            d_v.append(dot(weights.astype(bf16), d_out))
+            d_k.append(dot(d_scores, q))
+            d_q.append(dot(k_t[part, :], d_scores))
+        low = lanes < HEAD_DIM
+        down = HEAD_DIM ** (-0.5)
+        d_qkv[:, here] = (jnp.concatenate(d_q, axis=0).T * down).astype(bf16)
+        d_qkv[:, pl.ds(base + width, pair_width)] = (jnp.where(low, d_k[0], d_k[1]) * down).astype(bf16)
+        d_qkv[:, pl.ds(base + 2 * width, pair_width)] = jnp.where(low, d_v[0], d_v[1]).astype(bf16)
+        return 0
+
+    lax.fori_loop(0, HEADS // 2, attend, 0)
+    first_t = first_ref[...].T
+    ones = jnp.ones((8, rows), bf16)
+    for i in range(3):
+        part = slice(i * width, (i + 1) * width)
+        keep(i, dot(first_t, d_qkv[:, part]))
+        if i != 1:
+            small[2 + i // 2 : 3 + i // 2, :] = dot(ones, d_qkv[:, part])[0:1, :]
+        if i > 0:
+            advance(i - 1)
+    d_first = dot(d_qkv[...], qkv_w_ref[...], NT)
+    advance(2)
+    n, inverse = standardize(patches_ref[...].astype(f32))
+    small[0:1, :] = jnp.sum(d_first * n, axis=0, keepdims=True)
+    small[1:2, :] = jnp.sum(d_first, axis=0, keepdims=True)
+    copy_t(0).start()
+    m = d_first * flat(gain1_ref)
+    grad_patches_ref[...] = (
+        d_residual_ref[...]
+        + inverse * (m - jnp.mean(m, axis=-1, keepdims=True) - n * jnp.mean(m * n, axis=-1, keepdims=True))
+    ).astype(bf16)
+    own_p.wait()
+    for copy in returns:
+        copy.wait()
+    blocks = 3
+    lines = rows // blocks
+
+    def combine(i, _):
+        part = pl.ds(pl.multiple_of(i * lines, lines), lines)
+        facts = pairs_ref[part, :]
+        spots = iota((lines, slots), 1)
+        output_ref[part, :] = (
+            residual_ref[part, :]
+            + facts[:, 2:3] * dot(ones_where(spots == facts[:, 0:1].astype(i32)), recv_p[...])
+            + facts[:, 3:4] * dot(ones_where(spots == facts[:, 1:2].astype(i32)), recv_p[...])
+        ).astype(bf16)
+        return 0
+
+    lax.fori_loop(0, blocks, combine, 0)
+    for _ in range(len(bits) + 2):
+        for m in [3, 0, 1, 2]:
+            advance(m)
+        advance_small()
+    while todo:
+        advance_small()
+    small_sums_ref[...] = tiny[0, len(steps) - 1]
+    for copy in near:
+        copy.wait_send()
+    kept.wait()
+    for q in range(1, chips):
+        for w in range(2):
+            copy_f(w, q).wait()
+    for m in range(4):
+        copy_a(m).wait_send()
+        for i in range(len(bits)):
+            copy_b(m, i).wait_send()
+        for q in range(1, chips):
+            copy_c(m, q).wait_send()
+        pltpu.make_async_remote_copy(
+            sums_ref.at[m, core], sums_ref.at[m, 1 - core], e_ss.at[m], e_rs.at[m], partner, MESH
+        ).wait()
+    for i in range(len(steps)):
+        copy_t(i).wait_send()
+
+
+def run_back(copies, experts, most, *operands):
+    rows, width = operands[8].shape
+    slots = experts * most
+    chips = copies // 2
+    block = operands[3].shape[-1]
+    shape = jax.ShapeDtypeStruct
+    smalls = -(-(8 + experts) // 16) * 16
+    per, half = width // experts, width // 2
+    bits = experts.bit_length() - 1
+    steps = copies.bit_length() - 1 + bits
+    return pl.pallas_call(
+        partial(back_kernel, copies, experts, most),
+        out_shape=(
+            shape((rows, width), bf16),
+            shape((rows, width), bf16),
+            shape((4, 2, per, half), bf16),
+            shape((smalls, width), f32),
+            shape((2, width + 16, block), bf16),
+            shape((2, chips - 1, width + 16, block), bf16),
+        ),
+        in_specs=[VMEM] * 2 + [HBM] * 2 + [VMEM] * 15,
+        out_specs=(VMEM,) * 4 + (HBM,) * 2,
+        scratch_shapes=[
+            pltpu.VMEM((slots, width), bf16),
+            pltpu.VMEM((2, width + 16, block), bf16),
+            pltpu.VMEM((2, chips, width + 16, block), bf16),
+            pltpu.VMEM((rows, 3 * width), bf16),
+            pltpu.VMEM((rows, width), bf16),
+            pltpu.VMEM((width, rows), bf16),
+            pltpu.VMEM((rows, width), f32),
+            pltpu.VMEM((4, 2, experts, per, half), bf16),
+            pltpu.VMEM((smalls, width), f32),
+            pltpu.VMEM((4, experts, per, half), bf16),
+            pltpu.VMEM((4, experts, per, half), bf16),
+            pltpu.VMEM((4, chips - 1, per, half), bf16),
+            pltpu.VMEM((2, steps, smalls, width), f32),
+            DMA((experts,)), DMA((experts,)),
+            DMA((2, chips)), DMA((2, chips)),
+            DMA((2, chips)), DMA((2, chips)),
+            DMA((2,)), DMA(()),
+            DMA((4,)), DMA((4,)),
+            DMA((4, bits)), DMA((4, bits)),
+            DMA((4, chips)), DMA((4, chips)),
+            DMA((4,)), DMA((4,)),
+            DMA((steps,)), DMA((steps,)),
+        ],
+        compiler_params=pltpu.CompilerParams(
+            collective_id=2, has_side_effects=True, vmem_limit_bytes=VMEM_BYTES
+        ),
+        name="back",
+    )(*operands)
+
+
+def finish_kernel(
+    copies, experts,
+    kept_ref, far_ref, sums_ref, small_ref,
+    gain1_ref, bias1_ref, qkv_w_ref, qv_bias_ref, out_w_ref, out_bias_ref, gain2_ref, bias2_ref, router_ref,
+    in_w_ref, in_bias_ref, expert_out_ref, expert_out_bias_ref,
+    turned, turned_bias,
+):
+    width = small_ref.shape[1]
+    per, half = width // experts, width // 2
+    me = lax.axis_index("expert")
+    me_dp = lax.axis_index("dp")
+
+    def total(w, part):
+        value = kept_ref[w, part, :].astype(f32)
+        for q in range(copies // 2 - 1):
+            value += far_ref[w, q, part, :].astype(f32)
+        return value
+
+    body = slice(0, width)
+    in_w_ref[0] = total(0, body)
+    expert_out_ref[0] = total(1, body).T
+    tail = total(0, slice(width, width + 16))
+    in_bias_ref[...] = tail[0:1, :]
+    block = tail.shape[1]
+    lines = [tail[8 + i : 9 + i, :] for i in range(-(-width // block))]
+    bias_row = jnp.concatenate(lines, axis=1)[:, :width]
+    turned_bias[...] = jnp.concatenate([bias_row, jnp.zeros((127, width), f32)], axis=0).T
+    share = width // copies
+    mine = turned_bias[pl.ds(pl.multiple_of(me_dp * share, share), share), :]
+    pad = -share % 128
+    mine = jnp.concatenate([mine, jnp.zeros((pad, 128), f32)], axis=0) if pad else mine
+    expert_out_bias_ref[...] = mine.T[0:1, :share]
+    count = small_ref.shape[0]
+    turned[...] = jnp.concatenate([small_ref[...], jnp.zeros((128 - count, width), f32)], axis=0).T
+
+    def share_of(start, n):
+        value = turned[pl.ds(pl.multiple_of(start, 8), n), :]
+        pad = -n % 128
+        return (jnp.concatenate([value, jnp.zeros((pad, 128), f32)], axis=0) if pad else value).T
+
+    vectors = share_of(me * per, per)
+    for ref, i in [(gain1_ref, 0), (bias1_ref, 1), (out_bias_ref, 4), (gain2_ref, 5), (bias2_ref, 6)]:
+        ref[...] = vectors[i : i + 1, :per].reshape(per)
+    router_ref[...] = vectors[8 : 8 + experts, :per]
+    values = share_of(me % (experts // 2) * 2 * per, 2 * per)
+    picked = jnp.where(me < experts // 2, values[2:3, :], values[3:4, :])
+    qv_bias_ref[...] = picked[:, : 2 * per].reshape(2 * per)
+    for i in range(3):
+        for h in range(2):
+            qkv_w_ref[:, i * width + h * half : i * width + (h + 1) * half] = sums_ref[i, h].astype(f32)
+    for h in range(2):
+        out_w_ref[:, h * half : (h + 1) * half] = sums_ref[3, h].astype(f32)
+
+
+def run_finish(copies, experts, *operands):
+    smalls, width = operands[3].shape
+    block = operands[0].shape[-1]
+    per = width // experts
+    shape = jax.ShapeDtypeStruct
+    return pl.pallas_call(
+        partial(finish_kernel, copies, experts),
+        out_shape=(
+            shape((per,), f32), shape((per,), f32), shape((per, 3 * width), f32), shape((2 * per,), f32),
+            shape((per, width), f32), shape((per,), f32), shape((per,), f32), shape((per,), f32),
+            shape((experts, per), f32),
+            shape((1, width, block), f32), shape((1, block), f32),
+            shape((1, block, width), f32), shape((1, width // copies), f32),
+        ),
+        in_specs=[VMEM] * 4,
+        out_specs=(VMEM,) * 13,
+        scratch_shapes=[pltpu.VMEM((width, 128), f32), pltpu.VMEM((width, 128), f32)],
+        compiler_params=pltpu.CompilerParams(vmem_limit_bytes=VMEM_BYTES),
+        name="finish",
+    )(*operands)
 
 
 def local(
@@ -491,77 +909,25 @@
     total_rows = row_count * copies * experts
     capacity = (210 * total_rows + 100 * experts - 1) // (100 * experts)
     most = 8 * row_count // (3 * experts)
-    me = lax.axis_index("expert")
-    facts = [priority, expert_ids[:, 0], expert_ids[:, 1], padding]
-    facts = facts + [jnp.zeros_like(padding)] * 4
     (recv_cot, x_slots, gate_slots, qkv, att_t, lse, residual, second, first, pairs, probs) = run_front(
         copies, experts, most, capacity,
-        patches, cotangent, jnp.stack(facts), jnp.stack(facts, axis=1),
-        norm1_gain[None, :], norm1_bias[None, :], qkv_weight, qv_bias[None, :],
-        out_weight, out_bias[None, :], norm2_gain[None, :], norm2_bias[None, :], router,
-    )
-    order = jnp.arange(experts) ^ me
-
-    def exchange(block):
-        block = jnp.take(block.reshape(experts, -1, block.shape[-1]), order, axis=0)
-        out = lax.all_to_all(block, "expert", split_axis=0, concat_axis=0, tiled=True)
-        return jnp.take(out, order, axis=0)
-
-    ret_rows, ret_gate, produced, grads = run_experts(
+        patches, cotangent, priority, expert_ids.T, padding, norm1_gain, norm1_bias, qkv_weight, qv_bias,
+        out_weight, out_bias, norm2_gain, norm2_bias, router.T,
+    )
+    d_rows, d_gates, produced, grads = run_experts(
         copies, experts, most,
         x_slots, gate_slots, recv_cot, expert_in[0], expert_in_bias, expert_out[0], expert_out_bias,
     )
-    me_dp = lax.axis_index("dp")
-    grads = jnp.take(grads, jnp.arange(copies) ^ me_dp, axis=1)
-    block = grads.shape[-1]
-    g1 = grads[0].transpose(1, 0, 2).reshape(width + 16, -1)
-    g2 = grads[1].transpose(1, 0, 2).reshape(width + 16, -1)
-    g1 = lax.psum_scatter(g1, "dp", scatter_dimension=1, tiled=True).astype(f32)
-    g2 = lax.psum_scatter(g2, "dp", scatter_dimension=1, tiled=True).astype(f32)
-    grad_expert_in, grad_expert_in_bias = g1[:width][None], g1[width][None]
-    grad_expert_out = g2[:width].T[None]
-    gb2 = g1[width + 8 :].reshape(-1)[:width]
-    grad_expert_out_bias = lax.dynamic_slice(gb2, (me_dp * (width // copies),), (width // copies,))[None]
-    ret_produced = exchange(produced).reshape(-1, width)
-    ret_gate = ret_gate[:, 0].reshape(-1, 1)
-    slot = pairs[:, :2].astype(i32)
-    gk, kept, both = pairs[:, 2:4], pairs[:, 4:6], pairs[:, 6:7]
-    chosen = jnp.take(ret_produced, slot.reshape(-1), axis=0).reshape(row_count, 2, width).astype(f32)
-    output = (residual + jnp.sum(gk[:, :, None] * chosen, axis=1)).astype(bf16)
-    d_gate = jnp.take(ret_gate[:, 0], slot.reshape(-1), axis=0).reshape(row_count, 2) * kept
-    matches = expert_ids[:, :, None] == jnp.arange(experts)[None, None, :]
-    picked = jnp.sum(jnp.where(matches, probs[:, None, :], 0.0), axis=-1)
-    gate = picked / both
-    d_picked = (d_gate - jnp.sum(d_gate * gate, axis=1, keepdims=True)) / both
-    d_probs = jnp.sum(jnp.where(matches, d_picked[:, :, None], 0.0), axis=1)
-    d_logits = (probs * (d_probs - jnp.sum(probs * d_probs, axis=1, keepdims=True))).astype(bf16)
-    grad_router = jnp.dot(second.T, d_logits, preferred_element_type=jnp.float32)
-    d_pairs = jnp.take(ret_rows, slot.reshape(-1), axis=0).reshape(row_count, 2, width).astype(f32)
-    d_second = jnp.sum(d_pairs * kept[:, :, None], axis=1) + jnp.dot(d_logits, router.T, preferred_element_type=f32)
-    second_value, second_pull = jax.vjp(normalize, residual, norm2_gain, norm2_bias)
-    d_residual_norm, grad_norm2_gain, grad_norm2_bias = second_pull(d_second)
-    d_residual = cotangent.astype(f32) + d_residual_norm
-    d_branch = d_residual.astype(jnp.bfloat16)
-    grad_out_weight = jnp.dot(att_t, d_branch, preferred_element_type=jnp.float32)
-    grad_out_bias = jnp.sum(d_branch.astype(jnp.float32), axis=0)
-    d_att = jnp.dot(d_branch, out_weight.T, preferred_element_type=jnp.float32).astype(bf16)
-    d_att = d_att.reshape(SEQ_LEN, HEADS, HEAD_DIM)
-    heads = qkv.reshape(SEQ_LEN, 3, HEADS, HEAD_DIM)
-    lse2 = lse[:, :2].reshape(HEADS, row_count)
-    d_q, d_k, d_v = attend_backward((heads[:, 0], heads[:, 1], heads[:, 2], padding > 0, lse2, d_att))
-    d_projected = jnp.stack([d_q, d_k, d_v], axis=1).reshape(row_count, 3 * width).astype(bf16)
-    grad_qkv_weight = jnp.dot(first.T, d_projected, preferred_element_type=jnp.float32)
-    column_sums = jnp.sum(d_projected.astype(jnp.float32), axis=0)
-    grad_qv_bias = jnp.concatenate([column_sums[:width], column_sums[2 * width :]])
-    d_first = jnp.dot(d_projected, qkv_weight.T, preferred_element_type=jnp.float32)
-    first_value, first_pull = jax.vjp(normalize, patches.astype(f32), norm1_gain, norm1_bias)
-    d_inputs, grad_norm1_gain, grad_norm1_bias = first_pull(d_first)
-    grad_patches = (d_residual + d_inputs).astype(jnp.bfloat16)
-    dense = [grad_norm1_gain, grad_norm1_bias, grad_qkv_weight, grad_qv_bias, grad_out_weight, grad_out_bias,
-             grad_norm2_gain, grad_norm2_bias, grad_router]
-    dense = [lax.psum_scatter(g.astype(bf16), "expert", scatter_dimension=0, tiled=True) for g in dense]
-    dense = [lax.psum(g, "dp").astype(f32) for g in dense]
-    return (output, grad_patches, *dense, grad_expert_in, grad_expert_in_bias, grad_expert_out, grad_expert_out_bias)
+    output, grad_patches, sums, small, kept_grads, far_grads = run_back(
+        copies, experts, most,
+        d_rows, d_gates, produced, grads, pairs, probs,
+        second, residual, patches, cotangent, qkv, att_t, lse, first,
+        norm1_gain, norm2_gain, qkv_weight, out_weight, router.T,
+    )
+    (n1_gain, n1_bias, qkv_w, qv, out_w, out_b, n2_gain, n2_bias, router_t, *rest) = run_finish(
+        copies, experts, kept_grads, far_grads, sums, small
+    )
+    return (output, grad_patches, n1_gain, n1_bias, qkv_w, qv, out_w, out_b, n2_gain, n2_bias, router_t.T, *rest)
 
 
 def solution(mesh):

time: 605 us -> 294 us (0.49)
  Pallas kernels: 174 us -> 286 us
  waiting for transfers between devices: 111 us -> 0 us
  local copies, waits for them, and re-layouts: 111 us -> 3.05 us
  other arithmetic: 71 us -> 0 us
  matrix products: 57.9 us -> 0 us
  blocking collectives: 42.7 us -> 0 us
  starting transfers between devices: 15.9 us -> 0 us
  between operations: 16.1 us -> 0.83 us
    pallas_call x0 -> x2, Pallas kernels: none -> 105 us  [the longest x1 98.6 us: run_back(): pl.pallas_call(partial(back_kernel, copies, experts, most), out_shape=(sh...]
    dot_general x11 -> x0, matrix products: 57.9 us -> none  [the longest x1 16.8 us: attend_backward(): jnp.einsum('qhd,khd->hqk', queries, key_rows, preferred_element_type=f32)]
    gather x10 -> x0, local copies, waits for them, and re-layouts: 39.3 us -> none  [the longest x4 16.9 us: local(): grads = jnp.take(grads, jnp.arange(copies) ^ me_dp, axis=1)]
    all_to_all x1 -> x0, waiting for transfers between devices: 38.8 us -> none  [exchange(): lax.all_to_all(block, 'expert', split_axis=0, concat_axis=0, tiled=True)]
    reduce_scatter x4 -> x0, waiting for transfers between devices: 37.8 us -> none  [the longest x2 37.8 us: local(): lax.psum_scatter(g.astype(bf16), 'expert', scatter_dimension=0, tiled=True)]
    unnamed x1 -> x0, blocking collectives: 35.8 us -> none
    convert_element_type x15 -> x0, other arithmetic: 34.8 us -> none  [the longest x1 12 us: attend_backward(): d_scores = (probabilities * (d_weights - centre)).astype(jnp.bfloat16)]
    psum x1 -> x0, waiting for transfers between devices: 33.9 us -> none  [local(): dense = [lax.psum(g, 'dp').astype(f32) for g in dense]]
  transfers between devices with their start and end apart: 7 -> 0, of which waited for: 3 -> 0; matrix products, arithmetic and copies ran while one was open for 34% -> 0% of each run, Pallas kernels for 0% -> 0%
where the time goes in v4:
time: 294 us; the launch traced here: 290 us
  Pallas kernels  286 us (97%)
  local copies, waits for them, and re-layouts  3.05 us (1%)
    pallas_call x1, Pallas kernels, run_experts(): pl.pallas_call(partial(expert_kernel, copies, experts, most, chunks, 512)...  124 us
    pallas_call x1, Pallas kernels, run_back(): pl.pallas_call(partial(back_kernel, copies, experts, most), out_shape=(sh...  98.6 us
    pallas_call x1, Pallas kernels, run_front(): pl.pallas_call(partial(front_kernel, copies, experts, most, capacity), ou...  57.3 us
    pallas_call x1, Pallas kernels, run_finish(): pl.pallas_call(partial(finish_kernel, copies, experts), out_shape=(shape(...  6.31 us

profile of v4, /device:TPU:0, one launch (start us, length us, event | category | flops | bytes accessed | tf_op | source)
XLA Modules:
  0.0 290.3 jit_solution(10401980509783913705)
XLA Ops:
  0.6 57.3 %front.1 = (bf16[1536,768]{1,0:T(8,128)(2,1)}, bf16[1536,768]{1,0:T(8,128)(2,1)}, f32[8,8,192]{2,1,0:T(8,128)}, bf16[576,2304]{1,0:T(8,128)(2,1)}, bf16[768,576]...) custom-call(bf16[576,768]{1,0:T(8,128)(2,1)} %patches_ref.3, ...), custom_call_target="tpu_custom_call" | custom-call | tf_op jit(solution)/shard_map/front/pallas_call | solution.py:235
  58.0 124.2 %experts.1 = (bf16[1536,768]{1,0:T(8,128)(2,1)}, f32[8,8,192]{2,1,0:T(8,128)}, bf16[1536,768]{1,0:T(8,128)(2,1)}, bf16[2,4,784,768]{3,2,1,0:T(8,128)(2,1)}) custom-call(bf16[1536,768]{1,0:T(8,128)(2,1)} %get-tuple-element.49.x_ref, f32[8,8,192]{2,1,0:T(8,128)} %get-tuple-element.50.gates_ref, bf16[1536,768]{1,0:T(8,128)(2,1)} %get-tuple-element.51.cot_ref, ...), custom_call_target="tpu_custom_call" | custom-call | tf_op jit(solution)/shard_map/experts/pallas_call | solution.py:452
  182.1 98.6 %back.1 = (bf16[576,768]{1,0:T(8,128)(2,1)}, bf16[576,768]{1,0:T(8,128)(2,1)}, bf16[4,2,96,384]{3,2,1,0:T(8,128)(2,1)}, f32[16,768]{1,0:T(8,128)}, bf16[2,784,76...) custom-call(bf16[1536,768]{1,0:T(8,128)(2,1)} %get-tuple-element.52.d_rows_ref, ...), custom_call_target="tpu_custom_call" | custom-call | tf_op jit(solution)/shard_map/back/pallas_call | solution.py:783
  280.8 0.0 copy-start
  280.8 6.3 %finish.1 = (f32[96]{0:T(128)}, f32[96]{0:T(128)}, f32[96,2304]{1,0:T(8,128)}, f32[192]{0:T(256)}, f32[96,768]{1,0:T(8,128)}, /*index=5*/f32[96]{0:T(128)}, f32[...) custom-call(bf16[2,784,768]{2,1,0:T(8,128)(2,1)} %get-tuple-element., ...), custom_call_target="tpu_custom_call" | custom-call | tf_op jit(solution)/shard_map/finish/pallas_call | solution.py:885
  287.1 2.1 copy.35
  289.2 0.0 copy-done
  289.2 0.9 copy.36
Async XLA Ops:
  280.8 8.5 %copy-start = (bf16[576,768]{1,0:T(8,128)(2,1)S(1)}, bf16[576,768]{1,0:T(8,128)(2,1)}, u32[]{:S(2)}) copy-start(bf16[576,768]{1,0:T(8,128)(2,1)} %get-tuple-element.99) | copy-start | bytes 2654212

commit v5 on v4

--- a/solution.py
+++ b/solution.py
@@ -12,6 +12,7 @@
 SEQ_LEN = 576
 LOG2E = 1.4426950408889634
 EPS = 1e-06
+lane_count = 256
 MESH = pl.DeviceIdType.MESH
 NN = (((1,), (0,)), ((), ()))
 NT = (((1,), (1,)), ((), ()))
@@ -62,81 +63,117 @@
 
 def front_kernel(
     copies, experts, most, capacity,
-    patches_ref, cot_ref, priority_ref, ids_ref, padding_ref, gain1_ref, bias1_ref, qkv_w_ref, qv_bias_ref,
-    out_w_ref, out_bias_ref, gain2_ref, bias2_ref, router_ref,
-    recv_cot_ref, x_slots_ref, gate_slots_ref, qkv_ref, att_t_ref, lse_ref, residual_ref,
-    second_ref, first_ref, pairs_ref, probs_ref,
-    cot_send, rows_ref, table, counts, cot_ss, cot_rs, near_ss, near_rs, far_ss, far_rs,
+    patches_hbm, cot_hbm, priority_ref, ids_ref, padding_ref, gain1_ref, bias1_ref, qkv_w_hbm, qv_bias_ref,
+    out_w_hbm, out_bias_ref, gain2_ref, bias2_ref, router_ref,
+    recv_cot_hbm, raw_hbm, far_slots_ref, x_slots_hbm, gate_slots_ref, qkv_hbm, att_t_hbm, lse_ref,
+    residual_hbm, second_hbm, first_t_hbm, pairs_ref, probs_ref,
+    patches_ref, cot_ref, qkv_w_ref, out_w_ref, x_slots_ref, qkv_ref, att_t_ref, residual_ref, second_ref,
+    first_t_ref, fetch_sem, store_sem, cot_send, rows_ref, line_ref, table, counts, cot_ss, cot_rs, near_ss, near_rs, far_ss, far_rs, raw_sem,
 ):
     me_dp = lax.axis_index("dp")
     me = lax.axis_index("expert")
     rows, width = patches_ref.shape
+    ends = [(cot_hbm, cot_ref), (patches_hbm, patches_ref), (qkv_w_hbm, qkv_w_ref), (out_w_hbm, out_w_ref)]
+    fetches = [pltpu.make_async_copy(a, b, fetch_sem.at[i]) for i, (a, b) in enumerate(ends)]
+    for fetch in fetches:
+        fetch.start()
+    ends = [
+        (qkv_ref, qkv_hbm), (first_t_ref, first_t_hbm), (att_t_ref, att_t_hbm), (residual_ref, residual_hbm),
+        (second_ref, second_hbm), (x_slots_ref, x_slots_hbm),
+        (cot_send.at[pl.ds(0, most)], recv_cot_hbm.at[pl.ds(0, most)]),
+    ]
+    stores = [pltpu.make_async_copy(a, b, store_sem.at[i]) for i, (a, b) in enumerate(ends)]
     rows_ref[0:1, :] = priority_ref[...].reshape(1, rows)
     rows_ref[1:3, :] = ids_ref[...]
     rows_ref[3:4, :] = padding_ref[...].reshape(1, rows)
-    rows_ref[4:, :] = jnp.zeros((4, rows), i32)
+    rows_ref[4:6, :] = jnp.where(rows_ref[3:4, :] > 0, rows_ref[1:3, :], experts)
+    rows_ref[6:, :] = jnp.zeros((2, rows), i32)
     cols = rows_ref[...].T
+    starts = range(0, rows, lane_count)
+    parts = [(start, min(lane_count, rows - start)) for start in starts]
+
+    def spot(fact, i):
+        line = fact * len(parts) + i
+        return (line, 0) if line < line_ref.shape[0] else (len(parts) - 1, lane_count // 2)
+
+    line_ref[...] = jnp.zeros_like(line_ref)
+    for fact, row in enumerate([0, 4, 5]):
+        for i, (start, size) in enumerate(parts):
+            line, at = spot(fact, i)
+            line_ref[line : line + 1, at : at + size] = rows_ref[row : row + 1, start : start + size]
     greet(
         [(me_dp, me ^ o) for o in range(1, experts)]
         + [(me_dp ^ p, me) for p in range(1, copies)]
     )
     near = [
-        send(rows_ref, table.at[0, o], near_ss.at[o], near_rs.at[o], (me_dp, me ^ o))
+        send(line_ref, table.at[0, o], near_ss.at[o], near_rs.at[o], (me_dp, me ^ o))
         for o in range(1, experts)
     ]
-    table[0, 0] = rows_ref[...]
-    id0_row, id1_row = rows_ref[1:2, :] ^ me, rows_ref[2:3, :] ^ me
+    table[0, 0] = line_ref[...]
+    far_half = experts // 2
+    raw = send(cot_hbm, raw_hbm, raw_sem.at[0], raw_sem.at[1], (me_dp, me ^ far_half))
     expert_rows = iota((experts, rows), 0)
-    named_t = ones_where((expert_rows == id0_row) | (expert_rows == id1_row))
     before_t = ones_where(iota((rows, rows), 0) < iota((rows, rows), 1))
-    place_t = dot(named_t, before_t).astype(i32) + expert_rows * most
-    slot0_row = jnp.sum(jnp.where(expert_rows == id0_row, place_t, 0), axis=0, keepdims=True)
-    slot1_row = jnp.sum(jnp.where(expert_rows == id1_row, place_t, 0), axis=0, keepdims=True)
+
+    def slot_rows(ids, device):
+        ids = ids ^ device
+        hits = [expert_rows == ids[k : k + 1, :] for k in range(2)]
+        place = dot(ones_where(hits[0] | hits[1]), before_t).astype(i32) + expert_rows * most
+        none = ids[0:1, :] >= experts
+        return [
+            jnp.where(none, -1, jnp.sum(jnp.where(hit, place, 0), axis=0, keepdims=True)) for hit in hits
+        ]
+
+    slot0_row, slot1_row = slot_rows(rows_ref[4:6, :], me)
     id0_col, id1_col = cols[:, 1:2], cols[:, 2:3]
-    rel0_col, rel1_col = id0_col ^ me, id1_col ^ me
-    expert_cols = iota((rows, experts), 1)
-    named = ones_where((expert_cols == rel0_col) | (expert_cols == rel1_col))
-    before = ones_where(iota((rows, rows), 1) < iota((rows, rows), 0))
-    place = dot(before, named).astype(i32) + expert_cols * most
-    slot0_col = jnp.sum(jnp.where(expert_cols == rel0_col, place, 0), axis=1, keepdims=True)
-    slot1_col = jnp.sum(jnp.where(expert_cols == rel1_col, place, 0), axis=1, keepdims=True)
-
     def taken(o):
         slots = iota((most, rows), 0) + o * most
         return ones_where((slots == slot0_row) | (slots == slot1_row))
 
+    fetches[0].wait()
     cot_value = cot_ref[...]
     cots = []
-    for o in [*range(1, experts), 0]:
+    for o in range(far_half):
         picked = dot(taken(o), cot_value).astype(bf16)
-        if o == 0:
-            recv_cot_ref[0:most, :] = picked
-            continue
         part = pl.ds(o * most, most)
         cot_send[part, :] = picked
+        if o == 0:
+            stores[6].start()
+            continue
         cots.append(
-            send(cot_send.at[part], recv_cot_ref.at[part], cot_ss.at[o], cot_rs.at[o], (me_dp, me ^ o))
-        )
+            send(cot_send.at[part], recv_cot_hbm.at[part], cot_ss.at[o], cot_rs.at[o], (me_dp, me ^ o))
+        )
+    fetches[1].wait()
     inputs = patches_ref[...].astype(f32)
     first = (standardize(inputs)[0] * flat(gain1_ref) + flat(bias1_ref)).astype(bf16)
-    first_ref[...] = first
+    first_t_ref[...] = first.T
+    stores[1].start()
+    fetches[2].wait()
     qkv_ref[:, :width] = (dot(first, qkv_w_ref[:, :width]) + flat(qv_bias_ref)[:, :width]).astype(bf16)
     qkv_ref[:, width : 2 * width] = dot(first, qkv_w_ref[:, width : 2 * width]).astype(bf16)
     qkv_ref[:, 2 * width :] = (
         dot(first, qkv_w_ref[:, 2 * width :]) + flat(qv_bias_ref)[:, width:]
     ).astype(bf16)
+    stores[0].start()
     key_bias = jnp.where(cols[:, 3:4] > 0, 0.0, -1e30)
     scale = LOG2E * HEAD_DIM ** (-0.5)
     pair_width = 2 * HEAD_DIM
 
-    for near_copy in near:
-        near_copy.wait_recv()
     far = [
-        send(table.at[0], table.at[p], far_ss.at[p], far_rs.at[p], (me_dp ^ p, me))
+        pltpu.make_async_remote_copy(
+            table.at[0], table.at[p], far_ss.at[p], far_rs.at[p], (me_dp ^ p, me), MESH
+        )
         for p in range(1, copies)
     ]
 
     def attend(pair, _):
+        @pl.when(pair == 5)
+        def _():
+            for near_copy in near:
+                near_copy.wait_recv()
+            for far_copy in far:
+                far_copy.start()
+
         base = pl.multiple_of(pair * pair_width, pair_width)
         q = qkv_ref[:, pl.ds(base, pair_width)]
         k = qkv_ref[:, pl.ds(base + width, pair_width)]
@@ -157,12 +194,35 @@
         return 0
 
     lax.fori_loop(0, HEADS // 2, attend, 0)
+    rel0_col, rel1_col = cols[:, 4:5] ^ me, cols[:, 5:6] ^ me
+    expert_cols = iota((rows, experts), 1)
+    named = ones_where((expert_cols == rel0_col) | (expert_cols == rel1_col))
+    before = ones_where(iota((rows, rows), 1) < iota((rows, rows), 0))
+    place = dot(before, named).astype(i32) + expert_cols * most
+    slot0_col = jnp.sum(jnp.where(expert_cols == rel0_col, place, 0), axis=1, keepdims=True)
+    slot1_col = jnp.sum(jnp.where(expert_cols == rel1_col, place, 0), axis=1, keepdims=True)
+    none_col = cols[:, 4:5] >= experts
+    slot0_col, slot1_col = jnp.where(none_col, -1, slot0_col), jnp.where(none_col, -1, slot1_col)
+
+    far_line = table[0, far_half]
+    far_codes = []
+    for fact in (1, 2):
+        spots = [(spot(fact, i), size) for i, (start, size) in enumerate(parts)]
+        pieces = [far_line[line : line + 1, at : at + size] for (line, at), size in spots]
+        far_codes.append(jnp.concatenate(pieces, axis=1))
+    far0_row, far1_row = slot_rows(jnp.concatenate(far_codes, axis=0), me ^ far_half)
+    far_slots_ref[...] = jnp.concatenate([far0_row, far1_row, jnp.zeros((6, rows), i32)], axis=0)
+    stores[2].start()
+    fetches[3].wait()
     residual = inputs + dot(att_t_ref[...], out_w_ref[...], TN) + flat(out_bias_ref)
     residual_ref[...] = residual
+    stores[3].start()
     second = (standardize(residual)[0] * flat(gain2_ref) + flat(bias2_ref)).astype(bf16)
     second_ref[...] = second
+    stores[4].start()
     for o in range(experts):
         x_slots_ref[pl.ds(o * most, most), :] = dot(taken(o), second).astype(bf16)
+    stores[5].start()
     logits = dot(second, router_ref[...], NT)
     raised = jnp.exp(logits - jnp.max(logits, axis=-1, keepdims=True))
     probs = raised / jnp.sum(raised, axis=-1, keepdims=True)
@@ -178,17 +238,20 @@
 
     def count(block, _):
         entry = table[block // experts, block % experts]
-        real = entry[3:4, :] > 0
-        hits = jnp.concatenate(
-            [
-                ones_where((expert_rows == entry[1:2, :]) & real),
-                ones_where((expert_rows == entry[2:3, :]) & real),
-            ],
-            axis=0,
-        )
-        lower = ones_where(entry[0:1, :] < rank_col)
-        counts[:rows, :] += dot(lower, hits, NT)
-        counts[rows:, :] += dot(jnp.ones((8, rows), bf16), hits, NT)
+        ahead = jnp.zeros((rows, 2 * experts), f32)
+        loads = jnp.zeros((8, 2 * experts), f32)
+        for i, (start, size) in enumerate(parts):
+
+            def fact(k):
+                line, at = spot(k, i)
+                return entry[line : line + 1, at : at + size]
+
+            names = iota((experts, size), 0)
+            hits = jnp.concatenate([ones_where(names == fact(1)), ones_where(names == fact(2))], axis=0)
+            ahead += dot(ones_where(fact(0) < rank_col), hits, NT)
+            loads += dot(jnp.ones((8, size), bf16), hits, NT)
+        counts[:rows, :] += ahead
+        counts[rows:, :] += loads
         return 0
 
     lax.fori_loop(0, copies * experts, count, 0)
@@ -209,7 +272,7 @@
     for o in range(experts):
         slots = iota((rows, most), 1) + o * most
         gates = jnp.where(slots == slot0_col, gate0, 0.0) + jnp.where(slots == slot1_col, gate1, 0.0)
-        gate_slots_ref[o] = jnp.broadcast_to(jnp.sum(gates, axis=0, keepdims=True), (8, most))
+        gate_slots_ref[o] = jnp.sum(gates, axis=0, keepdims=True)
     lanes = iota((rows, 16), 1)
     columns = [slot0_col, slot1_col, gate0, gate1, kept0, kept1, both, cols[:, 3:4], id0_col, id1_col]
     columns = [column.astype(f32) for column in columns]
@@ -219,7 +282,7 @@
     pairs_ref[...] = packed
     for copy in near + far:
         copy.wait_send()
-    for copy in cots:
+    for copy in [*cots, raw, *stores]:
         copy.wait()
 
 
@@ -235,28 +298,42 @@
     return pl.pallas_call(
         partial(front_kernel, copies, experts, most, capacity),
         out_shape=(
+            shape((slots // 2, width), bf16),
+            shape((rows, width), bf16),
+            shape((8, rows), i32),
             shape((slots, width), bf16),
-            shape((slots, width), bf16),
-            shape((experts, 8, most), f32),
+            shape((experts, 1, most), f32),
             shape((rows, 3 * width), bf16),
             shape((width, rows), bf16),
             shape((HEADS // 2, 8, rows), f32),
             shape((rows, width), f32),
             shape((rows, width), bf16),
-            shape((rows, width), bf16),
+            shape((width, rows), bf16),
             shape((rows, 16), f32),
             shape((rows, experts), f32),
         ),
-        in_specs=[VMEM] * 14,
-        out_specs=(VMEM,) * 11,
+        in_specs=[HBM] * 2 + [VMEM] * 5 + [HBM, VMEM, HBM] + [VMEM] * 4,
+        out_specs=(HBM, HBM, VMEM, HBM, VMEM, HBM, HBM, VMEM, HBM, HBM, HBM, VMEM, VMEM),
         scratch_shapes=[
+            pltpu.VMEM((rows, width), bf16),
+            pltpu.VMEM((rows, width), bf16),
+            pltpu.VMEM((width, 3 * width), bf16),
+            pltpu.VMEM((width, width), bf16),
             pltpu.VMEM((slots, width), bf16),
+            pltpu.VMEM((rows, 3 * width), bf16),
+            pltpu.VMEM((width, rows), bf16),
+            pltpu.VMEM((rows, width), f32),
+            pltpu.VMEM((rows, width), bf16),
+            pltpu.VMEM((width, rows), bf16),
+            DMA((4,)), DMA((7,)),
+            pltpu.VMEM((slots // 2, width), bf16),
             pltpu.VMEM((8, rows), i32),
-            pltpu.VMEM((copies, experts, 8, rows), i32),
+            pltpu.VMEM((8, lane_count), i32),
+            pltpu.VMEM((copies, experts, 8, lane_count), i32),
             pltpu.VMEM((rows + 8, 2 * experts), f32),
             DMA((experts,)), DMA((experts,)),
             DMA((experts,)), DMA((experts,)),
-            DMA((copies,)), DMA((copies,)),
+            DMA((copies,)), DMA((copies,)), DMA((2,)),
         ],
         compiler_params=pltpu.CompilerParams(
             collective_id=0, has_side_effects=True, vmem_limit_bytes=VMEM_BYTES
@@ -286,10 +363,11 @@
 
 def expert_kernel(
     copies, experts, most, chunks, tile,
-    x_ref, gates_ref, cot_ref, in_w_ref, in_bias_ref, out_w_ref, out_bias_ref,
+    x_ref, gates_ref, near_cot_ref, raw_ref, far_slots_ref, in_w_hbm, in_bias_ref, out_w_hbm, out_bias_ref,
     d_rows_ref, d_gates_ref, produced_ref, grads_ref,
-    recv_x, recv_g, send_d, send_g, hidden, d_pre, x_t, d_t, bias_sum, total_p, total_d, stage,
+    in_w_ref, out_w_ref, cot_ref, send_cot, recv_x, recv_g, send_d, send_g, hidden, d_pre, x_t, d_t, bias_sum, total_p, total_d, stage,
     x_ss, x_rs, g_ss, g_rs, d_ss, d_rs, dg_ss, dg_rs, own_sem, own_d_sem, stage_sem,
+    cot_ss, cot_rs, near_sem, fetch_sem,
 ):
     me_dp = lax.axis_index("dp")
     me = lax.axis_index("expert")
@@ -320,8 +398,25 @@
             send_g.at[o], d_gates_ref.at[o], dg_ss.at[o], dg_rs.at[o], (me_dp, me ^ o), MESH
         )
 
+    far_half = experts // 2
+
+    def move_cot(j):
+        return pltpu.make_async_remote_copy(
+            send_cot.at[chunk(j)], cot_ref.at[chunk(far_half + j)], cot_ss.at[j], cot_rs.at[j],
+            (me_dp, me ^ j), MESH,
+        )
+
+    fetches = [
+        pltpu.make_async_copy(in_w_hbm, in_w_ref, fetch_sem.at[0]),
+        pltpu.make_async_copy(out_w_hbm, out_w_ref, fetch_sem.at[1]),
+    ]
+    for fetch in fetches:
+        fetch.start()
     own = pltpu.make_async_copy(x_ref.at[chunk(0)], recv_x.at[chunk(0)], own_sem)
     own.start()
+    half_slots = near_cot_ref.shape[0]
+    near_cot = pltpu.make_async_copy(near_cot_ref, cot_ref.at[pl.ds(0, half_slots)], near_sem)
+    near_cot.start()
     greet([(me_dp, me ^ o) for o in range(1, experts)])
 
     def begin(g):
@@ -333,6 +428,18 @@
     order = [0, *range(groups // 2, groups), *range(1, groups // 2)]
     begin(order[0])
     begin(order[1])
+    for j in [*range(1, far_half), 0]:
+        places = iota((most, raw_ref.shape[0]), 0) + (far_half + j) * most
+        taken = ones_where((places == far_slots_ref[0:1, :]) | (places == far_slots_ref[1:2, :]))
+        picked = dot(taken, raw_ref[...]).astype(bf16)
+        if j == 0:
+            cot_ref[chunk(far_half), :] = picked
+        else:
+            send_cot[chunk(j), :] = picked
+            move_cot(j).start()
+    near_cot.wait()
+    for fetch in fetches:
+        fetch.wait()
     recv_g[0] = gates_ref[0]
     bias_sum[...] = jnp.zeros_like(bias_sum)
     x_t[width:, :] = jnp.ones_like(x_t[width:, :])
@@ -349,9 +456,13 @@
                 move_g(o).wait_recv()
                 move_x(o).wait_recv()
 
+            @pl.when(o > far_half)
+            def _():
+                move_cot(o - far_half).wait_recv()
+
         at = pl.multiple_of(g * rows, rows)
         here = pl.ds(at, rows)
-        gate = jnp.concatenate([to_column(recv_g[g * chunks + j][0:1, :]) for j in range(chunks)], axis=0)
+        gate = jnp.concatenate([to_column(recv_g[g * chunks + j]) for j in range(chunks)], axis=0)
         x = recv_x[here, :]
         cot = cot_ref[here, :].astype(f32)
         d_produced = (cot * gate).astype(bf16)
@@ -386,7 +497,7 @@
         d_gate = jnp.sum(produced.astype(f32) * cot, axis=1, keepdims=True)
         for j in range(chunks):
             o = g * chunks + j
-            d_gate_row = jnp.broadcast_to(to_row(d_gate[j * most : (j + 1) * most, :]), (8, most))
+            d_gate_row = to_row(d_gate[j * most : (j + 1) * most, :])
             send_g[o] = d_gate_row
 
             @pl.when(o > 0)
@@ -435,6 +546,8 @@
     store(0, copies - 1).wait()
     store(1, copies - 1).wait()
     own_d.wait()
+    for j in range(1, far_half):
+        move_cot(j).wait_send()
     for o in range(1, experts):
         move_g(o).wait_send()
         move_x(o).wait_send()
@@ -444,7 +557,7 @@
 
 def run_experts(copies, experts, most, *operands):
     slots, width = operands[0].shape
-    hidden_width = operands[3].shape[1]
+    hidden_width = operands[5].shape[1]
     chunks = max(1, min(experts, 384 // most))
     rows = chunks * most
     block = hidden_width // copies
@@ -453,17 +566,21 @@
         partial(expert_kernel, copies, experts, most, chunks, 512),
         out_shape=(
             shape((slots, width), bf16),
-            shape((experts, 8, most), f32),
+            shape((experts, 1, most), f32),
             shape((slots, width), bf16),
             shape((2, copies, width + 16, block), bf16),
         ),
-        in_specs=[HBM] + [VMEM] * 6,
+        in_specs=[HBM, VMEM, HBM] + [VMEM] * 2 + [HBM, VMEM] * 2,
         out_specs=(HBM, VMEM, VMEM, HBM),
         scratch_shapes=[
+            pltpu.VMEM((width, hidden_width), bf16),
+            pltpu.VMEM((hidden_width, width), bf16),
             pltpu.VMEM((slots, width), bf16),
-            pltpu.VMEM((experts, 8, most), f32),
+            pltpu.VMEM((slots // 2, width), bf16),
             pltpu.VMEM((slots, width), bf16),
-            pltpu.VMEM((experts, 8, most), f32),
+            pltpu.VMEM((experts, 1, most), f32),
+            pltpu.VMEM((slots, width), bf16),
+            pltpu.VMEM((experts, 1, most), f32),
             pltpu.VMEM((slots, hidden_width), bf16),
             pltpu.VMEM((slots, hidden_width), bf16),
             pltpu.VMEM((width + 16, slots), bf16),
@@ -474,7 +591,7 @@
             pltpu.VMEM((2, width + 16, block), bf16),
         ]
         + [DMA((experts,))] * 8
-        + [DMA(()), DMA(()), DMA((2,))],
+        + [DMA(()), DMA(()), DMA((2,)), DMA((experts // 2,)), DMA((experts // 2,)), DMA(()), DMA((2,))],
         compiler_params=pltpu.CompilerParams(
             collective_id=1, has_side_effects=True, vmem_limit_bytes=VMEM_BYTES
         ),
@@ -484,10 +601,12 @@
 
 def back_kernel(
     copies, experts, most,
-    d_rows_ref, d_gates_ref, produced_ref, grads_ref, pairs_ref, probs_ref,
-    second_ref, residual_ref, patches_ref, cot_ref, qkv_ref, att_t_ref, lse_ref, first_ref,
-    gain1_ref, gain2_ref, qkv_w_ref, out_w_ref, router_ref,
+    d_rows_hbm, d_gates_ref, produced_ref, grads_ref, pairs_ref, probs_ref,
+    second_hbm, residual_hbm, patches_hbm, cot_hbm, qkv_hbm, att_t_hbm, lse_ref, first_t_hbm,
+    gain1_ref, gain2_ref, qkv_w_hbm, out_w_hbm, router_ref,
     output_ref, grad_patches_ref, sums_ref, small_sums_ref, kept_grads_ref, far_grads_ref,
+    d_rows_ref, second_ref, residual_ref, cot_ref, att_t_ref, out_w_ref, qkv_ref, first_t_ref, qkv_w_ref,
+    patches_ref, fetch_sem,
     recv_p, own_grads, near_grads, d_qkv, d_att, d_att_t, d_residual_ref,
     dense, small, halves, landed, crossed, tiny,
     p_ss, p_rs, n_ss, n_rs, f_ss, f_rs, own_sem, kept_sem,
@@ -496,6 +615,14 @@
     me_dp = lax.axis_index("dp")
     me = lax.axis_index("expert")
     rows, width = patches_ref.shape
+    ends = [
+        (d_rows_hbm, d_rows_ref), (second_hbm, second_ref), (residual_hbm, residual_ref), (cot_hbm, cot_ref),
+        (att_t_hbm, att_t_ref), (out_w_hbm, out_w_ref), (qkv_hbm, qkv_ref), (first_t_hbm, first_t_ref),
+        (qkv_w_hbm, qkv_w_ref), (patches_hbm, patches_ref),
+    ]
+    fetches = [pltpu.make_async_copy(a, b, fetch_sem.at[i]) for i, (a, b) in enumerate(ends)]
+    for fetch in fetches:
+        fetch.start()
     slots = experts * most
     chips = copies // 2
     core = me_dp % 2
@@ -503,6 +630,7 @@
     half = width // 2
     partner = (me_dp ^ 1, me)
     bits = [1, 0, *range(2, experts.bit_length() - 1)]
+    turns_of = [bits, [0, 1, *bits[2:]], bits, bits]
     steps = [(me_dp ^ (1 << i), me) for i in range(copies.bit_length() - 1)]
     steps += [(me_dp, me ^ (1 << i)) for i in range(experts.bit_length() - 1)]
 
@@ -515,7 +643,7 @@
         part = pl.ds(experts >> (i + 1), experts >> (i + 1))
         return pltpu.make_async_remote_copy(
             dense.at[m, core, part], landed.at[m, part], b_ss.at[m, i], b_rs.at[m, i],
-            (me_dp, me ^ (1 << bits[i])), MESH,
+            (me_dp, me ^ (1 << turns_of[m][i])), MESH,
         )
 
     def copy_c(m, q):
@@ -615,12 +743,13 @@
     slot0, slot1 = pairs_ref[:, 0:1].astype(i32), pairs_ref[:, 1:2].astype(i32)
     kept0, kept1, both = pairs_ref[:, 4:5], pairs_ref[:, 5:6], pairs_ref[:, 6:7]
     places = iota((rows, slots), 1)
+    fetches[0].wait()
     d_second = dot(ones_where((places == slot0) | (places == slot1)), d_rows_ref[...])
     d_gate0 = jnp.zeros((rows, 1), f32)
     d_gate1 = jnp.zeros((rows, 1), f32)
     for o in range(experts):
         part = iota((rows, most), 1) + o * most
-        line = d_gates_ref[o][0:1, :]
+        line = d_gates_ref[o]
         d_gate0 += jnp.sum(jnp.where(part == slot0, line, 0.0), axis=1, keepdims=True)
         d_gate1 += jnp.sum(jnp.where(part == slot1, line, 0.0), axis=1, keepdims=True)
     d_gate0, d_gate1 = d_gate0 * kept0, d_gate1 * kept1
@@ -633,8 +762,11 @@
     d_probs = jnp.where(is0, (d_gate0 - centre) / both, 0.0) + jnp.where(is1, (d_gate1 - centre) / both, 0.0)
     d_logits = (probs * (d_probs - jnp.sum(probs * d_probs, axis=1, keepdims=True))).astype(bf16)
     small[8:, :] = jnp.zeros_like(small[8:, :])
+    fetches[1].wait()
     small[8 : 8 + experts, :] = dot(d_logits, second_ref[...], TN)
     d_second += dot(d_logits, router_ref[...])
+    fetches[2].wait()
+    fetches[3].wait()
     n, inverse = standardize(residual_ref[...])
     small[5:6, :] = jnp.sum(d_second * n, axis=0, keepdims=True)
     small[6:7, :] = jnp.sum(d_second, axis=0, keepdims=True)
@@ -647,17 +779,18 @@
     small[4:5, :] = jnp.sum(d_branch.astype(f32), axis=0, keepdims=True)
     small[7:8, :] = jnp.zeros((1, width), f32)
 
-    def keep(matrix, value):
+    def keep(matrix, h, value):
         for e in range(experts):
             r = e ^ me
             at = 0
-            for bit in bits:
+            for bit in turns_of[matrix]:
                 at = at * 2 + (r // (1 << bit)) % 2
-            for h in range(2):
-                dense[matrix, h, at] = value[e * per : (e + 1) * per, h * half : (h + 1) * half].astype(bf16)
-        begin(matrix, 0)
-
-    keep(3, dot(att_t_ref[...], d_branch))
+            dense[matrix, h, at] = value[e * per : (e + 1) * per, :].astype(bf16)
+
+    fetches[4].wait()
+    for h in range(2):
+        keep(3, h, dot(att_t_ref[...], d_branch[:, h * half : (h + 1) * half]))
+    begin(3, 0)
     for copy in near:
         copy.wait_recv()
     for i, (w, q) in enumerate(turns):
@@ -670,13 +803,32 @@
     kept = pltpu.make_async_copy(near_grads.at[:, 0], kept_grads_ref, kept_sem)
     kept.start()
     advance(3)
+    fetches[5].wait()
     d_att[...] = dot(d_branch, out_w_ref[...], NT).astype(bf16)
     d_att_t[...] = dot(out_w_ref[...], d_branch, NT).astype(bf16)
     key_bias = jnp.where(pairs_ref[:, 7:8] > 0, 0.0, -1e30)
     scale = LOG2E * HEAD_DIM ** (-0.5)
     pair_width = 2 * HEAD_DIM
 
+    def columns(i, h):
+        return slice(i * width + h * half, i * width + (h + 1) * half)
+
     def attend(pair, _):
+        @pl.when(pair == 3)
+        def _():
+            for i in range(3):
+                keep(i, 0, dot(first_t_ref[...], d_qkv[:, columns(i, 0)]))
+
+                @pl.when(core == 1)
+                def _():
+                    begin(i, 0)
+
+        @pl.when((pair == 5) & (core == 0))
+        def _():
+            for i in range(3):
+                end(i, 0)
+                begin(i, 1)
+
         base = pl.multiple_of(pair * pair_width, pair_width)
         here = pl.ds(base, pair_width)
         q = qkv_ref[:, here]
@@ -705,18 +857,57 @@
         d_qkv[:, pl.ds(base + 2 * width, pair_width)] = jnp.where(low, d_v[0], d_v[1]).astype(bf16)
         return 0
 
+    fetches[6].wait()
+    fetches[7].wait()
     lax.fori_loop(0, HEADS // 2, attend, 0)
-    first_t = first_ref[...].T
+    for fetch in fetches[8:]:
+        fetch.wait()
+    def combine_results():
+        own_p.wait()
+        for copy in returns:
+            copy.wait()
+        blocks = 3
+        lines = rows // blocks
+
+        def combine(i, _):
+            part = pl.ds(pl.multiple_of(i * lines, lines), lines)
+            facts = pairs_ref[part, :]
+            spots = iota((lines, slots), 1)
+            output_ref[part, :] = (
+                residual_ref[part, :]
+                + facts[:, 2:3] * dot(ones_where(spots == facts[:, 0:1].astype(i32)), recv_p[...])
+                + facts[:, 3:4] * dot(ones_where(spots == facts[:, 1:2].astype(i32)), recv_p[...])
+            ).astype(bf16)
+            return 0
+
+        lax.fori_loop(0, blocks, combine, 0)
+
     ones = jnp.ones((8, rows), bf16)
     for i in range(3):
+        keep(i, 1, dot(first_t_ref[...], d_qkv[:, columns(i, 1)]))
+
+        @pl.when(core == 0)
+        def _():
+            begin(i, 0)
+
+        if i > 0:
+
+            @pl.when(core == 1)
+            def _():
+                end(i - 1, 0)
+                begin(i - 1, 1)
+
+    for i in (0, 2):
         part = slice(i * width, (i + 1) * width)
-        keep(i, dot(first_t, d_qkv[:, part]))
-        if i != 1:
-            small[2 + i // 2 : 3 + i // 2, :] = dot(ones, d_qkv[:, part])[0:1, :]
-        if i > 0:
-            advance(i - 1)
+        small[2 + i // 2 : 3 + i // 2, :] = dot(ones, d_qkv[:, part])[0:1, :]
+
+    @pl.when(core == 1)
+    def _():
+        end(2, 0)
+        begin(2, 1)
+
+    stages[0:3] = [1, 1, 1]
     d_first = dot(d_qkv[...], qkv_w_ref[...], NT)
-    advance(2)
     n, inverse = standardize(patches_ref[...].astype(f32))
     small[0:1, :] = jnp.sum(d_first * n, axis=0, keepdims=True)
     small[1:2, :] = jnp.sum(d_first, axis=0, keepdims=True)
@@ -726,28 +917,12 @@
         d_residual_ref[...]
         + inverse * (m - jnp.mean(m, axis=-1, keepdims=True) - n * jnp.mean(m * n, axis=-1, keepdims=True))
     ).astype(bf16)
-    own_p.wait()
-    for copy in returns:
-        copy.wait()
-    blocks = 3
-    lines = rows // blocks
-
-    def combine(i, _):
-        part = pl.ds(pl.multiple_of(i * lines, lines), lines)
-        facts = pairs_ref[part, :]
-        spots = iota((lines, slots), 1)
-        output_ref[part, :] = (
-            residual_ref[part, :]
-            + facts[:, 2:3] * dot(ones_where(spots == facts[:, 0:1].astype(i32)), recv_p[...])
-            + facts[:, 3:4] * dot(ones_where(spots == facts[:, 1:2].astype(i32)), recv_p[...])
-        ).astype(bf16)
-        return 0
-
-    lax.fori_loop(0, blocks, combine, 0)
-    for _ in range(len(bits) + 2):
+    for turn in range(len(bits) + 2):
         for m in [3, 0, 1, 2]:
             advance(m)
         advance_small()
+        if turn == 0:
+            combine_results()
     while todo:
         advance_small()
     small_sums_ref[...] = tiny[0, len(steps) - 1]
@@ -790,9 +965,20 @@
             shape((2, width + 16, block), bf16),
             shape((2, chips - 1, width + 16, block), bf16),
         ),
-        in_specs=[VMEM] * 2 + [HBM] * 2 + [VMEM] * 15,
+        in_specs=[HBM, VMEM, HBM, HBM, VMEM, VMEM] + [HBM] * 6 + [VMEM, HBM, VMEM, VMEM, HBM, HBM, VMEM],
         out_specs=(VMEM,) * 4 + (HBM,) * 2,
         scratch_shapes=[
+            pltpu.VMEM((slots, width), bf16),
+            pltpu.VMEM((rows, width), bf16),
+            pltpu.VMEM((rows, width), f32),
+            pltpu.VMEM((rows, width), bf16),
+            pltpu.VMEM((width, rows), bf16),
+            pltpu.VMEM((width, width), bf16),
+            pltpu.VMEM((rows, 3 * width), bf16),
+            pltpu.VMEM((width, rows), bf16),
+            pltpu.VMEM((width, 3 * width), bf16),
+            pltpu.VMEM((rows, width), bf16),
+            DMA((10,)),
             pltpu.VMEM((slots, width), bf16),
             pltpu.VMEM((2, width + 16, block), bf16),
             pltpu.VMEM((2, chips, width + 16, block), bf16),
@@ -825,11 +1011,13 @@
 
 def finish_kernel(
     copies, experts,
-    kept_ref, far_ref, sums_ref, small_ref,
-    gain1_ref, bias1_ref, qkv_w_ref, qv_bias_ref, out_w_ref, out_bias_ref, gain2_ref, bias2_ref, router_ref,
+    kept_ref, far_ref, sums_ref, small_ref, made_ref, grad_ref,
+    output_ref, grad_patches_ref, gain1_ref, bias1_ref, qkv_w_ref, qv_bias_ref, out_w_ref, out_bias_ref, gain2_ref, bias2_ref, router_ref,
     in_w_ref, in_bias_ref, expert_out_ref, expert_out_bias_ref,
     turned, turned_bias,
 ):
+    output_ref[...] = made_ref[...]
+    grad_patches_ref[...] = grad_ref[...]
     width = small_ref.shape[1]
     per, half = width // experts, width // 2
     me = lax.axis_index("expert")
@@ -885,14 +1073,15 @@
     return pl.pallas_call(
         partial(finish_kernel, copies, experts),
         out_shape=(
+            shape(operands[4].shape, bf16), shape(operands[5].shape, bf16),
             shape((per,), f32), shape((per,), f32), shape((per, 3 * width), f32), shape((2 * per,), f32),
             shape((per, width), f32), shape((per,), f32), shape((per,), f32), shape((per,), f32),
             shape((experts, per), f32),
             shape((1, width, block), f32), shape((1, block), f32),
             shape((1, block, width), f32), shape((1, width // copies), f32),
         ),
-        in_specs=[VMEM] * 4,
-        out_specs=(VMEM,) * 13,
+        in_specs=[VMEM] * 6,
+        out_specs=(VMEM,) * 15,
         scratch_shapes=[pltpu.VMEM((width, 128), f32), pltpu.VMEM((width, 128), f32)],
         compiler_params=pltpu.CompilerParams(vmem_limit_bytes=VMEM_BYTES),
         name="finish",
@@ -909,14 +1098,14 @@
     total_rows = row_count * copies * experts
     capacity = (210 * total_rows + 100 * experts - 1) // (100 * experts)
     most = 8 * row_count // (3 * experts)
-    (recv_cot, x_slots, gate_slots, qkv, att_t, lse, residual, second, first, pairs, probs) = run_front(
+    (near_cot, raw_cot, far_slots, x_slots, gate_slots, qkv, att_t, lse, residual, second, first, pairs, probs) = run_front(
         copies, experts, most, capacity,
         patches, cotangent, priority, expert_ids.T, padding, norm1_gain, norm1_bias, qkv_weight, qv_bias,
         out_weight, out_bias, norm2_gain, norm2_bias, router.T,
     )
     d_rows, d_gates, produced, grads = run_experts(
         copies, experts, most,
-        x_slots, gate_slots, recv_cot, expert_in[0], expert_in_bias, expert_out[0], expert_out_bias,
+        x_slots, gate_slots, near_cot, raw_cot, far_slots, expert_in[0], expert_in_bias, expert_out[0], expert_out_bias,
     )
     output, grad_patches, sums, small, kept_grads, far_grads = run_back(
         copies, experts, most,
@@ -924,8 +1113,8 @@
         second, residual, patches, cotangent, qkv, att_t, lse, first,
         norm1_gain, norm2_gain, qkv_weight, out_weight, router.T,
     )
-    (n1_gain, n1_bias, qkv_w, qv, out_w, out_b, n2_gain, n2_bias, router_t, *rest) = run_finish(
-        copies, experts, kept_grads, far_grads, sums, small
+    (output, grad_patches, n1_gain, n1_bias, qkv_w, qv, out_w, out_b, n2_gain, n2_bias, router_t, *rest) = run_finish(
+        copies, experts, kept_grads, far_grads, sums, small, output, grad_patches
     )
     return (output, grad_patches, n1_gain, n1_bias, qkv_w, qv, out_w, out_b, n2_gain, n2_bias, router_t.T, *rest)
 

time: 294 us -> 258 us (0.88)
  Pallas kernels: 286 us -> 254 us
  local copies, waits for them, and re-layouts: 3.05 us -> 0 us
    pallas_call x1, Pallas kernels: 124 us -> 106 us  [run_experts(): pl.pallas_call(partial(expert_kernel, copies, experts, most, chunks, 512)...]
    pallas_call x1, Pallas kernels: 98.6 us -> 88.2 us  [run_back(): pl.pallas_call(partial(back_kernel, copies, experts, most), out_shape=(sh...]
    pallas_call x1, Pallas kernels: 57.3 us -> 52.2 us  [run_front(): pl.pallas_call(partial(front_kernel, copies, experts, most, capacity), ou...]
    unnamed x4 -> x0, local copies, waits for them, and re-layouts: 3.05 us -> none
where the time goes in v5:
time: 258 us; the launch traced here: 255 us
  Pallas kernels  254 us (98%)
    pallas_call x1, Pallas kernels, run_experts(): pl.pallas_call(partial(expert_kernel, copies, experts, most, chunks, 512)...  106 us
    pallas_call x1, Pallas kernels, run_back(): pl.pallas_call(partial(back_kernel, copies, experts, most), out_shape=(sh...  88.2 us
    pallas_call x1, Pallas kernels, run_front(): pl.pallas_call(partial(front_kernel, copies, experts, most, capacity), ou...  52.2 us
    pallas_call x1, Pallas kernels, run_finish(): pl.pallas_call(partial(finish_kernel, copies, experts), out_shape=(shape(...  7.25 us

profile of v5, /device:TPU:0, one launch (start us, length us, event | category | flops | bytes accessed | tf_op | source)
XLA Modules:
  0.0 254.9 jit_solution(8836381787954085906)
XLA Ops:
  0.6 52.2 %front.1 = (bf16[768,768]{1,0:T(8,128)(2,1)}, bf16[576,768]{1,0:T(8,128)(2,1)}, s32[8,576]{1,0:T(8,128)}, bf16[1536,768]{1,0:T(8,128)(2,1)}, f32[8,1,192]{2,1,0:...) custom-call(bf16[576,768]{1,0:T(8,128)(2,1)} %patches_hbm.3, ...), custom_call_target="tpu_custom_call" | custom-call | tf_op jit(solution)/shard_map/front/pallas_call | solution.py:298
  52.8 106.4 %experts.1 = (bf16[1536,768]{1,0:T(8,128)(2,1)}, f32[8,1,192]{2,1,0:T(1,128)}, bf16[1536,768]{1,0:T(8,128)(2,1)}, bf16[2,4,784,768]{3,2,1,0:T(8,128)(2,1)}) custom-call(bf16[1536,768]{1,0:T(8,128)(2,1)} %get-tuple-element.53.x_ref, f32[8,1,192]{2,1,0:T(1,128)} %get-tuple-element.54.gates_ref, bf16[768,768]{1,0:T(8,128)(2,1)} %get-tuple-element.55.near_cot_ref, ...), custom_call_target="tpu_custom_call" | custom-call | tf_op jit(solution)/shard_map/experts/pallas_call | solution.py:565
  159.3 88.2 %back.1 = (bf16[576,768]{1,0:T(8,128)(2,1)}, bf16[576,768]{1,0:T(8,128)(2,1)}, bf16[4,2,96,384]{3,2,1,0:T(8,128)(2,1)}, f32[16,768]{1,0:T(8,128)}, bf16[2,784,76...) custom-call(bf16[1536,768]{1,0:T(8,128)(2,1)} %get-tuple-element.58.d_rows_hbm, ...), custom_call_target="tpu_custom_call" | custom-call | tf_op jit(solution)/shard_map/back/pallas_call | solution.py:958
  247.4 7.3 %finish.1 = (bf16[576,768]{1,0:T(8,128)(2,1)}, bf16[576,768]{1,0:T(8,128)(2,1)}, f32[96]{0:T(128)}, f32[96]{0:T(128)}, f32[96,2304]{1,0:T(8,128)}, /*index=5*/f3...) custom-call(bf16[2,784,768]{2,1,0:T(8,128)(2,1)} %get-tuple-element., ...), custom_call_target="tpu_custom_call" | custom-call | tf_op jit(solution)/shard_map/finish/pallas_call | solution.py:1073

commit v6 on v5

--- a/solution.py
+++ b/solution.py
@@ -629,8 +629,7 @@
     per = width // experts
     half = width // 2
     partner = (me_dp ^ 1, me)
-    bits = [1, 0, *range(2, experts.bit_length() - 1)]
-    turns_of = [bits, [0, 1, *bits[2:]], bits, bits]
+    bits = list(range(experts.bit_length() - 1))
     steps = [(me_dp ^ (1 << i), me) for i in range(copies.bit_length() - 1)]
     steps += [(me_dp, me ^ (1 << i)) for i in range(experts.bit_length() - 1)]
 
@@ -643,7 +642,7 @@
         part = pl.ds(experts >> (i + 1), experts >> (i + 1))
         return pltpu.make_async_remote_copy(
             dense.at[m, core, part], landed.at[m, part], b_ss.at[m, i], b_rs.at[m, i],
-            (me_dp, me ^ (1 << turns_of[m][i])), MESH,
+            (me_dp, me ^ (1 << bits[i])), MESH,
         )
 
     def copy_c(m, q):
@@ -693,8 +692,11 @@
             begin(m, stages[m])
 
     def copy_t(i):
-        src = small if i == 0 else tiny.at[0, i - 1]
-        return pltpu.make_async_remote_copy(src, tiny.at[1, i], t_ss.at[i], t_rs.at[i], steps[i], MESH)
+        return pltpu.make_async_remote_copy(tiny.at[0, i], tiny.at[1, i], t_ss.at[i], t_rs.at[i], steps[i], MESH)
+
+    def begin_small(i):
+        tiny[0, i] = small[...].astype(bf16)
+        copy_t(i).start()
 
     todo = list(range(len(steps)))
 
@@ -702,10 +704,9 @@
         if todo:
             i = todo.pop(0)
             copy_t(i).wait_recv()
-            mine = small[...] if i == 0 else tiny[0, i - 1]
-            tiny[0, i] = mine + tiny[1, i]
+            small[...] += tiny[1, i].astype(f32)
             if i + 1 < len(steps):
-                copy_t(i + 1).start()
+                begin_small(i + 1)
 
     def copy_f(w, q):
         return pltpu.make_async_remote_copy(
@@ -783,7 +784,7 @@
         for e in range(experts):
             r = e ^ me
             at = 0
-            for bit in turns_of[matrix]:
+            for bit in bits:
                 at = at * 2 + (r // (1 << bit)) % 2
             dense[matrix, h, at] = value[e * per : (e + 1) * per, :].astype(bf16)
 
@@ -860,6 +861,7 @@
     fetches[6].wait()
     fetches[7].wait()
     lax.fori_loop(0, HEADS // 2, attend, 0)
+    advance(3)
     for fetch in fetches[8:]:
         fetch.wait()
     def combine_results():
@@ -911,7 +913,7 @@
     n, inverse = standardize(patches_ref[...].astype(f32))
     small[0:1, :] = jnp.sum(d_first * n, axis=0, keepdims=True)
     small[1:2, :] = jnp.sum(d_first, axis=0, keepdims=True)
-    copy_t(0).start()
+    begin_small(0)
     m = d_first * flat(gain1_ref)
     grad_patches_ref[...] = (
         d_residual_ref[...]
@@ -925,7 +927,7 @@
             combine_results()
     while todo:
         advance_small()
-    small_sums_ref[...] = tiny[0, len(steps) - 1]
+    small_sums_ref[...] = small[...]
     for copy in near:
         copy.wait_send()
     kept.wait()
@@ -991,7 +993,7 @@
             pltpu.VMEM((4, experts, per, half), bf16),
             pltpu.VMEM((4, experts, per, half), bf16),
             pltpu.VMEM((4, chips - 1, per, half), bf16),
-            pltpu.VMEM((2, steps, smalls, width), f32),
+            pltpu.VMEM((2, steps, smalls, width), bf16),
             DMA((experts,)), DMA((experts,)),
             DMA((2, chips)), DMA((2, chips)),
             DMA((2, chips)), DMA((2, chips)),

time: 258 us -> 256 us (level)
  Pallas kernels: 254 us -> 251 us
    pallas_call x1, Pallas kernels: 88.2 us -> 85.3 us  [run_back(): pl.pallas_call(partial(back_kernel, copies, experts, most), out_shape=(sh...]
where the time goes in v6:
time: 256 us; the launch traced here: 252 us
  Pallas kernels  251 us (98%)
    pallas_call x1, Pallas kernels, run_experts(): pl.pallas_call(partial(expert_kernel, copies, experts, most, chunks, 512)...  106 us
    pallas_call x1, Pallas kernels, run_back(): pl.pallas_call(partial(back_kernel, copies, experts, most), out_shape=(sh...  85.3 us
    pallas_call x1, Pallas kernels, run_front(): pl.pallas_call(partial(front_kernel, copies, experts, most, capacity), ou...  52.2 us
    pallas_call x1, Pallas kernels, run_finish(): pl.pallas_call(partial(finish_kernel, copies, experts), out_shape=(shape(...  7.25 us

profile of v6, /device:TPU:0, one launch (start us, length us, event | category | flops | bytes accessed | tf_op | source)
XLA Modules:
  0.0 252.1 jit_solution(5784013966910592870)
XLA Ops:
  0.6 52.2 %front.1 = (bf16[768,768]{1,0:T(8,128)(2,1)}, bf16[576,768]{1,0:T(8,128)(2,1)}, s32[8,576]{1,0:T(8,128)}, bf16[1536,768]{1,0:T(8,128)(2,1)}, f32[8,1,192]{2,1,0:...) custom-call(bf16[576,768]{1,0:T(8,128)(2,1)} %patches_hbm.3, ...), custom_call_target="tpu_custom_call" | custom-call | tf_op jit(solution)/shard_map/front/pallas_call | solution.py:298
  52.8 106.4 %experts.1 = (bf16[1536,768]{1,0:T(8,128)(2,1)}, f32[8,1,192]{2,1,0:T(1,128)}, bf16[1536,768]{1,0:T(8,128)(2,1)}, bf16[2,4,784,768]{3,2,1,0:T(8,128)(2,1)}) custom-call(bf16[1536,768]{1,0:T(8,128)(2,1)} %get-tuple-element.53.x_ref, f32[8,1,192]{2,1,0:T(1,128)} %get-tuple-element.54.gates_ref, bf16[768,768]{1,0:T(8,128)(2,1)} %get-tuple-element.55.near_cot_ref, ...), custom_call_target="tpu_custom_call" | custom-call | tf_op jit(solution)/shard_map/experts/pallas_call | solution.py:565
  159.3 85.3 %back.1 = (bf16[576,768]{1,0:T(8,128)(2,1)}, bf16[576,768]{1,0:T(8,128)(2,1)}, bf16[4,2,96,384]{3,2,1,0:T(8,128)(2,1)}, f32[16,768]{1,0:T(8,128)}, bf16[2,784,76...) custom-call(bf16[1536,768]{1,0:T(8,128)(2,1)} %get-tuple-element.58.d_rows_hbm, ...), custom_call_target="tpu_custom_call" | custom-call | tf_op jit(solution)/shard_map/back/pallas_call | solution.py:960
  244.6 7.3 %finish.1 = (bf16[576,768]{1,0:T(8,128)(2,1)}, bf16[576,768]{1,0:T(8,128)(2,1)}, f32[96]{0:T(128)}, f32[96]{0:T(128)}, f32[96,2304]{1,0:T(8,128)}, /*index=5*/f3...) custom-call(bf16[2,784,768]{2,1,0:T(8,128)(2,1)} %get-tuple-element., ...), custom_call_target="tpu_custom_call" | custom-call | tf_op jit(solution)/shard_map/finish/pallas_call | solution.py:1075

commit v7 on v6

--- a/solution.py
+++ b/solution.py
@@ -563,7 +563,7 @@
     block = hidden_width // copies
     shape = jax.ShapeDtypeStruct
     return pl.pallas_call(
-        partial(expert_kernel, copies, experts, most, chunks, 512),
+        partial(expert_kernel, copies, experts, most, chunks, 768),
         out_shape=(
             shape((slots, width), bf16),
             shape((experts, 1, most), f32),

time: 256 us -> 253 us (0.988)
  Pallas kernels: 251 us -> 248 us
    pallas_call x1, Pallas kernels: 85.3 us -> 81.8 us  [run_back(): pl.pallas_call(partial(back_kernel, copies, experts, most), out_shape=(sh...]
where the time goes in v7:
time: 253 us; the launch traced here: 249 us
  Pallas kernels  248 us (98%)
    pallas_call x1, Pallas kernels, run_experts(): pl.pallas_call(partial(expert_kernel, copies, experts, most, chunks, 768)...  107 us
    pallas_call x1, Pallas kernels, run_back(): pl.pallas_call(partial(back_kernel, copies, experts, most), out_shape=(sh...  81.8 us
    pallas_call x1, Pallas kernels, run_front(): pl.pallas_call(partial(front_kernel, copies, experts, most, capacity), ou...  52.2 us
    pallas_call x1, Pallas kernels, run_finish(): pl.pallas_call(partial(finish_kernel, copies, experts), out_shape=(shape(...  7.25 us

profile of v7, /device:TPU:0, one launch (start us, length us, event | category | flops | bytes accessed | tf_op | source)
XLA Modules:
  0.0 249.0 jit_solution(13874309197133347332)
XLA Ops:
  0.6 52.2 %front.1 = (bf16[768,768]{1,0:T(8,128)(2,1)}, bf16[576,768]{1,0:T(8,128)(2,1)}, s32[8,576]{1,0:T(8,128)}, bf16[1536,768]{1,0:T(8,128)(2,1)}, f32[8,1,192]{2,1,0:...) custom-call(bf16[576,768]{1,0:T(8,128)(2,1)} %patches_hbm.3, ...), custom_call_target="tpu_custom_call" | custom-call | tf_op jit(solution)/shard_map/front/pallas_call | solution.py:298
  52.8 106.8 %experts.1 = (bf16[1536,768]{1,0:T(8,128)(2,1)}, f32[8,1,192]{2,1,0:T(1,128)}, bf16[1536,768]{1,0:T(8,128)(2,1)}, bf16[2,4,784,768]{3,2,1,0:T(8,128)(2,1)}) custom-call(bf16[1536,768]{1,0:T(8,128)(2,1)} %get-tuple-element.53.x_ref, f32[8,1,192]{2,1,0:T(1,128)} %get-tuple-element.54.gates_ref, bf16[768,768]{1,0:T(8,128)(2,1)} %get-tuple-element.55.near_cot_ref, ...), custom_call_target="tpu_custom_call" | custom-call | tf_op jit(solution)/shard_map/experts/pallas_call | solution.py:565
  159.7 81.8 %back.1 = (bf16[576,768]{1,0:T(8,128)(2,1)}, bf16[576,768]{1,0:T(8,128)(2,1)}, bf16[4,2,96,384]{3,2,1,0:T(8,128)(2,1)}, f32[16,768]{1,0:T(8,128)}, bf16[2,784,76...) custom-call(bf16[1536,768]{1,0:T(8,128)(2,1)} %get-tuple-element.58.d_rows_hbm, ...), custom_call_target="tpu_custom_call" | custom-call | tf_op jit(solution)/shard_map/back/pallas_call | solution.py:960
  241.5 7.3 %finish.1 = (bf16[576,768]{1,0:T(8,128)(2,1)}, bf16[576,768]{1,0:T(8,128)(2,1)}, f32[96]{0:T(128)}, f32[96]{0:T(128)}, f32[96,2304]{1,0:T(8,128)}, /*index=5*/f3...) custom-call(bf16[2,784,768]{2,1,0:T(8,128)(2,1)} %get-tuple-element., ...), custom_call_target="tpu_custom_call" | custom-call | tf_op jit(solution)/shard_map/finish/pallas_call | solution.py:1075
